TPU v7x, 256 devices: a whole 4x4x8 slice. The times are simulated.
256 devices in a mesh: zonal: 16 (over y, x_hi, core), merid: 16 (over z, x_lo).
Axes of the slice: x: 4 (x_hi: 2, x_lo: 2; x = x_hi * 2 + x_lo), y: 4, z: 8, core: 2. Of those that a mesh axis runs over, the one named last changes fastest.
Arguments:
- tracers: float32 [2, 8, 128, 6144], P(None, None, 'merid', 'zonal'), may hold values from -6 to 6
- speed_east: float32 [8, 128, 6144], P(None, 'merid', 'zonal'), may hold values from -0.12 to 0.12
- speed_north: float32 [8, 128, 6144], P(None, 'merid', 'zonal'), may hold values from -0.12 to 0.12
- diff_horiz: float32 [8, 128, 6144], P(None, 'merid', 'zonal'), may hold values from 0.06 to 0.08
- diff_vert: float32 [8, 128, 6144], P(None, 'merid', 'zonal'), may hold values from 0.005 to 0.1
- sea_mask: int32 [8, 128, 6144], P(None, 'merid', 'zonal'), may hold values 0 or 1
Outputs:
- tracers_out: float32 [2, 8, 128, 6144], P(None, None, 'merid', 'zonal')
Inputs may be any that keep to these rules, and one draw needn't show every extreme that they name: `sea_mask`: 1 marks a sea cell, 0 land.
All inputs are finite; a program needn't handle non-finite values. No bound on the sum of `sea_mask` on one device may be relied on, other than what follows from the above.
Results may differ from a plain program's by a relative error of at most 0.0001.
Values sent between devices are 32-bit elements; how exact they have to be, the bound alone decides.
No kernel may reach another device: no remote copies, remote signals or barrier semaphores. Data moves between devices by JAX's collectives and lax.ppermute only.
A program may use at most 192 MiB of HBM per device.

v0:
```python
import jax
import jax.numpy as jnp
from jax import lax
from jax.sharding import PartitionSpec as P

STEPS = 6
ITERS = 2


robin_weight = 0.5


def extended(block, sides, width, periodic):
    for axis, dim in sides:
        count = lax.axis_size(axis)
        forward = [(i, i + 1) for i in range(count - 1)]
        if periodic:
            forward.append((count - 1, 0))
        backward = [(target, source) for source, target in forward]
        low = lax.ppermute(
            lax.slice_in_dim(block, block.shape[dim] - width, None, axis=dim), axis, forward
        )
        high = lax.ppermute(lax.slice_in_dim(block, 0, width, axis=dim), axis, backward)
        block = jnp.concatenate([low, block, high], axis=dim)
    return block


def passed_along(value, axis, steps):
    count = lax.axis_size(axis)
    pairs = [(source, (source + steps) % count) for source in range(count)]
    return lax.ppermute(value, axis, pairs)


def face_tables(coeffs):
    (
        speed_east,
        speed_north,
        diff_horiz,
        diff_vert,
        sea_cells,
        speed_inlet,
        diff_inlet,
        sea_west,
        sea_east,
    ) = coeffs
    face_speed = jnp.concatenate([speed_inlet[..., None], speed_east], axis=-1)
    face_diff = jnp.concatenate([diff_inlet[..., None], diff_horiz], axis=-1)
    sea_padded = jnp.concatenate([sea_west[..., None], sea_cells, sea_east[..., None]], axis=-1)
    face_sea = sea_padded[..., :-1] * sea_padded[..., 1:]
    zonal_left = (jnp.maximum(face_speed, 0.0) + face_diff) * face_sea
    zonal_right = (jnp.minimum(face_speed, 0.0) - face_diff) * face_sea
    sea_north = jnp.concatenate([sea_cells[:, 1:], jnp.zeros_like(sea_cells[:, :1])], axis=1)
    north_sea = sea_cells * sea_north
    merid_here = (jnp.maximum(speed_north, 0.0) + diff_horiz) * north_sea
    merid_there = (jnp.minimum(speed_north, 0.0) - diff_horiz) * north_sea
    sea_below = jnp.concatenate([sea_cells[1:], jnp.zeros_like(sea_cells[:1])], axis=0)
    vertical_coef = diff_vert * sea_cells * sea_below
    return (zonal_left, zonal_right, merid_here, merid_there, vertical_coef, sea_cells)


def transport_step(tracer, ghost_west, ghost_east, tables):
    zonal_left, zonal_right, merid_here, merid_there, vertical_coef, sea_cells = tables
    padded = jnp.concatenate([ghost_west[..., None], tracer, ghost_east[..., None]], axis=-1)
    zonal_flux = zonal_left * padded[..., :-1] + zonal_right * padded[..., 1:]
    zonal_div = zonal_flux[..., 1:] - zonal_flux[..., :-1]
    northern = jnp.concatenate([tracer[:, :, 1:], jnp.zeros_like(tracer[:, :, :1])], axis=2)
    merid_flux = merid_here * tracer + merid_there * northern
    merid_div = merid_flux - jnp.concatenate(
        [jnp.zeros_like(merid_flux[:, :, :1]), merid_flux[:, :, :-1]], axis=2
    )
    lower_cell = jnp.concatenate([tracer[:, 1:], jnp.zeros_like(tracer[:, :1])], axis=1)
    vertical_flux = vertical_coef * (tracer - lower_cell)
    vertical_div = vertical_flux - jnp.concatenate(
        [jnp.zeros_like(vertical_flux[:, :1]), vertical_flux[:, :-1]], axis=1
    )
    return sea_cells * (tracer - zonal_div - merid_div - vertical_div)


def block_coeffs(fields, inlet_speed, inlet_diff, sea_west, sea_east):
    return (
        fields[2],
        fields[3],
        fields[4],
        fields[5],
        fields[6],
        inlet_speed,
        inlet_diff,
        sea_west,
        sea_east,
    )


def shards(tracers, speed_east, speed_north, diff_horiz, diff_vert, sea_mask):
    own_rows = tracers.shape[2]
    rim_depth = 1
    factor_a = 1.0 - robin_weight / 2.0
    factor_b = 1.0 + robin_weight / 2.0
    sea_float = sea_mask.astype(jnp.float32)
    stacked = jnp.concatenate(
        [tracers, jnp.stack([speed_east, speed_north, diff_horiz, diff_vert, sea_float])], axis=0
    )
    widened = extended(stacked, (("merid", 2),), rim_depth, False)
    chosen = jnp.concatenate([widened[0:3], widened[4:5], widened[6:7]], axis=0)
    edge_cols = jnp.stack([chosen[..., 0], chosen[..., -1]], axis=0)
    edge_rims = extended(edge_cols, (("zonal", 0),), 1, True)
    west_edge = edge_rims[0]
    east_edge = edge_rims[3]
    coeff_list = [block_coeffs(widened, west_edge[2], west_edge[3], west_edge[4], east_edge[4])]
    starts = [widened[0:2]]
    first_sides = [(west_edge[0:2], east_edge[0:2])]
    own_block = 0
    table_list = [face_tables(coeffs) for coeffs in coeff_list]
    starts = [start[:, :, 1 : 1 + own_rows] for start in starts]
    widths = [start.shape[-1] for start in starts]

    def ghost_values(current, side_west, side_east, moment, robin):
        if robin:
            ghost_west = (side_west[moment] + factor_a * current[..., 0]) / factor_b
            ghost_east = (side_east[moment] + factor_a * current[..., -1]) / factor_b
        else:
            ghost_west = side_west
            ghost_east = side_east
        return (ghost_west, ghost_east)

    def interface_traces(current, ghost_west, ghost_east):
        first_row = 1
        first_col = current[:, :, first_row : first_row + own_rows, 0]
        last_col = current[:, :, first_row : first_row + own_rows, -1]
        inner_west = ghost_west[:, :, first_row : first_row + own_rows]
        inner_east = ghost_east[:, :, first_row : first_row + own_rows]
        west_trace = first_col - inner_west + robin_weight * (first_col + inner_west) / 2.0
        east_trace = last_col - inner_east + robin_weight * (last_col + inner_east) / 2.0
        return (west_trace, east_trace)

    def fit_rows(side):
        return jnp.pad(side, ((0, 0), (0, 0), (0, 0), (1, 1)))

    def solve(sides_list, robin):
        states = list(starts)
        west_lists = [[] for start in starts]
        east_lists = [[] for start in starts]
        for moment in range(STEPS):
            joined = states[0]
            joined = extended(joined, (("merid", 2),), 1, False)
            offset = 0
            width_now = widths[0]
            offset = offset + width_now
            side_west, side_east = sides_list[0]
            ghost_west, ghost_east = ghost_values(joined, side_west, side_east, moment, robin)
            west_trace, east_trace = interface_traces(joined, ghost_west, ghost_east)
            west_lists[0].append(west_trace)
            east_lists[0].append(east_trace)
            stepped = transport_step(joined, ghost_west, ghost_east, table_list[0])
            new_states = [stepped[:, :, 1 : 1 + own_rows]]
            states = new_states
        west_hist = [jnp.stack(items) for items in west_lists]
        east_hist = [jnp.stack(items) for items in east_lists]
        return (states, west_hist, east_hist)

    states, trace_west, trace_east = solve(first_sides, False)
    for sweep in range(ITERS):
        west_side = passed_along(trace_east[0], "zonal", 1)
        east_side = passed_along(trace_west[0], "zonal", -1)
        sides_list = [(fit_rows(west_side), fit_rows(east_side))]
        states, trace_west, trace_east = solve(sides_list, True)
    result = states[own_block]
    return result


def solution(mesh):
    in_specs = (
        P(None, None, "merid", "zonal"),
        P(None, "merid", "zonal"),
        P(None, "merid", "zonal"),
        P(None, "merid", "zonal"),
        P(None, "merid", "zonal"),
        P(None, "merid", "zonal"),
    )
    out_specs = P(None, None, "merid", "zonal")
    return jax.shard_map(shards, mesh=mesh, in_specs=in_specs, out_specs=out_specs, check_vma=False)
```

profile of v0, /device:TPU:2, one launch (start us, length us, event | category | flops | bytes accessed | tf_op | source)
XLA Modules:
  0.0 200.1 jit_solution(8542457032911207558)
XLA Ops:
  1.1 4.2 %collective-permute-start.3 = (f32[2,8,1,384]{3,1,2,0:T(8,128)S(1)}, f32[2,8,1,384]{3,1,2,0:T(8,128)S(1)}, u32[]{:S(2)}, u32[]{:S(2)}) collective-permute-start(f32[2,8,1,384]{3,1,2,0:T(8,128)S(1)} %get-tuple-element.133), channel_id=1, source_target_pairs={{1,0},{2,1},{3,2},{4,3},{5,4},{6,5},{7,6},{8,7},{9,8},{10,9},{11,1... | collective-permute-start | bytes 73736 | tf_op jit(solution)/shard_map/ppermute | solution.py:23
  14.6 2.9 %collective-permute-start.1 = (f32[7,8,1,384]{3,1,2,0:T(8,128)S(1)}, f32[7,8,1,384]{3,1,2,0:T(8,128)S(1)}, u32[]{:S(2)}, u32[]{:S(2)}) collective-permute-start(f32[7,8,1,384]{3,1,2,0:T(8,128)S(1)} %copy.7054), channel_id=1, source_target_pairs={{1,0},{2,1},{3,2},{4,3},{5,4},{6,5},{7,6},{8,7},{9,8},{10,9},{11,1... | collective-permute-start | bytes 258056 | tf_op jit(solution)/shard_map/ppermute | solution.py:23
  18.3 3.6 %collective-permute-done.1 = f32[7,8,1,384]{3,1,2,0:T(8,128)S(1)} collective-permute-done((f32[7,8,1,384]{3,1,2,0:T(8,128)S(1)}, f32[7,8,1,384]{3,1,2,0:T(8,128)S(1)}, u32[]{:S(2)}, u32[]{:S(2)}) %collective-permute-start.1) | collective-permute-done | bytes 86048 | tf_op jit(solution)/shard_map/ppermute | solution.py:23
  22.9 5.3 %collective-permute-start.5 = (f32[1,5,8,10]{3,2,1,0:T(8,128)S(1)}, f32[1,5,8,10]{3,2,1,0:T(8,128)S(1)}, u32[]{:S(2)}, u32[]{:S(2)}) collective-permute-start(f32[1,5,8,10]{3,2,1,0:T(8,128)S(1)} %bitcast.488), channel_id=1, source_target_pairs={{16,0},{32,16},{48,32},{64,48},{80,64},{96,80},{112,96},{128,112},... | collective-permute-start | bytes 4808 | tf_op jit(solution)/shard_map/ppermute | solution.py:23
  31.4 3.4 %collective-permute-start.6 = (f32[2,8,1,384]{3,1,2,0:T(8,128)S(1)}, f32[2,8,1,384]{3,1,2,0:T(8,128)S(1)}, u32[]{:S(2)}, u32[]{:S(2)}) collective-permute-start(f32[2,8,1,384]{3,1,2,0:T(8,128)S(1)} %get-tuple-element.127), channel_id=1, source_target_pairs={{0,1},{1,2},{2,3},{3,4},{4,5},{5,6},{6,7},{7,8},{8,9},{9,10},{10,1... | collective-permute-start | bytes 73736 | tf_op jit(solution)/shard_map/ppermute | solution.py:20
  37.9 3.5 %collective-permute-done.7 = f32[2,8,1,384]{3,1,2,0:T(8,128)S(1)} collective-permute-done((f32[2,8,1,384]{3,1,2,0:T(8,128)S(1)}, f32[2,8,1,384]{3,1,2,0:T(8,128)S(1)}, u32[]{:S(2)}, u32[]{:S(2)}) %collective-permute-start.7) | collective-permute-done | bytes 24608 | tf_op jit(solution)/shard_map/ppermute | solution.py:23
  48.4 3.1 %collective-permute-done.9 = f32[2,8,1,384]{3,1,2,0:T(8,128)S(1)} collective-permute-done((f32[2,8,1,384]{3,1,2,0:T(8,128)S(1)}, f32[2,8,1,384]{3,1,2,0:T(8,128)S(1)}, u32[]{:S(2)}, u32[]{:S(2)}) %collective-permute-start.9) | collective-permute-done | bytes 24608 | tf_op jit(solution)/shard_map/ppermute | solution.py:23
  52.1 3.4 %collective-permute-start.10 = (f32[2,8,1,384]{3,1,2,0:T(8,128)S(1)}, f32[2,8,1,384]{3,1,2,0:T(8,128)S(1)}, u32[]{:S(2)}, u32[]{:S(2)}) collective-permute-start(f32[2,8,1,384]{3,1,2,0:T(8,128)S(1)} %get-tuple-element.119), channel_id=1, source_target_pairs={{0,1},{1,2},{2,3},{3,4},{4,5},{5,6},{6,7},{7,8},{8,9},{9,10},{10,1... | collective-permute-start | bytes 73736 | tf_op jit(solution)/shard_map/ppermute | solution.py:20
  58.5 3.6 %collective-permute-done.11 = f32[2,8,1,384]{3,1,2,0:T(8,128)S(1)} collective-permute-done((f32[2,8,1,384]{3,1,2,0:T(8,128)S(1)}, f32[2,8,1,384]{3,1,2,0:T(8,128)S(1)}, u32[]{:S(2)}, u32[]{:S(2)}) %collective-permute-start.11) | collective-permute-done | bytes 24608 | tf_op jit(solution)/shard_map/ppermute | solution.py:23
  62.7 3.8 %collective-permute-start.12 = (f32[2,8,1,384]{3,1,2,0:T(8,128)S(1)}, f32[2,8,1,384]{3,1,2,0:T(8,128)S(1)}, u32[]{:S(2)}, u32[]{:S(2)}) collective-permute-start(f32[2,8,1,384]{3,1,2,0:T(8,128)S(1)} %get-tuple-element.115), channel_id=1, source_target_pairs={{0,1},{1,2},{2,3},{3,4},{4,5},{5,6},{6,7},{7,8},{8,9},{9,10},{10,1... | collective-permute-start | bytes 73736 | tf_op jit(solution)/shard_map/ppermute | solution.py:20
  69.1 4.0 %collective-permute-done.13 = f32[2,8,1,384]{3,1,2,0:T(8,128)S(1)} collective-permute-done((f32[2,8,1,384]{3,1,2,0:T(8,128)S(1)}, f32[2,8,1,384]{3,1,2,0:T(8,128)S(1)}, u32[]{:S(2)}, u32[]{:S(2)}) %collective-permute-start.13) | collective-permute-done | bytes 24608 | tf_op jit(solution)/shard_map/ppermute | solution.py:23
  74.2 5.4 %collective-permute-start.14 = (f32[6,2,8,8]{3,2,1,0:T(8,128)S(1)}, f32[6,2,8,8]{3,2,1,0:T(8,128)S(1)}, u32[]{:S(2)}, u32[]{:S(2)}) collective-permute-start(f32[6,2,8,8]{3,2,1,0:T(8,128)S(1)} %constant_dynamic-update-slice_fusion.7), channel_id=1, source_target_pairs={{0,240},{16,0},{32,16},{48,32},{64,48},{80,64},{96,80},{112,96},{1... | collective-permute-start | bytes 9224 | tf_op jit(solution)/shard_map/ppermute | solution.py:31
  82.8 3.9 %collective-permute-start.16 = (f32[2,8,1,384]{3,1,2,0:T(8,128)S(1)}, f32[2,8,1,384]{3,1,2,0:T(8,128)S(1)}, u32[]{:S(2)}, u32[]{:S(2)}) collective-permute-start(f32[2,8,1,384]{3,1,2,0:T(8,128)S(1)} %get-tuple-element.101), channel_id=1, source_target_pairs={{0,1},{1,2},{2,3},{3,4},{4,5},{5,6},{6,7},{7,8},{8,9},{9,10},{10,1... | collective-permute-start | bytes 73736 | tf_op jit(solution)/shard_map/ppermute | solution.py:20
  94.4 3.9 %collective-permute-start.18 = (f32[2,8,1,384]{3,1,2,0:T(8,128)S(1)}, f32[2,8,1,384]{3,1,2,0:T(8,128)S(1)}, u32[]{:S(2)}, u32[]{:S(2)}) collective-permute-start(f32[2,8,1,384]{3,1,2,0:T(8,128)S(1)} %get-tuple-element.97), channel_id=1, source_target_pairs={{0,1},{1,2},{2,3},{3,4},{4,5},{5,6},{6,7},{7,8},{8,9},{9,10},{10,1... | collective-permute-start | bytes 73736 | tf_op jit(solution)/shard_map/ppermute | solution.py:20
  101.0 4.0 %collective-permute-done.19 = f32[2,8,1,384]{3,1,2,0:T(8,128)S(1)} collective-permute-done((f32[2,8,1,384]{3,1,2,0:T(8,128)S(1)}, f32[2,8,1,384]{3,1,2,0:T(8,128)S(1)}, u32[]{:S(2)}, u32[]{:S(2)}) %collective-permute-start.19) | collective-permute-done | bytes 24608 | tf_op jit(solution)/shard_map/ppermute | solution.py:23
  106.1 3.4 %collective-permute-start.20 = (f32[2,8,1,384]{3,1,2,0:T(8,128)S(1)}, f32[2,8,1,384]{3,1,2,0:T(8,128)S(1)}, u32[]{:S(2)}, u32[]{:S(2)}) collective-permute-start(f32[2,8,1,384]{3,1,2,0:T(8,128)S(1)} %get-tuple-element.93), channel_id=1, source_target_pairs={{0,1},{1,2},{2,3},{3,4},{4,5},{5,6},{6,7},{7,8},{8,9},{9,10},{10,1... | collective-permute-start | bytes 73736 | tf_op jit(solution)/shard_map/ppermute | solution.py:20
  112.5 3.8 %collective-permute-done.21 = f32[2,8,1,384]{3,1,2,0:T(8,128)S(1)} collective-permute-done((f32[2,8,1,384]{3,1,2,0:T(8,128)S(1)}, f32[2,8,1,384]{3,1,2,0:T(8,128)S(1)}, u32[]{:S(2)}, u32[]{:S(2)}) %collective-permute-start.21) | collective-permute-done | bytes 24608 | tf_op jit(solution)/shard_map/ppermute | solution.py:23
  117.3 3.0 %collective-permute-start.22 = (f32[2,8,1,384]{3,1,2,0:T(8,128)S(1)}, f32[2,8,1,384]{3,1,2,0:T(8,128)S(1)}, u32[]{:S(2)}, u32[]{:S(2)}) collective-permute-start(f32[2,8,1,384]{3,1,2,0:T(8,128)S(1)} %get-tuple-element.89), channel_id=1, source_target_pairs={{0,1},{1,2},{2,3},{3,4},{4,5},{5,6},{6,7},{7,8},{8,9},{9,10},{10,1... | collective-permute-start | bytes 73736 | tf_op jit(solution)/shard_map/ppermute | solution.py:20
  123.7 3.3 %collective-permute-done.23 = f32[2,8,1,384]{3,1,2,0:T(8,128)S(1)} collective-permute-done((f32[2,8,1,384]{3,1,2,0:T(8,128)S(1)}, f32[2,8,1,384]{3,1,2,0:T(8,128)S(1)}, u32[]{:S(2)}, u32[]{:S(2)}) %collective-permute-start.23) | collective-permute-done | bytes 24608 | tf_op jit(solution)/shard_map/ppermute | solution.py:23
  128.1 3.3 %collective-permute-start.24 = (f32[2,8,1,384]{3,1,2,0:T(8,128)S(1)}, f32[2,8,1,384]{3,1,2,0:T(8,128)S(1)}, u32[]{:S(2)}, u32[]{:S(2)}) collective-permute-start(f32[2,8,1,384]{3,1,2,0:T(8,128)S(1)} %get-tuple-element.85), channel_id=1, source_target_pairs={{0,1},{1,2},{2,3},{3,4},{4,5},{5,6},{6,7},{7,8},{8,9},{9,10},{10,1... | collective-permute-start | bytes 73736 | tf_op jit(solution)/shard_map/ppermute | solution.py:20
  134.4 3.5 %collective-permute-done.25 = f32[2,8,1,384]{3,1,2,0:T(8,128)S(1)} collective-permute-done((f32[2,8,1,384]{3,1,2,0:T(8,128)S(1)}, f32[2,8,1,384]{3,1,2,0:T(8,128)S(1)}, u32[]{:S(2)}, u32[]{:S(2)}) %collective-permute-start.25) | collective-permute-done | bytes 24608 | tf_op jit(solution)/shard_map/ppermute | solution.py:23
  140.9 4.9 %collective-permute-done.26 = f32[6,2,8,8]{3,2,1,0:T(8,128)S(1)} collective-permute-done((f32[6,2,8,8]{3,2,1,0:T(8,128)S(1)}, f32[6,2,8,8]{3,2,1,0:T(8,128)S(1)}, u32[]{:S(2)}, u32[]{:S(2)}) %collective-permute-start.26) | collective-permute-done | bytes 3104 | tf_op jit(solution)/shard_map/ppermute | solution.py:31
  146.5 3.0 %collective-permute-start.28 = (f32[2,8,1,384]{3,1,2,0:T(8,128)S(1)}, f32[2,8,1,384]{3,1,2,0:T(8,128)S(1)}, u32[]{:S(2)}, u32[]{:S(2)}) collective-permute-start(f32[2,8,1,384]{3,1,2,0:T(8,128)S(1)} %get-tuple-element.49), channel_id=1, source_target_pairs={{0,1},{1,2},{2,3},{3,4},{4,5},{5,6},{6,7},{7,8},{8,9},{9,10},{10,1... | collective-permute-start | bytes 73736 | tf_op jit(solution)/shard_map/ppermute | solution.py:20
  152.8 3.3 %collective-permute-done.29 = f32[2,8,1,384]{3,1,2,0:T(8,128)S(1)} collective-permute-done((f32[2,8,1,384]{3,1,2,0:T(8,128)S(1)}, f32[2,8,1,384]{3,1,2,0:T(8,128)S(1)}, u32[]{:S(2)}, u32[]{:S(2)}) %collective-permute-start.29) | collective-permute-done | bytes 24608 | tf_op jit(solution)/shard_map/ppermute | solution.py:23
  156.7 3.1 %collective-permute-start.30 = (f32[2,8,1,384]{3,1,2,0:T(8,128)S(1)}, f32[2,8,1,384]{3,1,2,0:T(8,128)S(1)}, u32[]{:S(2)}, u32[]{:S(2)}) collective-permute-start(f32[2,8,1,384]{3,1,2,0:T(8,128)S(1)} %get-tuple-element.43), channel_id=1, source_target_pairs={{0,1},{1,2},{2,3},{3,4},{4,5},{5,6},{6,7},{7,8},{8,9},{9,10},{10,1... | collective-permute-start | bytes 73736 | tf_op jit(solution)/shard_map/ppermute | solution.py:20
  163.0 3.5 %collective-permute-done.31 = f32[2,8,1,384]{3,1,2,0:T(8,128)S(1)} collective-permute-done((f32[2,8,1,384]{3,1,2,0:T(8,128)S(1)}, f32[2,8,1,384]{3,1,2,0:T(8,128)S(1)}, u32[]{:S(2)}, u32[]{:S(2)}) %collective-permute-start.31) | collective-permute-done | bytes 24608 | tf_op jit(solution)/shard_map/ppermute | solution.py:23
  167.1 3.5 %collective-permute-start.32 = (f32[2,8,1,384]{3,1,2,0:T(8,128)S(1)}, f32[2,8,1,384]{3,1,2,0:T(8,128)S(1)}, u32[]{:S(2)}, u32[]{:S(2)}) collective-permute-start(f32[2,8,1,384]{3,1,2,0:T(8,128)S(1)} %get-tuple-element.37), channel_id=1, source_target_pairs={{0,1},{1,2},{2,3},{3,4},{4,5},{5,6},{6,7},{7,8},{8,9},{9,10},{10,1... | collective-permute-start | bytes 73736 | tf_op jit(solution)/shard_map/ppermute | solution.py:20
  173.4 3.8 %collective-permute-done.33 = f32[2,8,1,384]{3,1,2,0:T(8,128)S(1)} collective-permute-done((f32[2,8,1,384]{3,1,2,0:T(8,128)S(1)}, f32[2,8,1,384]{3,1,2,0:T(8,128)S(1)}, u32[]{:S(2)}, u32[]{:S(2)}) %collective-permute-start.33) | collective-permute-done | bytes 24608 | tf_op jit(solution)/shard_map/ppermute | solution.py:23
  177.9 3.1 %collective-permute-start.34 = (f32[2,8,1,384]{3,1,2,0:T(8,128)S(1)}, f32[2,8,1,384]{3,1,2,0:T(8,128)S(1)}, u32[]{:S(2)}, u32[]{:S(2)}) collective-permute-start(f32[2,8,1,384]{3,1,2,0:T(8,128)S(1)} %get-tuple-element.31), channel_id=1, source_target_pairs={{0,1},{1,2},{2,3},{3,4},{4,5},{5,6},{6,7},{7,8},{8,9},{9,10},{10,1... | collective-permute-start | bytes 73736 | tf_op jit(solution)/shard_map/ppermute | solution.py:20
  184.1 3.5 %collective-permute-done.35 = f32[2,8,1,384]{3,1,2,0:T(8,128)S(1)} collective-permute-done((f32[2,8,1,384]{3,1,2,0:T(8,128)S(1)}, f32[2,8,1,384]{3,1,2,0:T(8,128)S(1)}, u32[]{:S(2)}, u32[]{:S(2)}) %collective-permute-start.35) | collective-permute-done | bytes 24608 | tf_op jit(solution)/shard_map/ppermute | solution.py:23
  188.2 3.9 %collective-permute-start.36 = (f32[2,8,1,384]{3,1,2,0:T(8,128)S(1)}, f32[2,8,1,384]{3,1,2,0:T(8,128)S(1)}, u32[]{:S(2)}, u32[]{:S(2)}) collective-permute-start(f32[2,8,1,384]{3,1,2,0:T(8,128)S(1)} %get-tuple-element.25), channel_id=1, source_target_pairs={{0,1},{1,2},{2,3},{3,4},{4,5},{5,6},{6,7},{7,8},{8,9},{9,10},{10,1... | collective-permute-start | bytes 73736 | tf_op jit(solution)/shard_map/ppermute | solution.py:20
  194.5 4.2 %collective-permute-done.37 = f32[2,8,1,384]{3,1,2,0:T(8,128)S(1)} collective-permute-done((f32[2,8,1,384]{3,1,2,0:T(8,128)S(1)}, f32[2,8,1,384]{3,1,2,0:T(8,128)S(1)}, u32[]{:S(2)}, u32[]{:S(2)}) %collective-permute-start.37) | collective-permute-done | bytes 24608 | tf_op jit(solution)/shard_map/ppermute | solution.py:23
  (316 shorter events, 80.4 us)
Async XLA Ops:
  1.1 17.0 %collective-permute-start.3 = (f32[2,8,1,384]{3,1,2,0:T(8,128)S(1)}, f32[2,8,1,384]{3,1,2,0:T(8,128)S(1)}, u32[]{:S(2)}, u32[]{:S(2)}) collective-permute-start(f32[2,8,1,384]{3,1,2,0:T(8,128)S(1)} %get-tuple-element.133), channel_id=1, source_target_pairs={{1,0},{2,1},{3,2},{4,3},{5,4},{6,5},{7,6},{8,7},{9,8},{10,9},{11,1... | collective-permute-start | bytes 73736 | tf_op jit(solution)/shard_map/ppermute | solution.py:23
  5.3 12.7 %collective-permute-start.2 = (f32[2,8,1,384]{3,1,2,0:T(8,128)S(1)}, f32[2,8,1,384]{3,1,2,0:T(8,128)S(1)}, u32[]{:S(2)}, u32[]{:S(2)}) collective-permute-start(f32[2,8,1,384]{3,1,2,0:T(8,128)S(1)} %get-tuple-element.134), channel_id=1, source_target_pairs={{0,1},{1,2},{2,3},{3,4},{4,5},{5,6},{6,7},{7,8},{8,9},{9,10},{10,1... | collective-permute-start | bytes 73736 | tf_op jit(solution)/shard_map/ppermute | solution.py:20
  11.7 6.4 %collective-permute-start = (f32[7,8,1,384]{3,1,2,0:T(8,128)S(1)}, f32[7,8,1,384]{3,1,2,0:T(8,128)S(1)}, u32[]{:S(2)}, u32[]{:S(2)}) collective-permute-start(f32[7,8,1,384]{3,1,2,0:T(8,128)S(1)} %copy.7053), channel_id=1, source_target_pairs={{0,1},{1,2},{2,3},{3,4},{4,5},{5,6},{6,7},{7,8},{8,9},{9,10},{10,1... | collective-permute-start | bytes 258056 | tf_op jit(solution)/shard_map/ppermute | solution.py:20
  14.6 7.3 %collective-permute-start.1 = (f32[7,8,1,384]{3,1,2,0:T(8,128)S(1)}, f32[7,8,1,384]{3,1,2,0:T(8,128)S(1)}, u32[]{:S(2)}, u32[]{:S(2)}) collective-permute-start(f32[7,8,1,384]{3,1,2,0:T(8,128)S(1)} %copy.7054), channel_id=1, source_target_pairs={{1,0},{2,1},{3,2},{4,3},{5,4},{6,5},{7,6},{8,7},{9,8},{10,9},{11,1... | collective-permute-start | bytes 258056 | tf_op jit(solution)/shard_map/ppermute | solution.py:23
  22.8 7.0 %collective-permute-start.4 = (f32[1,5,8,10]{3,2,1,0:T(8,128)S(1)}, f32[1,5,8,10]{3,2,1,0:T(8,128)S(1)}, u32[]{:S(2)}, u32[]{:S(2)}) collective-permute-start(f32[1,5,8,10]{3,2,1,0:T(8,128)S(1)} %bitcast.487), channel_id=1, source_target_pairs={{0,16},{16,32},{32,48},{48,64},{64,80},{80,96},{96,112},{112,128},... | collective-permute-start | bytes 4808 | tf_op jit(solution)/shard_map/ppermute | solution.py:20
  22.9 6.8 %collective-permute-start.5 = (f32[1,5,8,10]{3,2,1,0:T(8,128)S(1)}, f32[1,5,8,10]{3,2,1,0:T(8,128)S(1)}, u32[]{:S(2)}, u32[]{:S(2)}) collective-permute-start(f32[1,5,8,10]{3,2,1,0:T(8,128)S(1)} %bitcast.488), channel_id=1, source_target_pairs={{16,0},{32,16},{48,32},{64,48},{80,64},{96,80},{112,96},{128,112},... | collective-permute-start | bytes 4808 | tf_op jit(solution)/shard_map/ppermute | solution.py:23
  31.4 6.5 %collective-permute-start.6 = (f32[2,8,1,384]{3,1,2,0:T(8,128)S(1)}, f32[2,8,1,384]{3,1,2,0:T(8,128)S(1)}, u32[]{:S(2)}, u32[]{:S(2)}) collective-permute-start(f32[2,8,1,384]{3,1,2,0:T(8,128)S(1)} %get-tuple-element.127), channel_id=1, source_target_pairs={{0,1},{1,2},{2,3},{3,4},{4,5},{5,6},{6,7},{7,8},{8,9},{9,10},{10,1... | collective-permute-start | bytes 73736 | tf_op jit(solution)/shard_map/ppermute | solution.py:20
  34.8 6.6 %collective-permute-start.7 = (f32[2,8,1,384]{3,1,2,0:T(8,128)S(1)}, f32[2,8,1,384]{3,1,2,0:T(8,128)S(1)}, u32[]{:S(2)}, u32[]{:S(2)}) collective-permute-start(f32[2,8,1,384]{3,1,2,0:T(8,128)S(1)} %get-tuple-element.128), channel_id=1, source_target_pairs={{1,0},{2,1},{3,2},{4,3},{5,4},{6,5},{7,6},{8,7},{9,8},{10,9},{11,1... | collective-permute-start | bytes 73736 | tf_op jit(solution)/shard_map/ppermute | solution.py:23
  42.0 6.4 %collective-permute-start.8 = (f32[2,8,1,384]{3,1,2,0:T(8,128)S(1)}, f32[2,8,1,384]{3,1,2,0:T(8,128)S(1)}, u32[]{:S(2)}, u32[]{:S(2)}) collective-permute-start(f32[2,8,1,384]{3,1,2,0:T(8,128)S(1)} %get-tuple-element.123), channel_id=1, source_target_pairs={{0,1},{1,2},{2,3},{3,4},{4,5},{5,6},{6,7},{7,8},{8,9},{9,10},{10,1... | collective-permute-start | bytes 73736 | tf_op jit(solution)/shard_map/ppermute | solution.py:20
  44.9 6.6 %collective-permute-start.9 = (f32[2,8,1,384]{3,1,2,0:T(8,128)S(1)}, f32[2,8,1,384]{3,1,2,0:T(8,128)S(1)}, u32[]{:S(2)}, u32[]{:S(2)}) collective-permute-start(f32[2,8,1,384]{3,1,2,0:T(8,128)S(1)} %get-tuple-element.124), channel_id=1, source_target_pairs={{1,0},{2,1},{3,2},{4,3},{5,4},{6,5},{7,6},{8,7},{9,8},{10,9},{11,1... | collective-permute-start | bytes 73736 | tf_op jit(solution)/shard_map/ppermute | solution.py:23
  52.1 6.4 %collective-permute-start.10 = (f32[2,8,1,384]{3,1,2,0:T(8,128)S(1)}, f32[2,8,1,384]{3,1,2,0:T(8,128)S(1)}, u32[]{:S(2)}, u32[]{:S(2)}) collective-permute-start(f32[2,8,1,384]{3,1,2,0:T(8,128)S(1)} %get-tuple-element.119), channel_id=1, source_target_pairs={{0,1},{1,2},{2,3},{3,4},{4,5},{5,6},{6,7},{7,8},{8,9},{9,10},{10,1... | collective-permute-start | bytes 73736 | tf_op jit(solution)/shard_map/ppermute | solution.py:20
  55.5 6.6 %collective-permute-start.11 = (f32[2,8,1,384]{3,1,2,0:T(8,128)S(1)}, f32[2,8,1,384]{3,1,2,0:T(8,128)S(1)}, u32[]{:S(2)}, u32[]{:S(2)}) collective-permute-start(f32[2,8,1,384]{3,1,2,0:T(8,128)S(1)} %get-tuple-element.120), channel_id=1, source_target_pairs={{1,0},{2,1},{3,2},{4,3},{5,4},{6,5},{7,6},{8,7},{9,8},{10,9},{11,1... | collective-permute-start | bytes 73736 | tf_op jit(solution)/shard_map/ppermute | solution.py:23
  62.7 6.4 %collective-permute-start.12 = (f32[2,8,1,384]{3,1,2,0:T(8,128)S(1)}, f32[2,8,1,384]{3,1,2,0:T(8,128)S(1)}, u32[]{:S(2)}, u32[]{:S(2)}) collective-permute-start(f32[2,8,1,384]{3,1,2,0:T(8,128)S(1)} %get-tuple-element.115), channel_id=1, source_target_pairs={{0,1},{1,2},{2,3},{3,4},{4,5},{5,6},{6,7},{7,8},{8,9},{9,10},{10,1... | collective-permute-start | bytes 73736 | tf_op jit(solution)/shard_map/ppermute | solution.py:20
  66.5 6.6 %collective-permute-start.13 = (f32[2,8,1,384]{3,1,2,0:T(8,128)S(1)}, f32[2,8,1,384]{3,1,2,0:T(8,128)S(1)}, u32[]{:S(2)}, u32[]{:S(2)}) collective-permute-start(f32[2,8,1,384]{3,1,2,0:T(8,128)S(1)} %get-tuple-element.116), channel_id=1, source_target_pairs={{1,0},{2,1},{3,2},{4,3},{5,4},{6,5},{7,6},{8,7},{9,8},{10,9},{11,1... | collective-permute-start | bytes 73736 | tf_op jit(solution)/shard_map/ppermute | solution.py:23
  74.1 7.2 %collective-permute-start.15 = (f32[6,2,8,8]{3,2,1,0:T(8,128)S(1)}, f32[6,2,8,8]{3,2,1,0:T(8,128)S(1)}, u32[]{:S(2)}, u32[]{:S(2)}) collective-permute-start(f32[6,2,8,8]{3,2,1,0:T(8,128)S(1)} %constant_dynamic-update-slice_fusion.13), channel_id=1, source_target_pairs={{0,16},{16,32},{32,48},{48,64},{64,80},{80,96},{96,112},{112,128},... | collective-permute-start | bytes 9224 | tf_op jit(solution)/shard_map/ppermute | solution.py:31
  74.2 7.3 %collective-permute-start.14 = (f32[6,2,8,8]{3,2,1,0:T(8,128)S(1)}, f32[6,2,8,8]{3,2,1,0:T(8,128)S(1)}, u32[]{:S(2)}, u32[]{:S(2)}) collective-permute-start(f32[6,2,8,8]{3,2,1,0:T(8,128)S(1)} %constant_dynamic-update-slice_fusion.7), channel_id=1, source_target_pairs={{0,240},{16,0},{32,16},{48,32},{64,48},{80,64},{96,80},{112,96},{1... | collective-permute-start | bytes 9224 | tf_op jit(solution)/shard_map/ppermute | solution.py:31
  82.8 8.0 %collective-permute-start.16 = (f32[2,8,1,384]{3,1,2,0:T(8,128)S(1)}, f32[2,8,1,384]{3,1,2,0:T(8,128)S(1)}, u32[]{:S(2)}, u32[]{:S(2)}) collective-permute-start(f32[2,8,1,384]{3,1,2,0:T(8,128)S(1)} %get-tuple-element.101), channel_id=1, source_target_pairs={{0,1},{1,2},{2,3},{3,4},{4,5},{5,6},{6,7},{7,8},{8,9},{9,10},{10,1... | collective-permute-start | bytes 73736 | tf_op jit(solution)/shard_map/ppermute | solution.py:20
  86.7 6.6 %collective-permute-start.17 = (f32[2,8,1,384]{3,1,2,0:T(8,128)S(1)}, f32[2,8,1,384]{3,1,2,0:T(8,128)S(1)}, u32[]{:S(2)}, u32[]{:S(2)}) collective-permute-start(f32[2,8,1,384]{3,1,2,0:T(8,128)S(1)} %get-tuple-element.102), channel_id=1, source_target_pairs={{1,0},{2,1},{3,2},{4,3},{5,4},{6,5},{7,6},{8,7},{9,8},{10,9},{11,1... | collective-permute-start | bytes 73736 | tf_op jit(solution)/shard_map/ppermute | solution.py:23
  94.4 6.6 %collective-permute-start.18 = (f32[2,8,1,384]{3,1,2,0:T(8,128)S(1)}, f32[2,8,1,384]{3,1,2,0:T(8,128)S(1)}, u32[]{:S(2)}, u32[]{:S(2)}) collective-permute-start(f32[2,8,1,384]{3,1,2,0:T(8,128)S(1)} %get-tuple-element.97), channel_id=1, source_target_pairs={{0,1},{1,2},{2,3},{3,4},{4,5},{5,6},{6,7},{7,8},{8,9},{9,10},{10,1... | collective-permute-start | bytes 73736 | tf_op jit(solution)/shard_map/ppermute | solution.py:20
  98.4 6.6 %collective-permute-start.19 = (f32[2,8,1,384]{3,1,2,0:T(8,128)S(1)}, f32[2,8,1,384]{3,1,2,0:T(8,128)S(1)}, u32[]{:S(2)}, u32[]{:S(2)}) collective-permute-start(f32[2,8,1,384]{3,1,2,0:T(8,128)S(1)} %get-tuple-element.98), channel_id=1, source_target_pairs={{1,0},{2,1},{3,2},{4,3},{5,4},{6,5},{7,6},{8,7},{9,8},{10,9},{11,1... | collective-permute-start | bytes 73736 | tf_op jit(solution)/shard_map/ppermute | solution.py:23
  106.1 6.4 %collective-permute-start.20 = (f32[2,8,1,384]{3,1,2,0:T(8,128)S(1)}, f32[2,8,1,384]{3,1,2,0:T(8,128)S(1)}, u32[]{:S(2)}, u32[]{:S(2)}) collective-permute-start(f32[2,8,1,384]{3,1,2,0:T(8,128)S(1)} %get-tuple-element.93), channel_id=1, source_target_pairs={{0,1},{1,2},{2,3},{3,4},{4,5},{5,6},{6,7},{7,8},{8,9},{9,10},{10,1... | collective-permute-start | bytes 73736 | tf_op jit(solution)/shard_map/ppermute | solution.py:20
  109.5 6.7 %collective-permute-start.21 = (f32[2,8,1,384]{3,1,2,0:T(8,128)S(1)}, f32[2,8,1,384]{3,1,2,0:T(8,128)S(1)}, u32[]{:S(2)}, u32[]{:S(2)}) collective-permute-start(f32[2,8,1,384]{3,1,2,0:T(8,128)S(1)} %get-tuple-element.94), channel_id=1, source_target_pairs={{1,0},{2,1},{3,2},{4,3},{5,4},{6,5},{7,6},{8,7},{9,8},{10,9},{11,1... | collective-permute-start | bytes 73736 | tf_op jit(solution)/shard_map/ppermute | solution.py:23
  117.3 6.4 %collective-permute-start.22 = (f32[2,8,1,384]{3,1,2,0:T(8,128)S(1)}, f32[2,8,1,384]{3,1,2,0:T(8,128)S(1)}, u32[]{:S(2)}, u32[]{:S(2)}) collective-permute-start(f32[2,8,1,384]{3,1,2,0:T(8,128)S(1)} %get-tuple-element.89), channel_id=1, source_target_pairs={{0,1},{1,2},{2,3},{3,4},{4,5},{5,6},{6,7},{7,8},{8,9},{9,10},{10,1... | collective-permute-start | bytes 73736 | tf_op jit(solution)/shard_map/ppermute | solution.py:20
  120.3 6.6 %collective-permute-start.23 = (f32[2,8,1,384]{3,1,2,0:T(8,128)S(1)}, f32[2,8,1,384]{3,1,2,0:T(8,128)S(1)}, u32[]{:S(2)}, u32[]{:S(2)}) collective-permute-start(f32[2,8,1,384]{3,1,2,0:T(8,128)S(1)} %get-tuple-element.90), channel_id=1, source_target_pairs={{1,0},{2,1},{3,2},{4,3},{5,4},{6,5},{7,6},{8,7},{9,8},{10,9},{11,1... | collective-permute-start | bytes 73736 | tf_op jit(solution)/shard_map/ppermute | solution.py:23
  128.1 6.4 %collective-permute-start.24 = (f32[2,8,1,384]{3,1,2,0:T(8,128)S(1)}, f32[2,8,1,384]{3,1,2,0:T(8,128)S(1)}, u32[]{:S(2)}, u32[]{:S(2)}) collective-permute-start(f32[2,8,1,384]{3,1,2,0:T(8,128)S(1)} %get-tuple-element.85), channel_id=1, source_target_pairs={{0,1},{1,2},{2,3},{3,4},{4,5},{5,6},{6,7},{7,8},{8,9},{9,10},{10,1... | collective-permute-start | bytes 73736 | tf_op jit(solution)/shard_map/ppermute | solution.py:20
  131.3 6.6 %collective-permute-start.25 = (f32[2,8,1,384]{3,1,2,0:T(8,128)S(1)}, f32[2,8,1,384]{3,1,2,0:T(8,128)S(1)}, u32[]{:S(2)}, u32[]{:S(2)}) collective-permute-start(f32[2,8,1,384]{3,1,2,0:T(8,128)S(1)} %get-tuple-element.86), channel_id=1, source_target_pairs={{1,0},{2,1},{3,2},{4,3},{5,4},{6,5},{7,6},{8,7},{9,8},{10,9},{11,1... | collective-permute-start | bytes 73736 | tf_op jit(solution)/shard_map/ppermute | solution.py:23
  138.6 7.1 %collective-permute-start.26 = (f32[6,2,8,8]{3,2,1,0:T(8,128)S(1)}, f32[6,2,8,8]{3,2,1,0:T(8,128)S(1)}, u32[]{:S(2)}, u32[]{:S(2)}) collective-permute-start(f32[6,2,8,8]{3,2,1,0:T(8,128)S(1)} %constant_dynamic-update-slice_fusion.19), channel_id=1, source_target_pairs={{0,16},{16,32},{32,48},{48,64},{64,80},{80,96},{96,112},{112,128},... | collective-permute-start | bytes 9224 | tf_op jit(solution)/shard_map/ppermute | solution.py:31
  149.5 6.6 %collective-permute-start.29 = (f32[2,8,1,384]{3,1,2,0:T(8,128)S(1)}, f32[2,8,1,384]{3,1,2,0:T(8,128)S(1)}, u32[]{:S(2)}, u32[]{:S(2)}) collective-permute-start(f32[2,8,1,384]{3,1,2,0:T(8,128)S(1)} %get-tuple-element.50), channel_id=1, source_target_pairs={{1,0},{2,1},{3,2},{4,3},{5,4},{6,5},{7,6},{8,7},{9,8},{10,9},{11,1... | collective-permute-start | bytes 73736 | tf_op jit(solution)/shard_map/ppermute | solution.py:23
  159.9 6.6 %collective-permute-start.31 = (f32[2,8,1,384]{3,1,2,0:T(8,128)S(1)}, f32[2,8,1,384]{3,1,2,0:T(8,128)S(1)}, u32[]{:S(2)}, u32[]{:S(2)}) collective-permute-start(f32[2,8,1,384]{3,1,2,0:T(8,128)S(1)} %get-tuple-element.44), channel_id=1, source_target_pairs={{1,0},{2,1},{3,2},{4,3},{5,4},{6,5},{7,6},{8,7},{9,8},{10,9},{11,1... | collective-permute-start | bytes 73736 | tf_op jit(solution)/shard_map/ppermute | solution.py:23
  170.6 6.6 %collective-permute-start.33 = (f32[2,8,1,384]{3,1,2,0:T(8,128)S(1)}, f32[2,8,1,384]{3,1,2,0:T(8,128)S(1)}, u32[]{:S(2)}, u32[]{:S(2)}) collective-permute-start(f32[2,8,1,384]{3,1,2,0:T(8,128)S(1)} %get-tuple-element.38), channel_id=1, source_target_pairs={{1,0},{2,1},{3,2},{4,3},{5,4},{6,5},{7,6},{8,7},{9,8},{10,9},{11,1... | collective-permute-start | bytes 73736 | tf_op jit(solution)/shard_map/ppermute | solution.py:23
  181.0 6.6 %collective-permute-start.35 = (f32[2,8,1,384]{3,1,2,0:T(8,128)S(1)}, f32[2,8,1,384]{3,1,2,0:T(8,128)S(1)}, u32[]{:S(2)}, u32[]{:S(2)}) collective-permute-start(f32[2,8,1,384]{3,1,2,0:T(8,128)S(1)} %get-tuple-element.32), channel_id=1, source_target_pairs={{1,0},{2,1},{3,2},{4,3},{5,4},{6,5},{7,6},{8,7},{9,8},{10,9},{11,1... | collective-permute-start | bytes 73736 | tf_op jit(solution)/shard_map/ppermute | solution.py:23
  192.2 6.6 %collective-permute-start.37 = (f32[2,8,1,384]{3,1,2,0:T(8,128)S(1)}, f32[2,8,1,384]{3,1,2,0:T(8,128)S(1)}, u32[]{:S(2)}, u32[]{:S(2)}) collective-permute-start(f32[2,8,1,384]{3,1,2,0:T(8,128)S(1)} %get-tuple-element.26), channel_id=1, source_target_pairs={{1,0},{2,1},{3,2},{4,3},{5,4},{6,5},{7,6},{8,7},{9,8},{10,9},{11,1... | collective-permute-start | bytes 73736 | tf_op jit(solution)/shard_map/ppermute | solution.py:23
  (12 other events, 47.8 us)
where the time goes:
time: 201 us; the launch traced here: 200 us
  starting transfers between devices  106 us (53%)
  waiting for transfers between devices  62.7 us (31%)
  local copies, waits for them, and re-layouts  20.2 us (10%)
  other arithmetic  9.89 us (5%)
    ppermute x17, waiting for transfers between devices, extended(): lax.ppermute(lax.slice_in_dim(block, 0, width, axis=dim), axis, backward)  54.6 us
    ppermute x17, starting transfers between devices, extended(): lax.ppermute(lax.slice_in_dim(block, block.shape[dim] - width, None, axis...  53.3 us
    ppermute x17, starting transfers between devices, extended(): lax.ppermute(lax.slice_in_dim(block, 0, width, axis=dim), axis, backward)  46.7 us
    ppermute x4, waiting for transfers between devices, passed_along(): return lax.ppermute(value, axis, pairs)  8.03 us
    ppermute x4, starting transfers between devices, passed_along(): return lax.ppermute(value, axis, pairs)  5.91 us
    unnamed x28, local copies, waits for them, and re-layouts  5.82 us
  transfers between devices with their start and end apart: 38, of which 19 were waited for; matrix products, arithmetic and copies ran while one was open for 5% of the time, Pallas kernels for 0%

commit v1 on v0

v1 whole, which is shorter than its diff:
```python
import jax
import jax.numpy as jnp
from jax import lax
from jax.experimental import pallas as pl
from jax.experimental.pallas import tpu as pltpu
from jax.sharding import PartitionSpec as P

STEPS = 6
HALO = 6
LANES = 128
EDGE = 8

ROBIN_WEIGHT = 0.5
FACTOR_A = 1.0 - ROBIN_WEIGHT / 2.0
FACTOR_B = 1.0 + ROBIN_WEIGHT / 2.0

U, V, K, KZ, M = 2, 3, 4, 5, 6
FIELDS = 7

TO_NORTH = [(f, r) for f in (0, 1, V, K, M) for r in range(2, 8)] + [
    (f, r) for f in (U, KZ) for r in range(3, 8)
]
TO_SOUTH = [(f, r) for f in (0, 1, M) for r in range(6)] + [
    (f, r) for f in (U, V, K, KZ) for r in range(5)
]


def lane_of():
    return lax.broadcasted_iota(jnp.int32, (8, LANES), 1)


def level_of():
    return lax.broadcasted_iota(jnp.int32, (8, LANES), 0)


def pack_kernel(tracers, speed_east, speed_north, diff_horiz, diff_vert, sea, own, north, south, edges):
    tiles = own.shape[-1] // LANES
    lane = lane_of()
    sources = (
        tracers.at[0],
        tracers.at[1],
        speed_east,
        speed_north,
        diff_horiz,
        diff_vert,
        sea,
    )
    for f, source in enumerate(sources):
        edge = jnp.zeros((8, LANES), jnp.float32)
        for r in range(8):
            for k in range(tiles):
                cols = pl.ds(k * LANES, LANES)
                value = source[pl.ds(8 * k + r, 8, stride=8 * tiles), :].astype(jnp.float32)
                own[f, r, :, cols] = value
                if (f, r) in TO_NORTH:
                    north[TO_NORTH.index((f, r)), :, cols] = value
                if (f, r) in TO_SOUTH:
                    south[TO_SOUTH.index((f, r)), :, cols] = value
                if k == 0:
                    shift = EDGE * r
                    moved = pltpu.roll(value, shift, 1) if shift else value
                    edge = jnp.where((lane >= shift) & (lane < shift + EDGE), moved, edge)
                if k == tiles - 1:
                    first = LANES // 2 + EDGE * r
                    shift = (first - (LANES - EDGE)) % LANES
                    moved = pltpu.roll(value, shift, 1) if shift else value
                    edge = jnp.where((lane >= first) & (lane < first + EDGE), moved, edge)
        edges[f] = edge


def solve_kernel(
    own, from_south, from_north, side_own, side_south, side_north, out,
    field, coef, state, strip, robin,
):
    width = own.shape[-1]
    tiles = width // LANES
    ring = tiles + 1
    rows = 8 + 2 * HALO
    lane = lane_of()
    level = level_of()
    first = lane == 0
    last = lane == LANES - 1
    low_half = lane < LANES // 2

    def west(value, beside):
        return pltpu.roll(jnp.where(last, beside, value), 1, 1)

    def east(value, beside):
        return pltpu.roll(jnp.where(first, beside, value), LANES - 1, 1)

    def across(value):
        return jnp.where(low_half, pltpu.roll(value, 1, 1), pltpu.roll(value, LANES - 1, 1))

    for f in range(FIELDS):
        for r in range(8):
            field[f, HALO + r, :, pl.ds(0, width)] = own[f, r]
    for i, (f, r) in enumerate(TO_NORTH):
        field[f, r - 2, :, pl.ds(0, width)] = from_south[i]
    for i, (f, r) in enumerate(TO_SOUTH):
        field[f, HALO + 8 + r, :, pl.ds(0, width)] = from_north[i]

    for f in range(FIELDS):
        for source, begin, shown in (
            (side_south, 2, 0),
            (side_own, 0, HALO),
            (side_north, 0, HALO + 8),
        ):
            packed = source[f]
            for i in range(8 if shown == HALO else HALO):
                r = begin + i
                low = pltpu.roll(packed, (LANES - EDGE * r) % LANES, 1) if r else packed
                shift = (LANES // 2 - EDGE * (r + 1)) % LANES
                high = pltpu.roll(packed, shift, 1) if shift else packed
                kept = jnp.where(lane < EDGE, low, jnp.where(lane >= LANES - EDGE, high, 0.0))
                field[f, shown + i, :, pl.ds(width, LANES)] = kept

    def get(ref, f, e, k):
        return ref[f, e, :, pl.ds((k % ring) * LANES, LANES)]

    def north_face(e, k):
        speed = get(field, V, e, k)
        diff = get(field, K, e, k)
        both = get(field, M, e, k) * get(field, M, e + 1, k)
        return (jnp.maximum(speed, 0.0) + diff) * both, (jnp.minimum(speed, 0.0) - diff) * both

    def table_row(e, carry):
        faces = []
        for k in range(ring):
            sea = get(field, M, e, k)
            both = sea * east(sea, get(field, M, e, k + 1))
            speed = get(field, U, e, k)
            diff = get(field, K, e, k)
            faces.append(
                ((jnp.maximum(speed, 0.0) + diff) * both, (jnp.minimum(speed, 0.0) - diff) * both)
            )
        for k in range(ring):
            here, there = faces[k]
            here_west = west(here, faces[k - 1][0])
            there_west = west(there, faces[k - 1][1])
            north_here, north_there = north_face(e, k)
            south_here, south_there = north_face(e - 1, k)
            sea = get(field, M, e, k)
            beneath = jnp.where(level == 7, 0.0, pltpu.roll(sea, 7, 0))
            below = get(field, KZ, e, k) * sea * beneath
            above = pltpu.roll(below, 1, 0)
            centre = sea - (
                here - there_west + north_here - south_there + below + above
            )
            cols = pl.ds(k * LANES, LANES)
            for i, value in enumerate(
                (centre, -there, here_west, -north_there, south_here, below, above)
            ):
                coef[i, e, :, cols] = value
        return carry

    lax.fori_loop(1, rows - 1, table_row, 0)

    def stencil(weights, value, to_east, to_west, to_north, to_south):
        centre, w_east, w_west, w_north, w_south, w_below, w_above = weights
        return (
            (centre * value + w_east * to_east)
            + (w_west * to_west + w_north * to_north)
            + (w_south * to_south + w_below * pltpu.roll(value, 7, 0))
            + w_above * pltpu.roll(value, 1, 0)
        )

    def side_weights(e, i):
        return jnp.where(low_half, get(coef, i, e, 0), get(coef, i, e, tiles - 1))

    def fill(e, carry):
        for t in range(2):
            strip[0, 0, t, e] = jnp.where(low_half, get(field, t, e, 0), get(field, t, e, tiles - 1))
            strip[1, 0, t, e] = get(field, t, e, tiles)
        return carry

    lax.fori_loop(1, rows - 1, fill, 0)

    for n in range(STEPS):
        now, later = n % 2, (n + 1) % 2

        def traces(e, carry, n=n, now=now):
            for t in range(2):
                mine = strip[0, now, t, e]
                ghost = across(get(field, t, e, tiles))
                told = across(FACTOR_B * mine - FACTOR_A * ghost)
                theirs = strip[1, now, t, e]
                ghost = (told + FACTOR_A * theirs) * (1.0 / FACTOR_B)
                robin[0, n, t, e] = ghost
                robin[1, n, t, e] = across(FACTOR_B * theirs - FACTOR_A * ghost) * (1.0 / FACTOR_B)
            return carry

        lax.fori_loop(1 + n, rows - 1 - n, traces, 0, unroll=2)
        if n == STEPS - 1:
            break

        def advance(e, carry, n=n, now=now, later=later):
            own_weights = [side_weights(e, i) for i in range(7)]
            side = [get(coef, i, e, tiles) for i in range(7)]
            for t in range(2):
                mine = strip[0, now, t, e]
                beside = get(field, t, e, tiles)
                strip[0, later, t, e] = stencil(
                    own_weights, mine, east(mine, beside), west(mine, beside),
                    strip[0, now, t, e + 1], strip[0, now, t, e - 1],
                )
                theirs = strip[1, now, t, e]
                ghost = robin[0, n, t, e]
                strip[1, later, t, e] = stencil(
                    side, theirs,
                    jnp.where(last, ghost, pltpu.roll(theirs, LANES - 1, 1)),
                    jnp.where(first, ghost, pltpu.roll(theirs, 1, 1)),
                    strip[1, now, t, e + 1], strip[1, now, t, e - 1],
                )
            return carry

        lax.fori_loop(2 + n, rows - 2 - n, advance, 0, unroll=2)

    for n in range(STEPS):
        def sweep(e, carry, n=n):
            source = (lambda t, e, k: get(field, t, e, k)) if n == 0 else (
                lambda t, e, k: state[n % 2, t, e, :, pl.ds(k * LANES, LANES)]
            )
            for k in range(tiles):
                weights = [get(coef, i, e, k) for i in range(7)]
                for t in range(2):
                    value = source(t, e, k)
                    if k == 0:
                        ghost = robin[1, n, t, e] + (FACTOR_A / FACTOR_B) * value
                        to_west = jnp.where(first, ghost, pltpu.roll(value, 1, 1))
                    else:
                        to_west = west(value, source(t, e, k - 1))
                    if k == tiles - 1:
                        ghost = robin[1, n, t, e] + (FACTOR_A / FACTOR_B) * value
                        to_east = jnp.where(last, ghost, pltpu.roll(value, LANES - 1, 1))
                    else:
                        to_east = east(value, source(t, e, k + 1))
                    stepped = stencil(
                        weights, value, to_east, to_west, source(t, e + 1, k), source(t, e - 1, k)
                    )
                    cols = pl.ds(k * LANES, LANES)
                    if n == STEPS - 1:
                        out[t, pl.ds(8 * k + e - HALO, 8, stride=8 * tiles), :] = stepped
                    else:
                        state[(n + 1) % 2, t, e, :, cols] = stepped
            return carry

        if n == STEPS - 1:
            for e in range(HALO, HALO + 8):
                sweep(e, 0)
        else:
            lax.fori_loop(1 + n, rows - 1 - n, sweep, 0, unroll=2)


def in_vmem(count):
    return [pl.BlockSpec(memory_space=pltpu.VMEM)] * count


def in_tiles(array):
    lead = array.shape[:-2]
    tiled = array.reshape(lead + (8, -1, LANES))
    return jnp.swapaxes(tiled, -3, -2).reshape(lead[:-1] + (-1, LANES))


def from_tiles(array, shape):
    tiled = array.reshape(shape[:-2] + (-1, 8, LANES))
    return jnp.swapaxes(tiled, -3, -2).reshape(shape)


def shards(tracers, speed_east, speed_north, diff_horiz, diff_vert, sea_mask):
    shape = tracers.shape
    width = shape[-1]
    rows = 8 + 2 * HALO
    f32 = jnp.float32
    flat = [
        in_tiles(a) for a in (tracers, speed_east, speed_north, diff_horiz, diff_vert, sea_mask)
    ]
    own, north, south, edges = pl.pallas_call(
        pack_kernel,
        out_shape=(
            jax.ShapeDtypeStruct((FIELDS, 8, 8, width), f32),
            jax.ShapeDtypeStruct((len(TO_NORTH), 8, width), f32),
            jax.ShapeDtypeStruct((len(TO_SOUTH), 8, width), f32),
            jax.ShapeDtypeStruct((FIELDS, 8, LANES), f32),
        ),
        in_specs=in_vmem(6),
        out_specs=tuple(in_vmem(4)),
        name="pack",
    )(*flat)

    count_m = lax.axis_size("merid")
    up = [(i, i + 1) for i in range(count_m - 1)]
    down = [(b, a) for a, b in up]
    count_z = lax.axis_size("zonal")
    onward = [(i, (i + 1) % count_z) for i in range(count_z)]
    back = [(b, a) for a, b in onward]

    from_south = lax.ppermute(north, "merid", up)
    from_north = lax.ppermute(south, "merid", down)
    from_west = lax.ppermute(edges, "zonal", onward)
    from_east = lax.ppermute(edges, "zonal", back)
    lane = lax.broadcasted_iota(jnp.int32, edges.shape, 2)
    side_own = jnp.where(lane < LANES // 2, from_east, from_west)
    side_south = lax.ppermute(side_own, "merid", up)
    side_north = lax.ppermute(side_own, "merid", down)

    ring = width + LANES
    result = pl.pallas_call(
        solve_kernel,
        out_shape=jax.ShapeDtypeStruct(flat[0].shape, f32),
        in_specs=in_vmem(6),
        out_specs=in_vmem(1)[0],
        scratch_shapes=[
            pltpu.VMEM((FIELDS, rows, 8, ring), f32),
            pltpu.VMEM((7, rows, 8, ring), f32),
            pltpu.VMEM((2, 2, rows, 8, width), f32),
            pltpu.VMEM((2, 2, 2, rows, 8, LANES), f32),
            pltpu.VMEM((2, STEPS, 2, rows, 8, LANES), f32),
        ],
        compiler_params=pltpu.CompilerParams(vmem_limit_bytes=24 * 1024 * 1024),
        name="solve",
    )(own, from_south, from_north, side_own, side_south, side_north)
    return from_tiles(result, shape)


def solution(mesh):
    row = P(None, "merid", "zonal")
    whole = P(None, None, "merid", "zonal")
    return jax.shard_map(
        shards, mesh=mesh, in_specs=(whole, row, row, row, row, row), out_specs=whole, check_vma=False
    )
```

time: 201 us -> 66.9 us (0.33)
  the two profiles are of different devices: /device:TPU:2 before, /device:TPU:98 now
where the time goes in v1:
time: 66.9 us; the launch traced here: 66.7 us
  waiting for transfers between devices  24.7 us (37%)
  Pallas kernels  23.5 us (35%)
  starting transfers between devices  17.3 us (26%)
  local copies, waits for them, and re-layouts  1.1 us (2%)
    pallas_call x1, Pallas kernels, shards(): pl.pallas_call(solve_kernel, out_shape=jax.ShapeDtypeStruct(flat[0].shape...  21 us
    ppermute x1, waiting for transfers between devices, shards(): from_east = lax.ppermute(edges, 'zonal', back)  13.6 us
    ppermute x1, waiting for transfers between devices, shards(): side_north = lax.ppermute(side_own, 'merid', down)  5.93 us
    ppermute x1, waiting for transfers between devices, shards(): from_west = lax.ppermute(edges, 'zonal', onward)  5.23 us
    ppermute x1, starting transfers between devices, shards(): from_south = lax.ppermute(north, 'merid', up)  5 us
    ppermute x1, starting transfers between devices, shards(): side_south = lax.ppermute(side_own, 'merid', up)  4.31 us
    ppermute x1, starting transfers between devices, shards(): from_east = lax.ppermute(edges, 'zonal', back)  4.1 us
    pallas_call x1, Pallas kernels, shards(): pl.pallas_call(pack_kernel, out_shape=(jax.ShapeDtypeStruct((FIELDS, 8, 8...  2.51 us
  transfers between devices with their start and end apart: 6, of which 3 were waited for; matrix products, arithmetic and copies ran while one was open for 0% of the time, Pallas kernels for 0%

profile of v1, /device:TPU:98, one launch (start us, length us, event | category | flops | bytes accessed | tf_op | source)
XLA Modules:
  0.0 66.7 jit_solution(5086653520833864471)
XLA Ops:
  0.0 2.5 %pack.1 = (f32[7,8,8,384]{3,2,1,0:T(8,128)}, f32[40,8,384]{2,1,0:T(8,128)}, f32[38,8,384]{2,1,0:T(8,128)}, f32[7,8,128]{2,1,0:T(8,128)}) custom-call(f32[2,192,128]{2,1,0:T(8,128)} %bitcast.35, f32[192,128]{1,0:T(8,128)} %bitcast.36, f32[192,128]{1,0:T(8,128)} %bitcast.37, f32[192,128]{1,0:T(8,128)} %bitcast.38, f32[192,128]{1,0:T(8,128)} %bitcast.39, ...), custom_call_target="tpu_custom_call" | custom-call | tf_op jit(solution)/shard_map/pack/pallas_call | solution.py:277
  2.5 5.0 %collective-permute-start = (f32[40,8,384]{2,1,0:T(8,128)}, f32[40,8,384]{2,1,0:T(8,128)S(1)}, u32[]{:S(2)}, u32[]{:S(2)}) collective-permute-start(f32[40,8,384]{2,1,0:T(8,128)} %get-tuple-element.10), channel_id=1, source_target_pairs={{0,1},{1,2},{2,3},{3,4},{4,5},{5,6},{6,7},{7,8},{8,9},{9,10},{10,1... | collective-permute-start | bytes 1474568 | tf_op jit(solution)/shard_map/ppermute | solution.py:297
  7.5 1.9 %collective-permute-start.1 = (f32[38,8,384]{2,1,0:T(8,128)}, f32[38,8,384]{2,1,0:T(8,128)S(1)}, u32[]{:S(2)}, u32[]{:S(2)}) collective-permute-start(f32[38,8,384]{2,1,0:T(8,128)} %get-tuple-element.11), channel_id=1, source_target_pairs={{1,0},{2,1},{3,2},{4,3},{5,4},{6,5},{7,6},{8,7},{9,8},{10,9},{11,1... | collective-permute-start | bytes 1400840 | tf_op jit(solution)/shard_map/ppermute | solution.py:298
  9.4 4.1 %collective-permute-start.2 = (f32[7,8,128]{2,1,0:T(8,128)}, f32[7,8,128]{2,1,0:T(8,128)S(1)}, u32[]{:S(2)}, u32[]{:S(2)}) collective-permute-start(f32[7,8,128]{2,1,0:T(8,128)} %get-tuple-element.12), channel_id=1, source_target_pairs={{16,0},{32,16},{48,32},{64,48},{80,64},{96,80},{112,96},{128,112},... | collective-permute-start | bytes 86024 | tf_op jit(solution)/shard_map/ppermute | solution.py:300
  13.6 0.0 collective-permute-start.3
  13.6 13.6 %collective-permute-done.2 = f32[7,8,128]{2,1,0:T(8,128)S(1)} collective-permute-done((f32[7,8,128]{2,1,0:T(8,128)}, f32[7,8,128]{2,1,0:T(8,128)S(1)}, u32[]{:S(2)}, u32[]{:S(2)}) %collective-permute-start.2) | collective-permute-done | bytes 28704 | tf_op jit(solution)/shard_map/ppermute | solution.py:300
  27.1 5.2 %collective-permute-done.3 = f32[7,8,128]{2,1,0:T(8,128)S(1)} collective-permute-done((f32[7,8,128]{2,1,0:T(8,128)}, f32[7,8,128]{2,1,0:T(8,128)S(1)}, u32[]{:S(2)}, u32[]{:S(2)}) %collective-permute-start.3) | collective-permute-done | bytes 28704 | tf_op jit(solution)/shard_map/ppermute | solution.py:299
  32.4 4.3 %collective-permute-start.4 = (f32[7,8,128]{2,1,0:T(8,128)S(1)}, f32[7,8,128]{2,1,0:T(8,128)S(1)}, u32[]{:S(2)}, u32[]{:S(2)}) collective-permute-start(f32[7,8,128]{2,1,0:T(8,128)S(1)} %broadcast_select_fusion.side_own), channel_id=1, source_target_pairs={{0,1},{1,2},{2,3},{3,4},{4,5},{5,6},{6,7},{7,8},{8,9},{9,10},{10,1... | collective-permute-start | bytes 86024 | tf_op jit(solution)/shard_map/ppermute | solution.py:303
  36.7 1.9 %collective-permute-start.5 = (f32[7,8,128]{2,1,0:T(8,128)S(1)}, f32[7,8,128]{2,1,0:T(8,128)S(1)}, u32[]{:S(2)}, u32[]{:S(2)}) collective-permute-start(f32[7,8,128]{2,1,0:T(8,128)S(1)} %broadcast_select_fusion.side_own), channel_id=1, source_target_pairs={{1,0},{2,1},{3,2},{4,3},{5,4},{6,5},{7,6},{8,7},{9,8},{10,9},{11,1... | collective-permute-start | bytes 86024 | tf_op jit(solution)/shard_map/ppermute | solution.py:304
  38.6 0.0 collective-permute-done.4.side_south
  38.6 5.9 %collective-permute-done.5.side_north = f32[7,8,128]{2,1,0:T(8,128)S(1)} collective-permute-done((f32[7,8,128]{2,1,0:T(8,128)S(1)}, f32[7,8,128]{2,1,0:T(8,128)S(1)}, u32[]{:S(2)}, u32[]{:S(2)}) %collective-permute-start.5) | collective-permute-done | bytes 28704 | tf_op jit(solution)/shard_map/ppermute | solution.py:304
  44.6 0.0 collective-permute-done.1.from_north
  44.6 0.0 collective-permute-done.from_south
  44.6 0.0 copy-start
  44.6 1.1 %copy-done = f32[7,8,8,384]{3,2,1,0:T(8,128)S(1)} copy-done((f32[7,8,8,384]{3,2,1,0:T(8,128)S(1)}, f32[7,8,8,384]{3,2,1,0:T(8,128)}, u32[]{:S(2)}) %copy-start) | copy-done | bytes 688152
  45.7 21.0 %solve.1 = f32[2,192,128]{2,1,0:T(8,128)} custom-call(f32[7,8,8,384]{3,2,1,0:T(8,128)S(1)} %copy-done, f32[40,8,384]{2,1,0:T(8,128)S(1)} %collective-permute-done.from_south, f32[38,8,384]{2,1,0:T(8,128)S(1)} %collective-permute-done.1.from_north, f32[7,8,128]{2,1,0:T(8,128)S(1)} %broadcast_select_fusion.side_own, ...), custom_call_target="tpu_custom_call" | custom-call | tf_op jit(solution)/shard_map/solve/pallas_call | solution.py:307
  (2 shorter events, 0.0 us)
Async XLA Ops:
  2.5 42.1 %collective-permute-start = (f32[40,8,384]{2,1,0:T(8,128)}, f32[40,8,384]{2,1,0:T(8,128)S(1)}, u32[]{:S(2)}, u32[]{:S(2)}) collective-permute-start(f32[40,8,384]{2,1,0:T(8,128)} %get-tuple-element.10), channel_id=1, source_target_pairs={{0,1},{1,2},{2,3},{3,4},{4,5},{5,6},{6,7},{7,8},{8,9},{9,10},{10,1... | collective-permute-start | bytes 1474568 | tf_op jit(solution)/shard_map/ppermute | solution.py:297
  7.5 37.1 %collective-permute-start.1 = (f32[38,8,384]{2,1,0:T(8,128)}, f32[38,8,384]{2,1,0:T(8,128)S(1)}, u32[]{:S(2)}, u32[]{:S(2)}) collective-permute-start(f32[38,8,384]{2,1,0:T(8,128)} %get-tuple-element.11), channel_id=1, source_target_pairs={{1,0},{2,1},{3,2},{4,3},{5,4},{6,5},{7,6},{8,7},{9,8},{10,9},{11,1... | collective-permute-start | bytes 1400840 | tf_op jit(solution)/shard_map/ppermute | solution.py:298
  9.4 17.7 %collective-permute-start.2 = (f32[7,8,128]{2,1,0:T(8,128)}, f32[7,8,128]{2,1,0:T(8,128)S(1)}, u32[]{:S(2)}, u32[]{:S(2)}) collective-permute-start(f32[7,8,128]{2,1,0:T(8,128)} %get-tuple-element.12), channel_id=1, source_target_pairs={{16,0},{32,16},{48,32},{64,48},{80,64},{96,80},{112,96},{128,112},... | collective-permute-start | bytes 86024 | tf_op jit(solution)/shard_map/ppermute | solution.py:300
  13.6 18.8 %collective-permute-start.3 = (f32[7,8,128]{2,1,0:T(8,128)}, f32[7,8,128]{2,1,0:T(8,128)S(1)}, u32[]{:S(2)}, u32[]{:S(2)}) collective-permute-start(f32[7,8,128]{2,1,0:T(8,128)} %get-tuple-element.12), channel_id=1, source_target_pairs={{0,16},{16,32},{32,48},{48,64},{64,80},{80,96},{96,112},{112,128},... | collective-permute-start | bytes 86024 | tf_op jit(solution)/shard_map/ppermute | solution.py:299
  32.4 6.2 %collective-permute-start.4 = (f32[7,8,128]{2,1,0:T(8,128)S(1)}, f32[7,8,128]{2,1,0:T(8,128)S(1)}, u32[]{:S(2)}, u32[]{:S(2)}) collective-permute-start(f32[7,8,128]{2,1,0:T(8,128)S(1)} %broadcast_select_fusion.side_own), channel_id=1, source_target_pairs={{0,1},{1,2},{2,3},{3,4},{4,5},{5,6},{6,7},{7,8},{8,9},{9,10},{10,1... | collective-permute-start | bytes 86024 | tf_op jit(solution)/shard_map/ppermute | solution.py:303
  36.7 7.9 %collective-permute-start.5 = (f32[7,8,128]{2,1,0:T(8,128)S(1)}, f32[7,8,128]{2,1,0:T(8,128)S(1)}, u32[]{:S(2)}, u32[]{:S(2)}) collective-permute-start(f32[7,8,128]{2,1,0:T(8,128)S(1)} %broadcast_select_fusion.side_own), channel_id=1, source_target_pairs={{1,0},{2,1},{3,2},{4,3},{5,4},{6,5},{7,6},{8,7},{9,8},{10,9},{11,1... | collective-permute-start | bytes 86024 | tf_op jit(solution)/shard_map/ppermute | solution.py:304
  44.6 1.1 %copy-start = (f32[7,8,8,384]{3,2,1,0:T(8,128)S(1)}, f32[7,8,8,384]{3,2,1,0:T(8,128)}, u32[]{:S(2)}) copy-start(f32[7,8,8,384]{3,2,1,0:T(8,128)} %get-tuple-element.9.own) | copy-start | bytes 2064388

commit v2 on v0

v2 whole, which is shorter than its diff:
```python
import jax
import jax.numpy as jnp
from jax import lax
from jax.experimental import pallas as pl
from jax.experimental.pallas import tpu as pltpu
from jax.sharding import PartitionSpec as P

STEPS = 6
LANES = 128
ROWS = 8

ROBIN_WEIGHT = 0.5
FACTOR_A = 1.0 - ROBIN_WEIGHT / 2.0
FACTOR_B = 1.0 + ROBIN_WEIGHT / 2.0

U, V, K, KZ, M = 2, 3, 4, 5, 6
FIELDS = 7

TO_SOUTH = (
    [(0, t, r) for t in (0, 1) for r in (0, 1)]
    + [(1, t, r) for t in (0, 1) for r in (1, 2)]
    + [(2, t, r) for t in (0, 1) for r in (2, 3)]
    + [(0, f, r) for f in (U, V, K, KZ) for r in (0, 1, 2)]
    + [(0, M, r) for r in (0, 1, 2, 3)]
)
TO_NORTH = (
    [(0, t, r) for t in (0, 1) for r in (6, 7)]
    + [(1, t, r) for t in (0, 1) for r in (5, 6)]
    + [(2, t, r) for t in (0, 1) for r in (4, 5)]
    + [(0, f, r) for f in (U, KZ) for r in (5, 6, 7)]
    + [(0, f, r) for f in (V, K, M) for r in (4, 5, 6, 7)]
)
BORDER = 4

COLS = 6
RIM = 6
OWN_LANE = COLS * RIM

STRIPS_TO_SOUTH = ((36, 32, 0, 84), (36, 36, 32, 84), (36, 25, 68, 84), (36, 30, 93, 84))
STRIPS_TO_NORTH = ((48, 36, 0, 0), (52, 32, 36, 4), (54, 30, 68, 6), (59, 25, 98, 11))


def lanes():
    return lax.broadcasted_iota(jnp.int32, (8, LANES), 1)


def turn(value, shift):
    shift = shift % LANES
    return pltpu.roll(value, shift, 1) if shift else value


def upward(value):
    return pltpu.roll(value, 7, 0)


def downward(value):
    return pltpu.roll(value, 1, 0)


def west(value, beside):
    return turn(jnp.where(lanes() == LANES - 1, beside, value), 1)


def east(value, beside):
    return turn(jnp.where(lanes() == 0, beside, value), -1)


def face(speed, diff, both):
    return (jnp.maximum(speed, 0.0) + diff) * both, (jnp.minimum(speed, 0.0) - diff) * both


def vertical(diff, sea):
    level = lax.broadcasted_iota(jnp.int32, (8, LANES), 0)
    below = diff * sea * jnp.where(level == 7, 0.0, upward(sea))
    return below, downward(below)


def collected(sea, faces_east, faces_west, faces_north, faces_south, faces_vertical):
    here, there = faces_east
    here_west, there_west = faces_west
    north_here, north_there = faces_north
    south_here, south_there = faces_south
    below, above = faces_vertical
    centre = sea - ((here - there_west) + (north_here - south_there) + (below + above))
    return centre, -there, here_west, -north_there, south_here, below, above


def stencil(weights, value, to_east, to_west, to_north, to_south):
    centre, w_east, w_west, w_north, w_south, w_below, w_above = weights
    return (
        (centre * value + (w_north * to_north + w_south * to_south))
        + (w_below * upward(value) + w_above * downward(value))
        + (w_east * to_east + w_west * to_west)
    )


def north_faces(get, r, tiles):
    return [
        face(get(V, r, k), get(K, r, k), get(M, r, k) * get(M, r + 1, k)) for k in range(tiles)
    ]


def row_weights(get, r, tiles, faces_north, faces_south, interface=None):
    sea = [get(M, r, k) for k in range(tiles)]
    faces = []
    for k in range(tiles):
        both = sea[k] * (east(sea[k], sea[k + 1]) if k + 1 < tiles else turn(sea[k], -1))
        faces.append(face(get(U, r, k), get(K, r, k), both))
    ends = faces[-1]
    if interface is not None:
        at_end = lanes() == LANES - 1
        faces[-1] = tuple(jnp.where(at_end, i, e) for i, e in zip(interface, ends))
        ends = tuple(jnp.where(at_end, turn(i, -1), e) for i, e in zip(interface, ends))
    weights = []
    for k in range(tiles):
        before = faces[k - 1] if k else ends
        faces_west = tuple(west(v, b) for v, b in zip(faces[k], before))
        faces_vertical = vertical(get(KZ, r, k), sea[k])
        weights.append(
            collected(sea[k], faces[k], faces_west, faces_north[k], faces_south[k], faces_vertical)
        )
    return weights


def pack_kernel(
    tracers, speed_east, speed_north, diff_horiz, diff_vert, sea,
    own, firsts, lasts, loaded, loaded_sea, sems,
):
    tiles = own.shape[-1] // LANES
    lane = lanes()
    sources = (tracers.at[0], tracers.at[1], speed_east, speed_north, diff_horiz, diff_vert, sea)
    copies = [
        pltpu.make_async_copy(source, loaded_sea if f == M else loaded.at[f], sems.at[f])
        for f, source in enumerate(sources)
    ]
    for copy in copies:
        copy.start()

    for f in range(FIELDS):
        copies[f].wait()
        source = loaded_sea if f == M else loaded.at[f]
        first_cols = jnp.zeros((8, LANES), jnp.float32)
        last_cols = first_cols
        for r in range(ROWS):
            begin = OWN_LANE + COLS * r
            here = (lane >= begin) & (lane < begin + COLS)
            for k in range(tiles):
                value = source[pl.ds(8 * k + r, 8, stride=8 * tiles), :].astype(jnp.float32)
                own[f, r, :, pl.ds(k * LANES, LANES)] = value
                if k == 0:
                    first_cols = jnp.where(here, turn(value, begin), first_cols)
                if k == tiles - 1:
                    last_cols = jnp.where(here, turn(value, begin + COLS), last_cols)
        firsts[f] = first_cols
        lasts[f] = last_cols


def border_kernel(own, firsts, lasts, from_east, from_west, north, south, coef, state):
    tiles = own.shape[-1] // LANES
    lane = lanes()

    def put(item, k, value):
        if item in TO_NORTH:
            north[TO_NORTH.index(item) * tiles + k] = value
        if item in TO_SOUTH:
            south[TO_SOUTH.index(item) * tiles + k] = value

    def get(f, r, k):
        return own[f, r, :, pl.ds(k * LANES, LANES)]

    for f in range(FIELDS):
        for r in range(ROWS):
            for k in range(tiles):
                put((0, f, r), k, get(f, r, k))

    faces = [north_faces(get, r, tiles) for r in range(0, ROWS - 1)]
    for r in range(1, ROWS - 1):
        weights = row_weights(get, r, tiles, faces[r], faces[r - 1])
        for k in range(tiles):
            cols = pl.ds(k * LANES, LANES)
            for i in range(7):
                coef[i, r, :, cols] = weights[k][i]

    for n in range(2):
        def read(t, r, k, n=n):
            return get(t, r, k) if n == 0 else state[t, r, :, pl.ds(k * LANES, LANES)]

        for r in range(1 + n, ROWS - 1 - n):
            for k in range(tiles):
                cols = pl.ds(k * LANES, LANES)
                weights = [coef[i, r, :, cols] for i in range(7)]
                for t in range(2):
                    value = read(t, r, k)
                    stepped = stencil(
                        weights,
                        value,
                        east(value, read(t, r, k + 1)) if k + 1 < tiles else turn(value, -1),
                        west(value, read(t, r, k - 1)) if k else turn(value, 1),
                        read(t, r + 1, k),
                        read(t, r - 1, k),
                    )
                    if n == 0:
                        state[t, r, :, cols] = stepped
                    put((n + 1, t, r), k, stepped)

    for out, items, pieces in ((north, TO_NORTH, STRIPS_TO_NORTH), (south, TO_SOUTH, STRIPS_TO_SOUTH)):
        for f in range(FIELDS):
            message = jnp.zeros((8, LANES), jnp.float32)
            for strip, (begin, length, there, _) in zip((firsts, lasts, from_east, from_west), pieces):
                moved = turn(strip[f], there - begin)
                message = jnp.where((lane >= there) & (lane < there + length), moved, message)
            out[len(items) * tiles + f] = message


def solve_kernel(
    own, from_south, from_north, firsts, lasts, east_firsts, west_lasts, out, field, coef, state,
):
    tiles = own.shape[-1] // LANES
    lane = lanes()
    column = lax.rem(lane, COLS)
    at_first = column == 0
    at_last = column == COLS - 1

    def assembled(which, source):
        fields = []
        for f in range(FIELDS):
            value = source[f]
            for message, items, pieces in (
                (from_south, TO_NORTH, STRIPS_TO_NORTH),
                (from_north, TO_SOUTH, STRIPS_TO_SOUTH),
            ):
                _, length, there, begin = pieces[which]
                moved = turn(message[len(items) * tiles + f], begin - there)
                value = jnp.where((lane >= begin) & (lane < begin + length), moved, value)
            fields.append(value)
        return fields

    own_first = assembled(0, firsts)
    own_last = assembled(1, lasts)
    east_first = assembled(2, east_firsts)
    west_last = assembled(3, west_lasts)

    def to_first(value):
        return turn(value, 1 - COLS)

    def to_last(value):
        return turn(value, COLS - 1)

    def strip_weights(left, right):
        both = left[M] * jnp.where(at_last, to_last(right[M]), turn(left[M], -1))
        left_faces = face(left[U], left[K], both)
        right_faces = face(right[U], right[K], right[M] * turn(right[M], -1))
        left_west = tuple(turn(v, 1) for v in left_faces)
        right_west = tuple(
            jnp.where(at_first, to_first(l), turn(v, 1)) for l, v in zip(left_faces, right_faces)
        )
        weights = []
        for strip, faces, faces_west in ((left, left_faces, left_west), (right, right_faces, right_west)):
            north = face(strip[V], strip[K], strip[M] * turn(strip[M], -COLS))
            south = tuple(turn(v, COLS) for v in north)
            weights.append(
                collected(strip[M], faces, faces_west, north, south, vertical(strip[KZ], strip[M]))
            )
        return weights[0], weights[1], left_faces

    w_west_last, w_own_first, west_face = strip_weights(west_last, own_first)
    w_own_last, w_east_first, east_face = strip_weights(own_last, east_first)

    def step_first(weights, value, ghost):
        return stencil(
            weights, value, turn(value, -1), jnp.where(at_first, ghost, turn(value, 1)),
            turn(value, -COLS), turn(value, COLS),
        )

    def step_last(weights, value, ghost):
        return stencil(
            weights, value, jnp.where(at_last, ghost, turn(value, -1)), turn(value, 1),
            turn(value, -COLS), turn(value, COLS),
        )

    def trace(value, ghost):
        return FACTOR_B * value - FACTOR_A * ghost

    def robin(told, value):
        return (told + FACTOR_A * value) * (1.0 / FACTOR_B)

    ghosts = []
    first_steps = []
    last_steps = []
    for t in range(2):
        ghost_first = to_first(west_last[t])
        ghost_last = to_last(east_first[t])
        a_first, a_last = own_first[t], own_last[t]
        b_first, b_last = east_first[t], west_last[t]
        c_first, c_last = own_first[t], own_last[t]
        ghosts_t = []
        steps_first, steps_last = [], []
        for n in range(STEPS):
            told_last = to_last(trace(a_first, ghost_first))
            told_first = to_first(trace(a_last, ghost_last))
            robin_last = robin(told_last, b_last)
            robin_first = robin(told_first, b_first)
            trace_last = trace(b_last, robin_last)
            trace_first = trace(b_first, robin_first)
            ghosts_t.append(
                jnp.where(at_last, trace_last, turn(trace_first, COLS - 2)) * (1.0 / FACTOR_B)
            )
            if n < STEPS - 1:
                a_first = step_first(w_own_first, a_first, ghost_first)
                a_last = step_last(w_own_last, a_last, ghost_last)
                b_first = step_first(w_east_first, b_first, robin_first)
                b_last = step_last(w_west_last, b_last, robin_last)
            if n < 2:
                c_first = step_first(w_own_first, c_first, robin(to_first(trace_last), c_first))
                c_last = step_last(w_own_last, c_last, robin(to_last(trace_first), c_last))
                steps_first.append(c_first)
                steps_last.append(c_last)
        ghosts.append(ghosts_t)
        first_steps.append(steps_first)
        last_steps.append(steps_last)

    def ends_of(value, r):
        return turn(value, -(COLS * (r + RIM) + COLS - 1))

    faces_at_ends = [
        jnp.where(at_last, w, turn(e, -1)) for w, e in zip(west_face, east_face)
    ]

    def cols(k):
        return pl.ds(k * LANES, LANES)

    for source, items, offset in ((from_south, TO_NORTH, -ROWS), (from_north, TO_SOUTH, ROWS)):
        for i, (n, f, r) in enumerate(items):
            r = r + offset
            for k in range(tiles):
                value = source[i * tiles + k]
                if n and k == 0:
                    fixed = turn(first_steps[f][n - 1], -COLS * (r + RIM))
                    value = jnp.where(lane < n, fixed, value)
                if n and k == tiles - 1:
                    fixed = turn(last_steps[f][n - 1], -COLS * (r + RIM + 1))
                    value = jnp.where(lane >= LANES - n, fixed, value)
                if f < 2:
                    state[n % 2, f, r + BORDER, :, cols(k)] = value
                else:
                    field[f, r + BORDER, :, cols(k)] = value

    def get(f, r, k):
        if 0 <= r < ROWS:
            return own[f, r, :, cols(k)]
        return field[f, r + BORDER, :, cols(k)]

    def read(n, t, r, k):
        if n == 0 and 0 <= r < ROWS:
            return own[t, r, :, cols(k)]
        return state[n % 2, t, r + BORDER, :, cols(k)]

    reach = BORDER - 1
    faces_south = north_faces(get, -reach - 1, tiles)
    for r in range(-reach, ROWS + reach):
        faces_north = north_faces(get, r, tiles)
        interface = tuple(ends_of(v, r) for v in faces_at_ends)
        weights = row_weights(get, r, tiles, faces_north, faces_south, interface)
        faces_south = faces_north
        for k in range(tiles):
            for i in range(7):
                coef[i, r + BORDER, :, cols(k)] = weights[k][i]

    for n in range(STEPS):
        more = min(n + 1, STEPS - 1 - n)
        for r in range(-more, ROWS + more):
            ends = [ends_of(ghosts[t][n], r) for t in range(2)]
            for k in range(tiles):
                weights = [coef[i, r + BORDER, :, cols(k)] for i in range(7)]
                for t in range(2):
                    value = read(n, t, r, k)
                    if k == 0 or k == tiles - 1:
                        ghost = ends[t] + (FACTOR_A / FACTOR_B) * value
                    if k == 0:
                        to_west = jnp.where(lane == 0, ghost, turn(value, 1))
                    else:
                        to_west = west(value, read(n, t, r, k - 1))
                    if k == tiles - 1:
                        to_east = jnp.where(lane == LANES - 1, ghost, turn(value, -1))
                    else:
                        to_east = east(value, read(n, t, r, k + 1))
                    stepped = stencil(
                        weights, value, to_east, to_west, read(n, t, r + 1, k), read(n, t, r - 1, k)
                    )
                    if n == STEPS - 1:
                        out[t, pl.ds(8 * k + r, 8, stride=8 * tiles), :] = stepped
                    else:
                        state[(n + 1) % 2, t, r + BORDER, :, cols(k)] = stepped


def granted(mib=16):
    return pltpu.CompilerParams(vmem_limit_bytes=mib * 1024 * 1024)


def in_vmem(count):
    return [pl.BlockSpec(memory_space=pltpu.VMEM)] * count


def in_tiles(array):
    lead = array.shape[:-2]
    tiled = array.reshape(lead + (8, -1, LANES))
    return jnp.swapaxes(tiled, -3, -2).reshape(lead[:-1] + (-1, LANES))


def from_tiles(array, shape):
    tiled = array.reshape(shape[:-2] + (-1, 8, LANES))
    return jnp.swapaxes(tiled, -3, -2).reshape(shape)


def pack(*arrays):
    f32 = jnp.float32
    width = arrays[1].size // 64
    return pl.pallas_call(
        pack_kernel,
        out_shape=(
            jax.ShapeDtypeStruct((FIELDS, ROWS, 8, width), f32),
            jax.ShapeDtypeStruct((FIELDS, 8, LANES), f32),
            jax.ShapeDtypeStruct((FIELDS, 8, LANES), f32),
        ),
        in_specs=[pl.BlockSpec(memory_space=pltpu.HBM)] * 6,
        out_specs=tuple(in_vmem(3)),
        scratch_shapes=[
            pltpu.VMEM((M,) + arrays[1].shape, f32),
            pltpu.VMEM(arrays[5].shape, arrays[5].dtype),
            pltpu.SemaphoreType.DMA((FIELDS,)),
        ],
        compiler_params=granted(),
        name="pack",
    )(*arrays)


def border(own, *strips):
    f32 = jnp.float32
    width = own.shape[-1]
    tiles = width // LANES
    return pl.pallas_call(
        border_kernel,
        out_shape=(
            jax.ShapeDtypeStruct((len(TO_NORTH) * tiles + FIELDS, 8, LANES), f32),
            jax.ShapeDtypeStruct((len(TO_SOUTH) * tiles + FIELDS, 8, LANES), f32),
        ),
        in_specs=in_vmem(5),
        out_specs=tuple(in_vmem(2)),
        scratch_shapes=[
            pltpu.VMEM((7, ROWS, 8, width), f32),
            pltpu.VMEM((2, ROWS, 8, width), f32),
        ],
        compiler_params=granted(),
        name="border",
    )(own, *strips)


def solve(own, *others):
    f32 = jnp.float32
    width = own.shape[-1]
    rows = ROWS + 2 * BORDER
    return pl.pallas_call(
        solve_kernel,
        out_shape=jax.ShapeDtypeStruct((2, width // LANES * 64, LANES), f32),
        in_specs=in_vmem(7),
        out_specs=in_vmem(1)[0],
        scratch_shapes=[
            pltpu.VMEM((FIELDS, rows, 8, width), f32),
            pltpu.VMEM((7, rows, 8, width), f32),
            pltpu.VMEM((2, 2, rows, 8, width), f32),
        ],
        compiler_params=granted(),
        name="solve",
    )(own, *others)


def shards(tracers, speed_east, speed_north, diff_horiz, diff_vert, sea_mask):
    arrays = (tracers, speed_east, speed_north, diff_horiz, diff_vert, sea_mask)
    own, firsts, lasts = pack(
        *[pltpu.with_memory_space_constraint(in_tiles(a), pltpu.HBM) for a in arrays]
    )

    count_m = lax.axis_size("merid")
    up = [(i, i + 1) for i in range(count_m - 1)]
    down = [(b, a) for a, b in up]
    count_z = lax.axis_size("zonal")
    onward = [(i, (i + 1) % count_z) for i in range(count_z)]
    back = [(b, a) for a, b in onward]

    from_west = lax.ppermute(lasts, "zonal", onward)
    from_east = lax.ppermute(firsts, "zonal", back)
    north, south = border(own, firsts, lasts, from_east, from_west)
    from_south = lax.ppermute(north, "merid", up)
    from_north = lax.ppermute(south, "merid", down)
    result = solve(own, from_south, from_north, firsts, lasts, from_east, from_west)
    return from_tiles(result, tracers.shape)


def solution(mesh):
    row = P(None, "merid", "zonal")
    whole = P(None, None, "merid", "zonal")
    return jax.shard_map(
        shards, mesh=mesh, in_specs=(whole, row, row, row, row, row), out_specs=whole, check_vma=False
    )
```

time: 201 us -> 35.6 us (0.18)
  the two profiles are of different devices: /device:TPU:2 before, /device:TPU:128 now
where the time goes in v2:
time: 35.6 us; the launch traced here: 35.2 us
  waiting for transfers between devices  16.3 us (46%)
  starting transfers between devices  12.9 us (36%)
  Pallas kernels  5.89 us (17%)
    ppermute x1, waiting for transfers between devices, shards(): from_north = lax.ppermute(south, 'merid', down)  9.43 us
    ppermute x1, starting transfers between devices, shards(): from_north = lax.ppermute(south, 'merid', down)  5.45 us
    ppermute x1, waiting for transfers between devices, shards(): from_west = lax.ppermute(lasts, 'zonal', onward)  5.35 us
    ppermute x1, starting transfers between devices, shards(): from_east = lax.ppermute(firsts, 'zonal', back)  4.99 us
    pallas_call x1, Pallas kernels, solve(): pl.pallas_call(solve_kernel, out_shape=jax.ShapeDtypeStruct((2, width //...  3.91 us
    ppermute x1, starting transfers between devices, shards(): from_south = lax.ppermute(north, 'merid', up)  2.5 us
    pallas_call x1, Pallas kernels, pack(): pl.pallas_call(pack_kernel, out_shape=(jax.ShapeDtypeStruct((FIELDS, ROWS...  1.61 us
    ppermute x1, waiting for transfers between devices, shards(): from_east = lax.ppermute(firsts, 'zonal', back)  1.56 us
  transfers between devices with their start and end apart: 4, of which 3 were waited for; matrix products, arithmetic and copies ran while one was open for 0% of the time, Pallas kernels for 0%

profile of v2, /device:TPU:128, one launch (start us, length us, event | category | flops | bytes accessed | tf_op | source)
XLA Modules:
  0.0 35.2 jit_solution(11071203623726896952)
XLA Ops:
  0.0 1.6 %pack.1 = (f32[7,8,8,384]{3,2,1,0:T(8,128)S(1)}, f32[7,8,128]{2,1,0:T(8,128)S(1)}, f32[7,8,128]{2,1,0:T(8,128)S(1)}) custom-call(f32[2,192,128]{2,1,0:T(8,128)} %bitcast.35, f32[192,128]{1,0:T(8,128)} %bitcast.36, f32[192,128]{1,0:T(8,128)} %bitcast.37, f32[192,128]{1,0:T(8,128)} %bitcast.38, f32[192,128]{1,0:T(8,128)} %bitcast.39, s32[192,128]{1,0:T(8,128)} %bitcast.40), custom_call_target="tpu_custom_call" | custom-call | tf_op jit(solution)/shard_map/pack/pallas_call | solution.py:418
  1.6 5.0 %collective-permute-start = (f32[7,8,128]{2,1,0:T(8,128)S(1)}, f32[7,8,128]{2,1,0:T(8,128)S(1)}, u32[]{:S(2)}, u32[]{:S(2)}) collective-permute-start(f32[7,8,128]{2,1,0:T(8,128)S(1)} %get-tuple-element.11.firsts), channel_id=1, source_target_pairs={{16,0},{32,16},{48,32},{64,48},{80,64},{96,80},{112,96},{128,112},... | collective-permute-start | bytes 86024 | tf_op jit(solution)/shard_map/ppermute | solution.py:491
  6.6 0.0 collective-permute-start.1
  6.6 1.6 %collective-permute-done.from_east.east_firsts = f32[7,8,128]{2,1,0:T(8,128)S(1)} collective-permute-done((f32[7,8,128]{2,1,0:T(8,128)S(1)}, f32[7,8,128]{2,1,0:T(8,128)S(1)}, u32[]{:S(2)}, u32[]{:S(2)}) %collective-permute-start) | collective-permute-done | bytes 28704 | tf_op jit(solution)/shard_map/ppermute | solution.py:491
  8.2 5.3 %collective-permute-done.1.from_west.west_lasts = f32[7,8,128]{2,1,0:T(8,128)S(1)} collective-permute-done((f32[7,8,128]{2,1,0:T(8,128)S(1)}, f32[7,8,128]{2,1,0:T(8,128)S(1)}, u32[]{:S(2)}, u32[]{:S(2)}) %collective-permute-start.1) | collective-permute-done | bytes 28704 | tf_op jit(solution)/shard_map/ppermute | solution.py:490
  13.5 0.4 %border.1 = (f32[97,8,128]{2,1,0:T(8,128)S(1)}, f32[91,8,128]{2,1,0:T(8,128)S(1)}) custom-call(f32[7,8,8,384]{3,2,1,0:T(8,128)S(1)} %get-tuple-element.10.own, f32[7,8,128]{2,1,0:T(8,128)S(1)} %get-tuple-element.11.firsts, f32[7,8,128]{2,1,0:T(8,128)S(1)} %get-tuple-element.12.lasts, f32[7,8,128]{2,1,0:T(8,128)S(1)} %collective-permute-done.from_east.east_firsts, ...), custom_call_target="tpu_custom_call" | custom-call | tf_op jit(solution)/shard_map/border/pallas_call | solution.py:441
  13.9 2.5 %collective-permute-start.2 = (f32[97,8,128]{2,1,0:T(8,128)S(1)}, f32[97,8,128]{2,1,0:T(8,128)S(1)}, u32[]{:S(2)}, u32[]{:S(2)}) collective-permute-start(f32[97,8,128]{2,1,0:T(8,128)S(1)} %get-tuple-element.13), channel_id=1, source_target_pairs={{0,1},{1,2},{2,3},{3,4},{4,5},{5,6},{6,7},{7,8},{8,9},{9,10},{10,1... | collective-permute-start | bytes 1191944 | tf_op jit(solution)/shard_map/ppermute | solution.py:493
  16.4 5.5 %collective-permute-start.3 = (f32[91,8,128]{2,1,0:T(8,128)S(1)}, f32[91,8,128]{2,1,0:T(8,128)S(1)}, u32[]{:S(2)}, u32[]{:S(2)}) collective-permute-start(f32[91,8,128]{2,1,0:T(8,128)S(1)} %get-tuple-element.14), channel_id=1, source_target_pairs={{1,0},{2,1},{3,2},{4,3},{5,4},{6,5},{7,6},{8,7},{9,8},{10,9},{11,1... | collective-permute-start | bytes 1118216 | tf_op jit(solution)/shard_map/ppermute | solution.py:494
  21.9 9.4 %collective-permute-done.3.from_north = f32[91,8,128]{2,1,0:T(8,128)S(1)} collective-permute-done((f32[91,8,128]{2,1,0:T(8,128)S(1)}, f32[91,8,128]{2,1,0:T(8,128)S(1)}, u32[]{:S(2)}, u32[]{:S(2)}) %collective-permute-start.3) | collective-permute-done | bytes 372768 | tf_op jit(solution)/shard_map/ppermute | solution.py:494
  31.3 0.0 collective-permute-done.2.from_south
  31.3 3.9 %solve.1 = f32[2,192,128]{2,1,0:T(8,128)} custom-call(f32[7,8,8,384]{3,2,1,0:T(8,128)S(1)} %get-tuple-element.10.own, f32[97,8,128]{2,1,0:T(8,128)S(1)} %collective-permute-done.2.from_south, f32[91,8,128]{2,1,0:T(8,128)S(1)} %collective-permute-done.3.from_north, f32[7,8,128]{2,1,0:T(8,128)S(1)} %get-tuple-element.11.firsts, ...), custom_call_target="tpu_custom_call" | custom-call | tf_op jit(solution)/shard_map/solve/pallas_call | solution.py:462
Async XLA Ops:
  1.6 6.6 %collective-permute-start = (f32[7,8,128]{2,1,0:T(8,128)S(1)}, f32[7,8,128]{2,1,0:T(8,128)S(1)}, u32[]{:S(2)}, u32[]{:S(2)}) collective-permute-start(f32[7,8,128]{2,1,0:T(8,128)S(1)} %get-tuple-element.11.firsts), channel_id=1, source_target_pairs={{16,0},{32,16},{48,32},{64,48},{80,64},{96,80},{112,96},{128,112},... | collective-permute-start | bytes 86024 | tf_op jit(solution)/shard_map/ppermute | solution.py:491
  6.6 6.9 %collective-permute-start.1 = (f32[7,8,128]{2,1,0:T(8,128)S(1)}, f32[7,8,128]{2,1,0:T(8,128)S(1)}, u32[]{:S(2)}, u32[]{:S(2)}) collective-permute-start(f32[7,8,128]{2,1,0:T(8,128)S(1)} %get-tuple-element.12.lasts), channel_id=1, source_target_pairs={{0,16},{16,32},{32,48},{48,64},{64,80},{80,96},{96,112},{112,128},... | collective-permute-start | bytes 86024 | tf_op jit(solution)/shard_map/ppermute | solution.py:490
  13.9 17.4 %collective-permute-start.2 = (f32[97,8,128]{2,1,0:T(8,128)S(1)}, f32[97,8,128]{2,1,0:T(8,128)S(1)}, u32[]{:S(2)}, u32[]{:S(2)}) collective-permute-start(f32[97,8,128]{2,1,0:T(8,128)S(1)} %get-tuple-element.13), channel_id=1, source_target_pairs={{0,1},{1,2},{2,3},{3,4},{4,5},{5,6},{6,7},{7,8},{8,9},{9,10},{10,1... | collective-permute-start | bytes 1191944 | tf_op jit(solution)/shard_map/ppermute | solution.py:493
  16.4 14.9 %collective-permute-start.3 = (f32[91,8,128]{2,1,0:T(8,128)S(1)}, f32[91,8,128]{2,1,0:T(8,128)S(1)}, u32[]{:S(2)}, u32[]{:S(2)}) collective-permute-start(f32[91,8,128]{2,1,0:T(8,128)S(1)} %get-tuple-element.14), channel_id=1, source_target_pairs={{1,0},{2,1},{3,2},{4,3},{5,4},{6,5},{7,6},{8,7},{9,8},{10,9},{11,1... | collective-permute-start | bytes 1118216 | tf_op jit(solution)/shard_map/ppermute | solution.py:494

commit v3 on v2

--- a/solution.py
+++ b/solution.py
@@ -42,6 +42,10 @@
 
 def lanes():
     return lax.broadcasted_iota(jnp.int32, (8, LANES), 1)
+
+
+def is_even(axis):
+    return lax.rem(lax.axis_index(axis), 2) == 0
 
 
 def turn(value, shift):
@@ -124,9 +128,10 @@
 
 def pack_kernel(
     tracers, speed_east, speed_north, diff_horiz, diff_vert, sea,
-    own, firsts, lasts, loaded, loaded_sea, sems,
+    own, firsts, lasts, swap_even, swap_odd, loaded, loaded_sea, sems,
 ):
     tiles = own.shape[-1] // LANES
+    even = is_even("zonal")
     lane = lanes()
     sources = (tracers.at[0], tracers.at[1], speed_east, speed_north, diff_horiz, diff_vert, sea)
     copies = [
@@ -153,17 +158,17 @@
                     last_cols = jnp.where(here, turn(value, begin + COLS), last_cols)
         firsts[f] = first_cols
         lasts[f] = last_cols
-
-
-def border_kernel(own, firsts, lasts, from_east, from_west, north, south, coef, state):
+        swap_even[f] = jnp.where(even, last_cols, first_cols)
+        swap_odd[f] = jnp.where(even, first_cols, last_cols)
+
+
+def border_kernel(own, swap_even, swap_odd, coef, state, kept):
     tiles = own.shape[-1] // LANES
-    lane = lanes()
 
     def put(item, k, value):
-        if item in TO_NORTH:
-            north[TO_NORTH.index(item) * tiles + k] = value
-        if item in TO_SOUTH:
-            south[TO_SOUTH.index(item) * tiles + k] = value
+        for which, items in enumerate((TO_NORTH, TO_SOUTH)):
+            if item in items:
+                kept[which, items.index(item) * tiles + k] = value
 
     def get(f, r, k):
         return own[f, r, :, pl.ds(k * LANES, LANES)]
@@ -203,17 +208,42 @@
                         state[t, r, :, cols] = stepped
                     put((n + 1, t, r), k, stepped)
 
-    for out, items, pieces in ((north, TO_NORTH, STRIPS_TO_NORTH), (south, TO_SOUTH, STRIPS_TO_SOUTH)):
-        for f in range(FIELDS):
+    even = is_even("merid")
+
+    @pl.when(even)
+    def _():
+        swap_even[...] = kept[0]
+        swap_odd[...] = kept[1]
+
+    @pl.when(jnp.logical_not(even))
+    def _():
+        swap_even[...] = kept[1]
+        swap_odd[...] = kept[0]
+
+
+def strips_kernel(firsts, lasts, zonal_even, zonal_odd, swap_even, swap_odd):
+    lane = lanes()
+    even = is_even("merid")
+    even_zonal = is_even("zonal")
+    for f in range(FIELDS):
+        from_east = jnp.where(even_zonal, zonal_even[f], zonal_odd[f])
+        from_west = jnp.where(even_zonal, zonal_odd[f], zonal_even[f])
+        messages = []
+        for pieces in (STRIPS_TO_NORTH, STRIPS_TO_SOUTH):
             message = jnp.zeros((8, LANES), jnp.float32)
-            for strip, (begin, length, there, _) in zip((firsts, lasts, from_east, from_west), pieces):
-                moved = turn(strip[f], there - begin)
+            for strip, (begin, length, there, _) in zip(
+                (firsts[f], lasts[f], from_east, from_west), pieces
+            ):
+                moved = turn(strip, there - begin)
                 message = jnp.where((lane >= there) & (lane < there + length), moved, message)
-            out[len(items) * tiles + f] = message
+            messages.append(message)
+        swap_even[f] = jnp.where(even, messages[0], messages[1])
+        swap_odd[f] = jnp.where(even, messages[1], messages[0])
 
 
 def solve_kernel(
-    own, from_south, from_north, firsts, lasts, east_firsts, west_lasts, out, field, coef, state,
+    own, rows_even, rows_odd, firsts, lasts, zonal_even, zonal_odd, strips_even, strips_odd,
+    out, received, field, coef, state,
 ):
     tiles = own.shape[-1] // LANES
     lane = lanes()
@@ -221,24 +251,36 @@
     at_first = column == 0
     at_last = column == COLS - 1
 
+    even = is_even("merid")
+    even_zonal = is_even("zonal")
+
+    @pl.when(even)
+    def _():
+        received[0] = rows_odd[...]
+        received[1] = rows_even[...]
+
+    @pl.when(jnp.logical_not(even))
+    def _():
+        received[0] = rows_even[...]
+        received[1] = rows_odd[...]
+
     def assembled(which, source):
         fields = []
         for f in range(FIELDS):
-            value = source[f]
-            for message, items, pieces in (
-                (from_south, TO_NORTH, STRIPS_TO_NORTH),
-                (from_north, TO_SOUTH, STRIPS_TO_SOUTH),
-            ):
+            value = source(f)
+            strips_south = jnp.where(even, strips_odd[f], strips_even[f])
+            strips_north = jnp.where(even, strips_even[f], strips_odd[f])
+            for message, pieces in ((strips_south, STRIPS_TO_NORTH), (strips_north, STRIPS_TO_SOUTH)):
                 _, length, there, begin = pieces[which]
-                moved = turn(message[len(items) * tiles + f], begin - there)
+                moved = turn(message, begin - there)
                 value = jnp.where((lane >= begin) & (lane < begin + length), moved, value)
             fields.append(value)
         return fields
 
-    own_first = assembled(0, firsts)
-    own_last = assembled(1, lasts)
-    east_first = assembled(2, east_firsts)
-    west_last = assembled(3, west_lasts)
+    own_first = assembled(0, lambda f: firsts[f])
+    own_last = assembled(1, lambda f: lasts[f])
+    east_first = assembled(2, lambda f: jnp.where(even_zonal, zonal_even[f], zonal_odd[f]))
+    west_last = assembled(3, lambda f: jnp.where(even_zonal, zonal_odd[f], zonal_even[f]))
 
     def to_first(value):
         return turn(value, 1 - COLS)
@@ -329,11 +371,11 @@
     def cols(k):
         return pl.ds(k * LANES, LANES)
 
-    for source, items, offset in ((from_south, TO_NORTH, -ROWS), (from_north, TO_SOUTH, ROWS)):
+    for side, items, offset in ((0, TO_NORTH, -ROWS), (1, TO_SOUTH, ROWS)):
         for i, (n, f, r) in enumerate(items):
             r = r + offset
             for k in range(tiles):
-                value = source[i * tiles + k]
+                value = received[side, i * tiles + k]
                 if n and k == 0:
                     fixed = turn(first_steps[f][n - 1], -COLS * (r + RIM))
                     value = jnp.where(lane < n, fixed, value)
@@ -397,6 +439,10 @@
     return pltpu.CompilerParams(vmem_limit_bytes=mib * 1024 * 1024)
 
 
+def long_work():
+    return pl.CostEstimate(flops=100_000_000_000, bytes_accessed=1_000_000_000, transcendentals=0)
+
+
 def in_vmem(count):
     return [pl.BlockSpec(memory_space=pltpu.VMEM)] * count
 
@@ -419,11 +465,10 @@
         pack_kernel,
         out_shape=(
             jax.ShapeDtypeStruct((FIELDS, ROWS, 8, width), f32),
-            jax.ShapeDtypeStruct((FIELDS, 8, LANES), f32),
-            jax.ShapeDtypeStruct((FIELDS, 8, LANES), f32),
-        ),
+        )
+        + (jax.ShapeDtypeStruct((FIELDS, 8, LANES), f32),) * 4,
         in_specs=[pl.BlockSpec(memory_space=pltpu.HBM)] * 6,
-        out_specs=tuple(in_vmem(3)),
+        out_specs=tuple(in_vmem(5)),
         scratch_shapes=[
             pltpu.VMEM((M,) + arrays[1].shape, f32),
             pltpu.VMEM(arrays[5].shape, arrays[5].dtype),
@@ -434,25 +479,37 @@
     )(*arrays)
 
 
-def border(own, *strips):
+def border(own):
     f32 = jnp.float32
     width = own.shape[-1]
-    tiles = width // LANES
+    message = (len(TO_NORTH) * width // LANES, 8, LANES)
     return pl.pallas_call(
         border_kernel,
-        out_shape=(
-            jax.ShapeDtypeStruct((len(TO_NORTH) * tiles + FIELDS, 8, LANES), f32),
-            jax.ShapeDtypeStruct((len(TO_SOUTH) * tiles + FIELDS, 8, LANES), f32),
-        ),
-        in_specs=in_vmem(5),
+        out_shape=(jax.ShapeDtypeStruct(message, f32),) * 2,
+        in_specs=in_vmem(1),
         out_specs=tuple(in_vmem(2)),
         scratch_shapes=[
             pltpu.VMEM((7, ROWS, 8, width), f32),
             pltpu.VMEM((2, ROWS, 8, width), f32),
+            pltpu.VMEM((2,) + message, f32),
         ],
         compiler_params=granted(),
+        cost_estimate=long_work(),
         name="border",
-    )(own, *strips)
+    )(own)
+
+
+def exchange_strips(*strips):
+    shape = jax.ShapeDtypeStruct((FIELDS, 8, LANES), jnp.float32)
+    return pl.pallas_call(
+        strips_kernel,
+        out_shape=(shape, shape),
+        in_specs=in_vmem(4),
+        out_specs=tuple(in_vmem(2)),
+        compiler_params=granted(),
+        cost_estimate=long_work(),
+        name="strips",
+    )(*strips)
 
 
 def solve(own, *others):
@@ -462,9 +519,10 @@
     return pl.pallas_call(
         solve_kernel,
         out_shape=jax.ShapeDtypeStruct((2, width // LANES * 64, LANES), f32),
-        in_specs=in_vmem(7),
+        in_specs=in_vmem(9),
         out_specs=in_vmem(1)[0],
         scratch_shapes=[
+            pltpu.VMEM((2,) + others[0].shape, f32),
             pltpu.VMEM((FIELDS, rows, 8, width), f32),
             pltpu.VMEM((7, rows, 8, width), f32),
             pltpu.VMEM((2, 2, rows, 8, width), f32),
@@ -474,25 +532,24 @@
     )(own, *others)
 
 
+def swapped(axis, arrays, periodic):
+    count = lax.axis_size(axis)
+    received = []
+    for start, array in enumerate(arrays):
+        pairs = [(i, (i + 1) % count) for i in range(start, count, 2) if periodic or i + 1 < count]
+        received.append(lax.ppermute(array, axis, pairs + [(b, a) for a, b in pairs]))
+    return received
+
+
 def shards(tracers, speed_east, speed_north, diff_horiz, diff_vert, sea_mask):
     arrays = (tracers, speed_east, speed_north, diff_horiz, diff_vert, sea_mask)
-    own, firsts, lasts = pack(
+    own, firsts, lasts, *zonal = pack(
         *[pltpu.with_memory_space_constraint(in_tiles(a), pltpu.HBM) for a in arrays]
     )
-
-    count_m = lax.axis_size("merid")
-    up = [(i, i + 1) for i in range(count_m - 1)]
-    down = [(b, a) for a, b in up]
-    count_z = lax.axis_size("zonal")
-    onward = [(i, (i + 1) % count_z) for i in range(count_z)]
-    back = [(b, a) for a, b in onward]
-
-    from_west = lax.ppermute(lasts, "zonal", onward)
-    from_east = lax.ppermute(firsts, "zonal", back)
-    north, south = border(own, firsts, lasts, from_east, from_west)
-    from_south = lax.ppermute(north, "merid", up)
-    from_north = lax.ppermute(south, "merid", down)
-    result = solve(own, from_south, from_north, firsts, lasts, from_east, from_west)
+    zonal = swapped("zonal", zonal, True)
+    rows = swapped("merid", border(own), False)
+    strips = swapped("merid", exchange_strips(firsts, lasts, *zonal), False)
+    result = solve(own, *rows, firsts, lasts, *zonal, *strips)
     return from_tiles(result, tracers.shape)
 
 

time: 35.6 us -> 29.5 us (0.83)
  waiting for transfers between devices: 16.3 us -> 8.78 us
  starting transfers between devices: 12.9 us -> 14.4 us
    ppermute x4 -> x6, waiting for transfers between devices: 16.3 us -> 8.78 us  [swapped(): lax.ppermute(array, axis, pairs + [(b, a) for a, b in pairs])]
    ppermute x4 -> x6, starting transfers between devices: 12.9 us -> 14.4 us  [swapped(): lax.ppermute(array, axis, pairs + [(b, a) for a, b in pairs])]
  transfers between devices with their start and end apart: 4 -> 6, of which waited for: 3 -> 1; matrix products, arithmetic and copies ran while one was open for 0% -> 0% of each run, Pallas kernels for 0% -> 2%
where the time goes in v3:
time: 29.5 us; the launch traced here: 29.4 us
  starting transfers between devices  14.4 us (49%)
  waiting for transfers between devices  8.78 us (30%)
  Pallas kernels  6.13 us (21%)
    ppermute x6, starting transfers between devices, swapped(): lax.ppermute(array, axis, pairs + [(b, a) for a, b in pairs])  14.4 us
    ppermute x6, waiting for transfers between devices, swapped(): lax.ppermute(array, axis, pairs + [(b, a) for a, b in pairs])  8.78 us
    pallas_call x1, Pallas kernels, solve(): pl.pallas_call(solve_kernel, out_shape=jax.ShapeDtypeStruct((2, width //...  4.01 us
    pallas_call x1, Pallas kernels, pack(): pl.pallas_call(pack_kernel, out_shape=(jax.ShapeDtypeStruct((FIELDS, ROWS...  1.61 us
  transfers between devices with their start and end apart: 6, of which 1 were waited for; matrix products, arithmetic and copies ran while one was open for 0% of the time, Pallas kernels for 2%

profile of v3, /device:TPU:128, one launch (start us, length us, event | category | flops | bytes accessed | tf_op | source)
XLA Modules:
  0.0 29.4 jit_solution(2027231015223464412)
XLA Ops:
  0.0 1.6 %pack.1 = (f32[7,8,8,384]{3,2,1,0:T(8,128)S(1)}, f32[7,8,128]{2,1,0:T(8,128)S(1)}, f32[7,8,128]{2,1,0:T(8,128)S(1)}, f32[7,8,128]{2,1,0:T(8,128)S(1)}, f32[7,8,128]{2,1,0:T(8,128)S(1)}) custom-call(f32[2,192,128]{2,1,0:T(8,128)} %bitcast.35, f32[192,128]{1,0:T(8,128)} %bitcast.36, f32[192,128]{1,0:T(8,128)} %bitcast.37, f32[192,128]{1,0:T(8,128)} %bitcast.38, ...), custom_call_target="tpu_custom_call" | custom-call | tf_op jit(solution)/shard_map/pack/pallas_call | solution.py:464
  1.6 0.1 collective-permute-start.2
  1.7 5.6 %collective-permute-start.3 = (f32[7,8,128]{2,1,0:T(8,128)S(1)}, f32[7,8,128]{2,1,0:T(8,128)S(1)}, u32[]{:S(2)}, u32[]{:S(2)}) collective-permute-start(f32[7,8,128]{2,1,0:T(8,128)S(1)} %get-tuple-element.20), channel_id=1, source_target_pairs={{16,32},{48,64},{80,96},{112,128},{144,160},{176,192},{208,224},{2... | collective-permute-start | bytes 86024 | tf_op jit(solution)/shard_map/ppermute | solution.py:540
  7.3 0.4 %border.1 = (f32[90,8,128]{2,1,0:T(8,128)S(1)}, f32[90,8,128]{2,1,0:T(8,128)S(1)}) custom-call(f32[7,8,8,384]{3,2,1,0:T(8,128)S(1)} %get-tuple-element.14.own), custom_call_target="tpu_custom_call" | custom-call | flops 99999997952 | bytes 1000000000 | tf_op jit(solution)/shard_map/border/pallas_call | solution.py:486
  7.7 0.7 %collective-permute-start = (f32[90,8,128]{2,1,0:T(8,128)S(1)}, f32[90,8,128]{2,1,0:T(8,128)S(1)}, u32[]{:S(2)}, u32[]{:S(2)}) collective-permute-start(f32[90,8,128]{2,1,0:T(8,128)S(1)} %get-tuple-element.15), channel_id=1, source_target_pairs={{0,1},{2,3},{4,5},{6,7},{8,9},{10,11},{12,13},{14,15},{1,0},{3,2},... | collective-permute-start | bytes 1105928 | tf_op jit(solution)/shard_map/ppermute | solution.py:540
  8.4 2.9 %collective-permute-start.1 = (f32[90,8,128]{2,1,0:T(8,128)S(1)}, f32[90,8,128]{2,1,0:T(8,128)S(1)}, u32[]{:S(2)}, u32[]{:S(2)}) collective-permute-start(f32[90,8,128]{2,1,0:T(8,128)S(1)} %get-tuple-element.16), channel_id=1, source_target_pairs={{1,2},{3,4},{5,6},{7,8},{9,10},{11,12},{13,14},{2,1},{4,3},{6,5},{... | collective-permute-start | bytes 1105928 | tf_op jit(solution)/shard_map/ppermute | solution.py:540
  11.2 0.0 collective-permute-done.2.zonal_even
  11.3 0.0 collective-permute-done.3.zonal_odd
  11.3 0.1 strips.1
  11.4 1.6 %collective-permute-start.4 = (f32[7,8,128]{2,1,0:T(8,128)S(1)}, f32[7,8,128]{2,1,0:T(8,128)S(1)}, u32[]{:S(2)}, u32[]{:S(2)}) collective-permute-start(f32[7,8,128]{2,1,0:T(8,128)S(1)} %get-tuple-element.21), channel_id=1, source_target_pairs={{0,1},{2,3},{4,5},{6,7},{8,9},{10,11},{12,13},{14,15},{1,0},{3,2},... | collective-permute-start | bytes 86024 | tf_op jit(solution)/shard_map/ppermute | solution.py:540
  13.0 3.6 %collective-permute-start.5 = (f32[7,8,128]{2,1,0:T(8,128)S(1)}, f32[7,8,128]{2,1,0:T(8,128)S(1)}, u32[]{:S(2)}, u32[]{:S(2)}) collective-permute-start(f32[7,8,128]{2,1,0:T(8,128)S(1)} %get-tuple-element.22), channel_id=1, source_target_pairs={{1,2},{3,4},{5,6},{7,8},{9,10},{11,12},{13,14},{2,1},{4,3},{6,5},{... | collective-permute-start | bytes 86024 | tf_op jit(solution)/shard_map/ppermute | solution.py:540
  16.6 8.8 %collective-permute-done.4.strips_even = f32[7,8,128]{2,1,0:T(8,128)S(1)} collective-permute-done((f32[7,8,128]{2,1,0:T(8,128)S(1)}, f32[7,8,128]{2,1,0:T(8,128)S(1)}, u32[]{:S(2)}, u32[]{:S(2)}) %collective-permute-start.4) | collective-permute-done | bytes 28704 | tf_op jit(solution)/shard_map/ppermute | solution.py:540
  25.4 0.0 collective-permute-done.5.strips_odd
  25.4 0.0 collective-permute-done.rows_even
  25.4 0.0 collective-permute-done.1.rows_odd
  25.4 4.0 %solve.1 = f32[2,192,128]{2,1,0:T(8,128)} custom-call(f32[7,8,8,384]{3,2,1,0:T(8,128)S(1)} %get-tuple-element.14.own, f32[90,8,128]{2,1,0:T(8,128)S(1)} %collective-permute-done.rows_even, f32[90,8,128]{2,1,0:T(8,128)S(1)} %collective-permute-done.1.rows_odd, f32[7,8,128]{2,1,0:T(8,128)S(1)} %get-tuple-element.17.firsts, ...), custom_call_target="tpu_custom_call" | custom-call | tf_op jit(solution)/shard_map/solve/pallas_call | solution.py:519
Async XLA Ops:
  1.6 9.6 %collective-permute-start.2 = (f32[7,8,128]{2,1,0:T(8,128)S(1)}, f32[7,8,128]{2,1,0:T(8,128)S(1)}, u32[]{:S(2)}, u32[]{:S(2)}) collective-permute-start(f32[7,8,128]{2,1,0:T(8,128)S(1)} %get-tuple-element.19), channel_id=1, source_target_pairs={{0,16},{32,48},{64,80},{96,112},{128,144},{160,176},{192,208},{224... | collective-permute-start | bytes 86024 | tf_op jit(solution)/shard_map/ppermute | solution.py:540
  1.7 9.5 %collective-permute-start.3 = (f32[7,8,128]{2,1,0:T(8,128)S(1)}, f32[7,8,128]{2,1,0:T(8,128)S(1)}, u32[]{:S(2)}, u32[]{:S(2)}) collective-permute-start(f32[7,8,128]{2,1,0:T(8,128)S(1)} %get-tuple-element.20), channel_id=1, source_target_pairs={{16,32},{48,64},{80,96},{112,128},{144,160},{176,192},{208,224},{2... | collective-permute-start | bytes 86024 | tf_op jit(solution)/shard_map/ppermute | solution.py:540
  7.7 17.7 %collective-permute-start = (f32[90,8,128]{2,1,0:T(8,128)S(1)}, f32[90,8,128]{2,1,0:T(8,128)S(1)}, u32[]{:S(2)}, u32[]{:S(2)}) collective-permute-start(f32[90,8,128]{2,1,0:T(8,128)S(1)} %get-tuple-element.15), channel_id=1, source_target_pairs={{0,1},{2,3},{4,5},{6,7},{8,9},{10,11},{12,13},{14,15},{1,0},{3,2},... | collective-permute-start | bytes 1105928 | tf_op jit(solution)/shard_map/ppermute | solution.py:540
  8.4 17.0 %collective-permute-start.1 = (f32[90,8,128]{2,1,0:T(8,128)S(1)}, f32[90,8,128]{2,1,0:T(8,128)S(1)}, u32[]{:S(2)}, u32[]{:S(2)}) collective-permute-start(f32[90,8,128]{2,1,0:T(8,128)S(1)} %get-tuple-element.16), channel_id=1, source_target_pairs={{1,2},{3,4},{5,6},{7,8},{9,10},{11,12},{13,14},{2,1},{4,3},{6,5},{... | collective-permute-start | bytes 1105928 | tf_op jit(solution)/shard_map/ppermute | solution.py:540
  11.4 13.9 %collective-permute-start.4 = (f32[7,8,128]{2,1,0:T(8,128)S(1)}, f32[7,8,128]{2,1,0:T(8,128)S(1)}, u32[]{:S(2)}, u32[]{:S(2)}) collective-permute-start(f32[7,8,128]{2,1,0:T(8,128)S(1)} %get-tuple-element.21), channel_id=1, source_target_pairs={{0,1},{2,3},{4,5},{6,7},{8,9},{10,11},{12,13},{14,15},{1,0},{3,2},... | collective-permute-start | bytes 86024 | tf_op jit(solution)/shard_map/ppermute | solution.py:540
  13.0 12.4 %collective-permute-start.5 = (f32[7,8,128]{2,1,0:T(8,128)S(1)}, f32[7,8,128]{2,1,0:T(8,128)S(1)}, u32[]{:S(2)}, u32[]{:S(2)}) collective-permute-start(f32[7,8,128]{2,1,0:T(8,128)S(1)} %get-tuple-element.22), channel_id=1, source_target_pairs={{1,2},{3,4},{5,6},{7,8},{9,10},{11,12},{13,14},{2,1},{4,3},{6,5},{... | collective-permute-start | bytes 86024 | tf_op jit(solution)/shard_map/ppermute | solution.py:540

commit v4 on v3

--- a/solution.py
+++ b/solution.py
@@ -16,28 +16,28 @@
 U, V, K, KZ, M = 2, 3, 4, 5, 6
 FIELDS = 7
 
+PART, FACE = 3, 4
 TO_SOUTH = (
-    [(0, t, r) for t in (0, 1) for r in (0, 1)]
-    + [(1, t, r) for t in (0, 1) for r in (1, 2)]
-    + [(2, t, r) for t in (0, 1) for r in (2, 3)]
-    + [(0, f, r) for f in (U, V, K, KZ) for r in (0, 1, 2)]
-    + [(0, M, r) for r in (0, 1, 2, 3)]
+    [(n, t, n) for t in (0, 1) for n in (0, 1, 2)]
+    + [(PART, t, n) for t in (0, 1) for n in (0, 1, 2)]
+    + [(0, f, r) for f in (U, V, K, KZ) for r in (0, 1)]
+    + [(0, M, r) for r in (0, 1, 2)]
 )
 TO_NORTH = (
-    [(0, t, r) for t in (0, 1) for r in (6, 7)]
-    + [(1, t, r) for t in (0, 1) for r in (5, 6)]
-    + [(2, t, r) for t in (0, 1) for r in (4, 5)]
-    + [(0, f, r) for f in (U, KZ) for r in (5, 6, 7)]
-    + [(0, f, r) for f in (V, K, M) for r in (4, 5, 6, 7)]
+    [(n, t, 7 - n) for t in (0, 1) for n in (0, 1, 2)]
+    + [(PART, t, 7 - n) for t in (0, 1) for n in (0, 1, 2)]
+    + [(0, f, r) for f in (U, V, K, KZ, M) for r in (6, 7)]
+    + [(FACE, i, 5) for i in (0, 1)]
 )
-BORDER = 4
+UNITS = max(len(TO_SOUTH), len(TO_NORTH))
+BORDER = 3
 
 COLS = 6
 RIM = 6
 OWN_LANE = COLS * RIM
 
-STRIPS_TO_SOUTH = ((36, 32, 0, 84), (36, 36, 32, 84), (36, 25, 68, 84), (36, 30, 93, 84))
-STRIPS_TO_NORTH = ((48, 36, 0, 0), (52, 32, 36, 4), (54, 30, 68, 6), (59, 25, 98, 11))
+STRIPS_TO_SOUTH = ((36, 33, 0, 84), (36, 36, 33, 84), (36, 25, 69, 84), (36, 30, 94, 84))
+STRIPS_TO_NORTH = ((48, 36, 0, 0), (51, 33, 36, 3), (54, 30, 69, 6), (59, 25, 99, 11))
 
 
 def lanes():
@@ -178,35 +178,51 @@
             for k in range(tiles):
                 put((0, f, r), k, get(f, r, k))
 
-    faces = [north_faces(get, r, tiles) for r in range(0, ROWS - 1)]
-    for r in range(1, ROWS - 1):
-        weights = row_weights(get, r, tiles, faces[r], faces[r - 1])
+    closed = [(jnp.zeros((8, LANES), jnp.float32),) * 2] * tiles
+    faces_south = closed
+    for r in range(ROWS):
+        faces_north = north_faces(get, r, tiles) if r + 1 < ROWS else closed
+        weights = row_weights(get, r, tiles, faces_north, faces_south)
+        faces_south = faces_north
         for k in range(tiles):
-            cols = pl.ds(k * LANES, LANES)
             for i in range(7):
-                coef[i, r, :, cols] = weights[k][i]
-
-    for n in range(2):
+                coef[i, r, :, pl.ds(k * LANES, LANES)] = weights[k][i]
+            for i in range(2):
+                put((FACE, i, r), k, faces_north[k][i])
+
+    for n in range(3):
         def read(t, r, k, n=n):
-            return get(t, r, k) if n == 0 else state[t, r, :, pl.ds(k * LANES, LANES)]
-
-        for r in range(1 + n, ROWS - 1 - n):
+            return get(t, r, k) if n == 0 else state[n - 1, t, r, :, pl.ds(k * LANES, LANES)]
+
+        for r in range(n, ROWS - n):
+            if n == 2 and r not in (n, ROWS - 1 - n):
+                continue
             for k in range(tiles):
                 cols = pl.ds(k * LANES, LANES)
                 weights = [coef[i, r, :, cols] for i in range(7)]
                 for t in range(2):
                     value = read(t, r, k)
+                    to_north = read(t, r + 1, k) if r + 1 < ROWS - n else 0.0
+                    to_south = read(t, r - 1, k) if r > n else 0.0
                     stepped = stencil(
                         weights,
                         value,
                         east(value, read(t, r, k + 1)) if k + 1 < tiles else turn(value, -1),
                         west(value, read(t, r, k - 1)) if k else turn(value, 1),
-                        read(t, r + 1, k),
-                        read(t, r - 1, k),
+                        to_north,
+                        to_south,
                     )
-                    if n == 0:
-                        state[t, r, :, cols] = stepped
-                    put((n + 1, t, r), k, stepped)
+                    if r == n:
+                        if n:
+                            stepped = stepped + coef[3, r - 1, :, cols] * value
+                        put((PART, t, r), k, stepped)
+                    elif r == ROWS - 1 - n:
+                        if n:
+                            stepped = stepped + coef[4, r + 1, :, cols] * value
+                        put((PART, t, r), k, stepped)
+                    else:
+                        state[n, t, r, :, cols] = stepped
+                        put((n + 1, t, r), k, stepped)
 
     even = is_even("merid")
 
@@ -243,7 +259,7 @@
 
 def solve_kernel(
     own, rows_even, rows_odd, firsts, lasts, zonal_even, zonal_odd, strips_even, strips_odd,
-    out, received, field, coef, state,
+    out, field, coef, state, part,
 ):
     tiles = own.shape[-1] // LANES
     lane = lanes()
@@ -254,15 +270,32 @@
     even = is_even("merid")
     even_zonal = is_even("zonal")
 
+    def cols(k):
+        return pl.ds(k * LANES, LANES)
+
+    def unpack(source, items, offset):
+        for i, (n, f, r) in enumerate(items):
+            e = r + offset + BORDER
+            for k in range(tiles):
+                value = source[i * tiles + k]
+                if n == FACE:
+                    coef[3 + f, e, :, cols(k)] = value
+                elif n == PART:
+                    part[f, e, :, cols(k)] = value
+                elif f < 2:
+                    state[n % 2, f, e, :, cols(k)] = value
+                else:
+                    field[f, e, :, cols(k)] = value
+
     @pl.when(even)
     def _():
-        received[0] = rows_odd[...]
-        received[1] = rows_even[...]
+        unpack(rows_odd, TO_NORTH, -ROWS)
+        unpack(rows_even, TO_SOUTH, ROWS)
 
     @pl.when(jnp.logical_not(even))
     def _():
-        received[0] = rows_even[...]
-        received[1] = rows_odd[...]
+        unpack(rows_even, TO_NORTH, -ROWS)
+        unpack(rows_odd, TO_SOUTH, ROWS)
 
     def assembled(which, source):
         fields = []
@@ -352,7 +385,7 @@
                 a_last = step_last(w_own_last, a_last, ghost_last)
                 b_first = step_first(w_east_first, b_first, robin_first)
                 b_last = step_last(w_west_last, b_last, robin_last)
-            if n < 2:
+            if n < 3:
                 c_first = step_first(w_own_first, c_first, robin(to_first(trace_last), c_first))
                 c_last = step_last(w_own_last, c_last, robin(to_last(trace_first), c_last))
                 steps_first.append(c_first)
@@ -368,24 +401,21 @@
         jnp.where(at_last, w, turn(e, -1)) for w, e in zip(west_face, east_face)
     ]
 
-    def cols(k):
-        return pl.ds(k * LANES, LANES)
-
-    for side, items, offset in ((0, TO_NORTH, -ROWS), (1, TO_SOUTH, ROWS)):
-        for i, (n, f, r) in enumerate(items):
-            r = r + offset
-            for k in range(tiles):
-                value = received[side, i * tiles + k]
-                if n and k == 0:
-                    fixed = turn(first_steps[f][n - 1], -COLS * (r + RIM))
-                    value = jnp.where(lane < n, fixed, value)
-                if n and k == tiles - 1:
-                    fixed = turn(last_steps[f][n - 1], -COLS * (r + RIM + 1))
-                    value = jnp.where(lane >= LANES - n, fixed, value)
-                if f < 2:
-                    state[n % 2, f, r + BORDER, :, cols(k)] = value
-                else:
-                    field[f, r + BORDER, :, cols(k)] = value
+    def fixed(value, n, t, r, k):
+        if n and k == 0:
+            exact = turn(first_steps[t][n - 1], -COLS * (r + RIM))
+            value = jnp.where(lane < n, exact, value)
+        if n and k == tiles - 1:
+            exact = turn(last_steps[t][n - 1], -COLS * (r + RIM + 1))
+            value = jnp.where(lane >= LANES - n, exact, value)
+        return value
+
+    for n in (1, 2):
+        for t in range(2):
+            for r in (-1 - n, ROWS + n):
+                for k in (0, tiles - 1):
+                    value = state[n % 2, t, r + BORDER, :, cols(k)]
+                    state[n % 2, t, r + BORDER, :, cols(k)] = fixed(value, n, t, r, k)
 
     def get(f, r, k):
         if 0 <= r < ROWS:
@@ -397,8 +427,12 @@
             return own[t, r, :, cols(k)]
         return state[n % 2, t, r + BORDER, :, cols(k)]
 
+    faces_south = []
+    for k in range(tiles):
+        here, there = (coef[i, 0, :, cols(k)] for i in (3, 4))
+        faces_south.append((here, there))
+        coef[3, 0, :, cols(k)] = -there
     reach = BORDER - 1
-    faces_south = north_faces(get, -reach - 1, tiles)
     for r in range(-reach, ROWS + reach):
         faces_north = north_faces(get, r, tiles)
         interface = tuple(ends_of(v, r) for v in faces_at_ends)
@@ -407,9 +441,30 @@
         for k in range(tiles):
             for i in range(7):
                 coef[i, r + BORDER, :, cols(k)] = weights[k][i]
+    for k in range(tiles):
+        coef[4, ROWS + reach + BORDER, :, cols(k)] = faces_south[k][0]
 
     for n in range(STEPS):
-        more = min(n + 1, STEPS - 1 - n)
+        if n < BORDER:
+            for t in range(2):
+                for k in range(tiles):
+                    r = -1 - n
+                    e = r + BORDER
+                    stepped = (
+                        part[t, e, :, cols(k)]
+                        + coef[3, e, :, cols(k)] * read(n, t, r + 1, k)
+                        - coef[4, e + 1, :, cols(k)] * read(n, t, r, k)
+                    )
+                    state[(n + 1) % 2, t, e, :, cols(k)] = fixed(stepped, n + 1, t, r, k)
+                    r = ROWS + n
+                    e = r + BORDER
+                    stepped = (
+                        part[t, e, :, cols(k)]
+                        + coef[4, e, :, cols(k)] * read(n, t, r - 1, k)
+                        - coef[3, e - 1, :, cols(k)] * read(n, t, r, k)
+                    )
+                    state[(n + 1) % 2, t, e, :, cols(k)] = fixed(stepped, n + 1, t, r, k)
+        more = min(n, STEPS - 1 - n)
         for r in range(-more, ROWS + more):
             ends = [ends_of(ghosts[t][n], r) for t in range(2)]
             for k in range(tiles):
@@ -482,7 +537,7 @@
 def border(own):
     f32 = jnp.float32
     width = own.shape[-1]
-    message = (len(TO_NORTH) * width // LANES, 8, LANES)
+    message = (UNITS * width // LANES, 8, LANES)
     return pl.pallas_call(
         border_kernel,
         out_shape=(jax.ShapeDtypeStruct(message, f32),) * 2,
@@ -490,7 +545,7 @@
         out_specs=tuple(in_vmem(2)),
         scratch_shapes=[
             pltpu.VMEM((7, ROWS, 8, width), f32),
-            pltpu.VMEM((2, ROWS, 8, width), f32),
+            pltpu.VMEM((2, 2, ROWS, 8, width), f32),
             pltpu.VMEM((2,) + message, f32),
         ],
         compiler_params=granted(),
@@ -522,10 +577,10 @@
         in_specs=in_vmem(9),
         out_specs=in_vmem(1)[0],
         scratch_shapes=[
-            pltpu.VMEM((2,) + others[0].shape, f32),
             pltpu.VMEM((FIELDS, rows, 8, width), f32),
             pltpu.VMEM((7, rows, 8, width), f32),
             pltpu.VMEM((2, 2, rows, 8, width), f32),
+            pltpu.VMEM((2, rows, 8, width), f32),
         ],
         compiler_params=granted(),
         name="solve",

time: 29.5 us -> 26.1 us (0.88)
  waiting for transfers between devices: 8.78 us -> 5.62 us
    ppermute x6, waiting for transfers between devices: 8.78 us -> 5.62 us  [swapped(): lax.ppermute(array, axis, pairs + [(b, a) for a, b in pairs])]
    pallas_call x1, Pallas kernels: 4.01 us -> 3.63 us  [solve(): pl.pallas_call(solve_kernel, out_shape=jax.ShapeDtypeStruct((2, width //...]
where the time goes in v4:
time: 26.1 us; the launch traced here: 26 us
  starting transfers between devices  14.4 us (55%)
  Pallas kernels  5.87 us (22%)
  waiting for transfers between devices  5.62 us (22%)
    ppermute x6, starting transfers between devices, swapped(): lax.ppermute(array, axis, pairs + [(b, a) for a, b in pairs])  14.4 us
    ppermute x6, waiting for transfers between devices, swapped(): lax.ppermute(array, axis, pairs + [(b, a) for a, b in pairs])  5.62 us
    pallas_call x1, Pallas kernels, solve(): pl.pallas_call(solve_kernel, out_shape=jax.ShapeDtypeStruct((2, width //...  3.63 us
    pallas_call x1, Pallas kernels, pack(): pl.pallas_call(pack_kernel, out_shape=(jax.ShapeDtypeStruct((FIELDS, ROWS...  1.61 us
  transfers between devices with their start and end apart: 6, of which 1 were waited for; matrix products, arithmetic and copies ran while one was open for 0% of the time, Pallas kernels for 2%

profile of v4, /device:TPU:128, one launch (start us, length us, event | category | flops | bytes accessed | tf_op | source)
XLA Modules:
  0.0 26.0 jit_solution(586840948650772748)
XLA Ops:
  0.0 1.6 %pack.1 = (f32[7,8,8,384]{3,2,1,0:T(8,128)S(1)}, f32[7,8,128]{2,1,0:T(8,128)S(1)}, f32[7,8,128]{2,1,0:T(8,128)S(1)}, f32[7,8,128]{2,1,0:T(8,128)S(1)}, f32[7,8,128]{2,1,0:T(8,128)S(1)}) custom-call(f32[2,192,128]{2,1,0:T(8,128)} %bitcast.35, f32[192,128]{1,0:T(8,128)} %bitcast.36, f32[192,128]{1,0:T(8,128)} %bitcast.37, f32[192,128]{1,0:T(8,128)} %bitcast.38, ...), custom_call_target="tpu_custom_call" | custom-call | tf_op jit(solution)/shard_map/pack/pallas_call | solution.py:519
  1.6 0.1 collective-permute-start.2
  1.7 5.6 %collective-permute-start.3 = (f32[7,8,128]{2,1,0:T(8,128)S(1)}, f32[7,8,128]{2,1,0:T(8,128)S(1)}, u32[]{:S(2)}, u32[]{:S(2)}) collective-permute-start(f32[7,8,128]{2,1,0:T(8,128)S(1)} %get-tuple-element.20), channel_id=1, source_target_pairs={{16,32},{48,64},{80,96},{112,128},{144,160},{176,192},{208,224},{2... | collective-permute-start | bytes 86024 | tf_op jit(solution)/shard_map/ppermute | solution.py:595
  7.3 0.5 %border.1 = (f32[72,8,128]{2,1,0:T(8,128)S(1)}, f32[72,8,128]{2,1,0:T(8,128)S(1)}) custom-call(f32[7,8,8,384]{3,2,1,0:T(8,128)S(1)} %get-tuple-element.14.own), custom_call_target="tpu_custom_call" | custom-call | flops 99999997952 | bytes 1000000000 | tf_op jit(solution)/shard_map/border/pallas_call | solution.py:541
  7.8 0.7 %collective-permute-start = (f32[72,8,128]{2,1,0:T(8,128)S(1)}, f32[72,8,128]{2,1,0:T(8,128)S(1)}, u32[]{:S(2)}, u32[]{:S(2)}) collective-permute-start(f32[72,8,128]{2,1,0:T(8,128)S(1)} %get-tuple-element.15), channel_id=1, source_target_pairs={{0,1},{2,3},{4,5},{6,7},{8,9},{10,11},{12,13},{14,15},{1,0},{3,2},... | collective-permute-start | bytes 884744 | tf_op jit(solution)/shard_map/ppermute | solution.py:595
  8.5 2.9 %collective-permute-start.1 = (f32[72,8,128]{2,1,0:T(8,128)S(1)}, f32[72,8,128]{2,1,0:T(8,128)S(1)}, u32[]{:S(2)}, u32[]{:S(2)}) collective-permute-start(f32[72,8,128]{2,1,0:T(8,128)S(1)} %get-tuple-element.16), channel_id=1, source_target_pairs={{1,2},{3,4},{5,6},{7,8},{9,10},{11,12},{13,14},{2,1},{4,3},{6,5},{... | collective-permute-start | bytes 884744 | tf_op jit(solution)/shard_map/ppermute | solution.py:595
  11.4 0.0 collective-permute-done.2.zonal_even
  11.4 0.0 collective-permute-done.3.zonal_odd
  11.4 0.1 strips.1
  11.5 1.6 %collective-permute-start.4 = (f32[7,8,128]{2,1,0:T(8,128)S(1)}, f32[7,8,128]{2,1,0:T(8,128)S(1)}, u32[]{:S(2)}, u32[]{:S(2)}) collective-permute-start(f32[7,8,128]{2,1,0:T(8,128)S(1)} %get-tuple-element.21), channel_id=1, source_target_pairs={{0,1},{2,3},{4,5},{6,7},{8,9},{10,11},{12,13},{14,15},{1,0},{3,2},... | collective-permute-start | bytes 86024 | tf_op jit(solution)/shard_map/ppermute | solution.py:595
  13.1 3.6 %collective-permute-start.5 = (f32[7,8,128]{2,1,0:T(8,128)S(1)}, f32[7,8,128]{2,1,0:T(8,128)S(1)}, u32[]{:S(2)}, u32[]{:S(2)}) collective-permute-start(f32[7,8,128]{2,1,0:T(8,128)S(1)} %get-tuple-element.22), channel_id=1, source_target_pairs={{1,2},{3,4},{5,6},{7,8},{9,10},{11,12},{13,14},{2,1},{4,3},{6,5},{... | collective-permute-start | bytes 86024 | tf_op jit(solution)/shard_map/ppermute | solution.py:595
  16.7 5.6 %collective-permute-done.4.strips_even = f32[7,8,128]{2,1,0:T(8,128)S(1)} collective-permute-done((f32[7,8,128]{2,1,0:T(8,128)S(1)}, f32[7,8,128]{2,1,0:T(8,128)S(1)}, u32[]{:S(2)}, u32[]{:S(2)}) %collective-permute-start.4) | collective-permute-done | bytes 28704 | tf_op jit(solution)/shard_map/ppermute | solution.py:595
  22.3 0.0 collective-permute-done.5.strips_odd
  22.3 0.0 collective-permute-done.rows_even
  22.3 0.0 collective-permute-done.1.rows_odd
  22.3 3.6 %solve.1 = f32[2,192,128]{2,1,0:T(8,128)} custom-call(f32[7,8,8,384]{3,2,1,0:T(8,128)S(1)} %get-tuple-element.14.own, f32[72,8,128]{2,1,0:T(8,128)S(1)} %collective-permute-done.rows_even, f32[72,8,128]{2,1,0:T(8,128)S(1)} %collective-permute-done.1.rows_odd, f32[7,8,128]{2,1,0:T(8,128)S(1)} %get-tuple-element.17.firsts, ...), custom_call_target="tpu_custom_call" | custom-call | tf_op jit(solution)/shard_map/solve/pallas_call | solution.py:574
Async XLA Ops:
  1.6 9.8 %collective-permute-start.2 = (f32[7,8,128]{2,1,0:T(8,128)S(1)}, f32[7,8,128]{2,1,0:T(8,128)S(1)}, u32[]{:S(2)}, u32[]{:S(2)}) collective-permute-start(f32[7,8,128]{2,1,0:T(8,128)S(1)} %get-tuple-element.19), channel_id=1, source_target_pairs={{0,16},{32,48},{64,80},{96,112},{128,144},{160,176},{192,208},{224... | collective-permute-start | bytes 86024 | tf_op jit(solution)/shard_map/ppermute | solution.py:595
  1.7 9.7 %collective-permute-start.3 = (f32[7,8,128]{2,1,0:T(8,128)S(1)}, f32[7,8,128]{2,1,0:T(8,128)S(1)}, u32[]{:S(2)}, u32[]{:S(2)}) collective-permute-start(f32[7,8,128]{2,1,0:T(8,128)S(1)} %get-tuple-element.20), channel_id=1, source_target_pairs={{16,32},{48,64},{80,96},{112,128},{144,160},{176,192},{208,224},{2... | collective-permute-start | bytes 86024 | tf_op jit(solution)/shard_map/ppermute | solution.py:595
  7.8 14.5 %collective-permute-start = (f32[72,8,128]{2,1,0:T(8,128)S(1)}, f32[72,8,128]{2,1,0:T(8,128)S(1)}, u32[]{:S(2)}, u32[]{:S(2)}) collective-permute-start(f32[72,8,128]{2,1,0:T(8,128)S(1)} %get-tuple-element.15), channel_id=1, source_target_pairs={{0,1},{2,3},{4,5},{6,7},{8,9},{10,11},{12,13},{14,15},{1,0},{3,2},... | collective-permute-start | bytes 884744 | tf_op jit(solution)/shard_map/ppermute | solution.py:595
  8.5 13.8 %collective-permute-start.1 = (f32[72,8,128]{2,1,0:T(8,128)S(1)}, f32[72,8,128]{2,1,0:T(8,128)S(1)}, u32[]{:S(2)}, u32[]{:S(2)}) collective-permute-start(f32[72,8,128]{2,1,0:T(8,128)S(1)} %get-tuple-element.16), channel_id=1, source_target_pairs={{1,2},{3,4},{5,6},{7,8},{9,10},{11,12},{13,14},{2,1},{4,3},{6,5},{... | collective-permute-start | bytes 884744 | tf_op jit(solution)/shard_map/ppermute | solution.py:595
  11.5 10.8 %collective-permute-start.4 = (f32[7,8,128]{2,1,0:T(8,128)S(1)}, f32[7,8,128]{2,1,0:T(8,128)S(1)}, u32[]{:S(2)}, u32[]{:S(2)}) collective-permute-start(f32[7,8,128]{2,1,0:T(8,128)S(1)} %get-tuple-element.21), channel_id=1, source_target_pairs={{0,1},{2,3},{4,5},{6,7},{8,9},{10,11},{12,13},{14,15},{1,0},{3,2},... | collective-permute-start | bytes 86024 | tf_op jit(solution)/shard_map/ppermute | solution.py:595
  13.1 9.2 %collective-permute-start.5 = (f32[7,8,128]{2,1,0:T(8,128)S(1)}, f32[7,8,128]{2,1,0:T(8,128)S(1)}, u32[]{:S(2)}, u32[]{:S(2)}) collective-permute-start(f32[7,8,128]{2,1,0:T(8,128)S(1)} %get-tuple-element.22), channel_id=1, source_target_pairs={{1,2},{3,4},{5,6},{7,8},{9,10},{11,12},{13,14},{2,1},{4,3},{6,5},{... | collective-permute-start | bytes 86024 | tf_op jit(solution)/shard_map/ppermute | solution.py:595

commit v5 on v4

--- a/solution.py
+++ b/solution.py
@@ -31,6 +31,8 @@
 )
 UNITS = max(len(TO_SOUTH), len(TO_NORTH))
 BORDER = 3
+BORDER_GROUP = 4
+GROUP = 6
 
 COLS = 6
 RIM = 6
@@ -89,13 +91,19 @@
     return centre, -there, here_west, -north_there, south_here, below, above
 
 
-def stencil(weights, value, to_east, to_west, to_north, to_south):
+def weighted(weights, values):
     centre, w_east, w_west, w_north, w_south, w_below, w_above = weights
+    value, to_east, to_west, to_north, to_south, below, above = values
     return (
         (centre * value + (w_north * to_north + w_south * to_south))
-        + (w_below * upward(value) + w_above * downward(value))
+        + (w_below * below + w_above * above)
         + (w_east * to_east + w_west * to_west)
     )
+
+
+def stencil(weights, value, to_east, to_west, to_north, to_south):
+    values = (value, to_east, to_west, to_north, to_south, upward(value), downward(value))
+    return weighted(weights, values)
 
 
 def north_faces(get, r, tiles):
@@ -104,26 +112,44 @@
     ]
 
 
-def row_weights(get, r, tiles, faces_north, faces_south, interface=None):
-    sea = [get(M, r, k) for k in range(tiles)]
-    faces = []
-    for k in range(tiles):
-        both = sea[k] * (east(sea[k], sea[k + 1]) if k + 1 < tiles else turn(sea[k], -1))
-        faces.append(face(get(U, r, k), get(K, r, k), both))
-    ends = faces[-1]
-    if interface is not None:
-        at_end = lanes() == LANES - 1
-        faces[-1] = tuple(jnp.where(at_end, i, e) for i, e in zip(interface, ends))
-        ends = tuple(jnp.where(at_end, turn(i, -1), e) for i, e in zip(interface, ends))
-    weights = []
-    for k in range(tiles):
-        before = faces[k - 1] if k else ends
-        faces_west = tuple(west(v, b) for v, b in zip(faces[k], before))
-        faces_vertical = vertical(get(KZ, r, k), sea[k])
-        weights.append(
-            collected(sea[k], faces[k], faces_west, faces_north[k], faces_south[k], faces_vertical)
-        )
-    return weights
+def weights_of(get, rows, tiles, faces_north, faces_south, interfaces=None):
+    lane = lanes()
+    cells = [(r, k) for r in rows for k in range(tiles)]
+    sea = {(r, k): get(M, r, k) for r, k in cells}
+    beside = {
+        (r, k): east(sea[r, k], sea[r, k + 1]) if k + 1 < tiles else turn(sea[r, k], -1) for r, k in cells
+    }
+    beneath = {c: upward(sea[c]) for c in cells}
+    bottom = lax.broadcasted_iota(jnp.int32, (8, LANES), 0) == 7
+    faces, below = {}, {}
+    for c in cells:
+        faces[c] = face(get(U, *c), get(K, *c), sea[c] * beside[c])
+        below[c] = get(KZ, *c) * sea[c] * jnp.where(bottom, 0.0, beneath[c])
+    before = {}
+    for i, r in enumerate(rows):
+        ends = faces[r, tiles - 1]
+        if interfaces is not None:
+            at_end = lane == LANES - 1
+            faces[r, tiles - 1] = tuple(
+                jnp.where(at_end, turned, end) for turned, end in zip(interfaces[i], ends)
+            )
+            ends = tuple(turn(v, -1) for v in interfaces[i])
+        before[r] = ends
+    above = {c: downward(below[c]) for c in cells}
+    faces_west = {}
+    for r, k in cells:
+        others = faces[r, k - 1] if k else before[r]
+        faces_west[r, k] = tuple(west(v, b) for v, b in zip(faces[r, k], others))
+    return [
+        [
+            collected(
+                sea[r, k], faces[r, k], faces_west[r, k], faces_north[i][k], faces_south[i][k],
+                (below[r, k], above[r, k]),
+            )
+            for k in range(tiles)
+        ]
+        for i, r in enumerate(rows)
+    ]
 
 
 def pack_kernel(
@@ -179,16 +205,18 @@
                 put((0, f, r), k, get(f, r, k))
 
     closed = [(jnp.zeros((8, LANES), jnp.float32),) * 2] * tiles
-    faces_south = closed
+    faces = [closed] + [north_faces(get, r, tiles) for r in range(ROWS - 1)] + [closed]
     for r in range(ROWS):
-        faces_north = north_faces(get, r, tiles) if r + 1 < ROWS else closed
-        weights = row_weights(get, r, tiles, faces_north, faces_south)
-        faces_south = faces_north
         for k in range(tiles):
-            for i in range(7):
-                coef[i, r, :, pl.ds(k * LANES, LANES)] = weights[k][i]
             for i in range(2):
-                put((FACE, i, r), k, faces_north[k][i])
+                put((FACE, i, r), k, faces[r + 1][k][i])
+    for begin in range(0, ROWS, BORDER_GROUP):
+        rows = range(begin, begin + BORDER_GROUP)
+        weights = weights_of(get, rows, tiles, faces[begin + 1 :], faces[begin:])
+        for r in rows:
+            for k in range(tiles):
+                for i in range(7):
+                    coef[i, r, :, pl.ds(k * LANES, LANES)] = weights[r - begin][k][i]
 
     for n in range(3):
         def read(t, r, k, n=n):
@@ -341,58 +369,69 @@
     w_west_last, w_own_first, west_face = strip_weights(west_last, own_first)
     w_own_last, w_east_first, east_face = strip_weights(own_last, east_first)
 
-    def step_first(weights, value, ghost):
-        return stencil(
-            weights, value, turn(value, -1), jnp.where(at_first, ghost, turn(value, 1)),
-            turn(value, -COLS), turn(value, COLS),
-        )
-
-    def step_last(weights, value, ghost):
-        return stencil(
-            weights, value, jnp.where(at_last, ghost, turn(value, -1)), turn(value, 1),
-            turn(value, -COLS), turn(value, COLS),
-        )
-
     def trace(value, ghost):
         return FACTOR_B * value - FACTOR_A * ghost
 
     def robin(told, value):
         return (told + FACTOR_A * value) * (1.0 / FACTOR_B)
 
-    ghosts = []
-    first_steps = []
-    last_steps = []
-    for t in range(2):
-        ghost_first = to_first(west_last[t])
-        ghost_last = to_last(east_first[t])
-        a_first, a_last = own_first[t], own_last[t]
-        b_first, b_last = east_first[t], west_last[t]
-        c_first, c_last = own_first[t], own_last[t]
-        ghosts_t = []
-        steps_first, steps_last = [], []
-        for n in range(STEPS):
-            told_last = to_last(trace(a_first, ghost_first))
-            told_first = to_first(trace(a_last, ghost_last))
-            robin_last = robin(told_last, b_last)
-            robin_first = robin(told_first, b_first)
-            trace_last = trace(b_last, robin_last)
-            trace_first = trace(b_first, robin_first)
-            ghosts_t.append(
+    ghosts = [[], []]
+    first_steps = [[], []]
+    last_steps = [[], []]
+    held = [
+        (own_first[t], own_last[t], east_first[t], west_last[t], own_first[t], own_last[t])
+        for t in range(2)
+    ]
+    constant = [(to_first(west_last[t]), to_last(east_first[t])) for t in range(2)]
+    for n in range(STEPS):
+        told = []
+        for (a_first, a_last, *_), (ghost_first, ghost_last) in zip(held, constant):
+            told.append(
+                (to_first(trace(a_last, ghost_last)), to_last(trace(a_first, ghost_first)))
+            )
+        robins = []
+        traces = []
+        for (_, _, b_first, b_last, *_), (told_first, told_last) in zip(held, told):
+            robins.append((robin(told_first, b_first), robin(told_last, b_last)))
+            traces.append((trace(b_first, robins[-1][0]), trace(b_last, robins[-1][1])))
+        for t in range(2):
+            trace_first, trace_last = traces[t]
+            ghosts[t].append(
                 jnp.where(at_last, trace_last, turn(trace_first, COLS - 2)) * (1.0 / FACTOR_B)
             )
+        steps = []
+        for t in range(2):
+            a_first, a_last, b_first, b_last, c_first, c_last = held[t]
             if n < STEPS - 1:
-                a_first = step_first(w_own_first, a_first, ghost_first)
-                a_last = step_last(w_own_last, a_last, ghost_last)
-                b_first = step_first(w_east_first, b_first, robin_first)
-                b_last = step_last(w_west_last, b_last, robin_last)
-            if n < 3:
-                c_first = step_first(w_own_first, c_first, robin(to_first(trace_last), c_first))
-                c_last = step_last(w_own_last, c_last, robin(to_last(trace_first), c_last))
-                steps_first.append(c_first)
-                steps_last.append(c_last)
-        ghosts.append(ghosts_t)
-        first_steps.append(steps_first)
-        last_steps.append(steps_last)
+                steps += [
+                    (w_own_first, a_first, constant[t][0], True),
+                    (w_own_last, a_last, constant[t][1], False),
+                    (w_east_first, b_first, robins[t][0], True),
+                    (w_west_last, b_last, robins[t][1], False),
+                ]
+            if n < BORDER:
+                steps += [
+                    (w_own_first, c_first, robin(to_first(traces[t][1]), c_first), True),
+                    (w_own_last, c_last, robin(to_last(traces[t][0]), c_last), False),
+                ]
+        turned = [
+            (turn(v, -1), turn(v, 1), turn(v, -COLS), turn(v, COLS), upward(v), downward(v))
+            for _, v, _, _ in steps
+        ]
+        stepped = []
+        for (weights, value, ghost, is_first), (e, w, north, south, up, down) in zip(steps, turned):
+            if is_first:
+                w = jnp.where(at_first, ghost, w)
+            else:
+                e = jnp.where(at_last, ghost, e)
+            stepped.append(weighted(weights, (value, e, w, north, south, up, down)))
+        count = len(stepped) // 2
+        for t in range(2):
+            mine = stepped[t * count : (t + 1) * count]
+            if n < BORDER:
+                first_steps[t].append(mine[-2])
+                last_steps[t].append(mine[-1])
+            held[t] = tuple(mine) + (mine[0],) * (6 - count) if count else held[t]
 
     def ends_of(value, r):
         return turn(value, -(COLS * (r + RIM) + COLS - 1))
@@ -433,14 +472,16 @@
         faces_south.append((here, there))
         coef[3, 0, :, cols(k)] = -there
     reach = BORDER - 1
-    for r in range(-reach, ROWS + reach):
-        faces_north = north_faces(get, r, tiles)
-        interface = tuple(ends_of(v, r) for v in faces_at_ends)
-        weights = row_weights(get, r, tiles, faces_north, faces_south, interface)
-        faces_south = faces_north
-        for k in range(tiles):
-            for i in range(7):
-                coef[i, r + BORDER, :, cols(k)] = weights[k][i]
+    for begin in range(-reach, ROWS + reach, GROUP):
+        rows = range(begin, begin + GROUP)
+        faces = [faces_south] + [north_faces(get, r, tiles) for r in rows]
+        interfaces = [tuple(ends_of(v, r) for v in faces_at_ends) for r in rows]
+        weights = weights_of(get, rows, tiles, faces[1:], faces[:-1], interfaces)
+        faces_south = faces[-1]
+        for r in rows:
+            for k in range(tiles):
+                for i in range(7):
+                    coef[i, r + BORDER, :, cols(k)] = weights[r - begin][k][i]
     for k in range(tiles):
         coef[4, ROWS + reach + BORDER, :, cols(k)] = faces_south[k][0]
 
@@ -494,8 +535,8 @@
     return pltpu.CompilerParams(vmem_limit_bytes=mib * 1024 * 1024)
 
 
-def long_work():
-    return pl.CostEstimate(flops=100_000_000_000, bytes_accessed=1_000_000_000, transcendentals=0)
+def work(flops):
+    return pl.CostEstimate(flops=flops, bytes_accessed=0, transcendentals=0)
 
 
 def in_vmem(count):
@@ -549,7 +590,6 @@
             pltpu.VMEM((2,) + message, f32),
         ],
         compiler_params=granted(),
-        cost_estimate=long_work(),
         name="border",
     )(own)
 
@@ -562,7 +602,7 @@
         in_specs=in_vmem(4),
         out_specs=tuple(in_vmem(2)),
         compiler_params=granted(),
-        cost_estimate=long_work(),
+        cost_estimate=work(100_000_000_000),
         name="strips",
     )(*strips)
 

time: 26.1 us -> 25 us (0.958)
  Pallas kernels: 5.87 us -> 4.78 us
    pallas_call x1, Pallas kernels: 3.63 us -> 2.53 us  [solve(): pl.pallas_call(solve_kernel, out_shape=jax.ShapeDtypeStruct((2, width //...]
  transfers between devices with their start and end apart: 6 -> 6, of which waited for: 1 -> 1; matrix products, arithmetic and copies ran while one was open for 0% -> 0% of each run, Pallas kernels for 2% -> 3%
where the time goes in v5:
time: 25 us; the launch traced here: 24.9 us
  starting transfers between devices  14.4 us (58%)
  waiting for transfers between devices  5.62 us (22%)
  Pallas kernels  4.78 us (19%)
    ppermute x6, starting transfers between devices, swapped(): lax.ppermute(array, axis, pairs + [(b, a) for a, b in pairs])  14.4 us
    ppermute x6, waiting for transfers between devices, swapped(): lax.ppermute(array, axis, pairs + [(b, a) for a, b in pairs])  5.62 us
    pallas_call x1, Pallas kernels, solve(): pl.pallas_call(solve_kernel, out_shape=jax.ShapeDtypeStruct((2, width //...  2.53 us
    pallas_call x1, Pallas kernels, pack(): pl.pallas_call(pack_kernel, out_shape=(jax.ShapeDtypeStruct((FIELDS, ROWS...  1.61 us
  transfers between devices with their start and end apart: 6, of which 1 were waited for; matrix products, arithmetic and copies ran while one was open for 0% of the time, Pallas kernels for 3%

profile of v5, /device:TPU:128, one launch (start us, length us, event | category | flops | bytes accessed | tf_op | source)
XLA Modules:
  0.0 24.9 jit_solution(4135564804068532999)
XLA Ops:
  0.0 1.6 %pack.1 = (f32[7,8,8,384]{3,2,1,0:T(8,128)S(1)}, f32[7,8,128]{2,1,0:T(8,128)S(1)}, f32[7,8,128]{2,1,0:T(8,128)S(1)}, f32[7,8,128]{2,1,0:T(8,128)S(1)}, f32[7,8,128]{2,1,0:T(8,128)S(1)}) custom-call(f32[2,192,128]{2,1,0:T(8,128)} %bitcast.35, f32[192,128]{1,0:T(8,128)} %bitcast.36, f32[192,128]{1,0:T(8,128)} %bitcast.37, f32[192,128]{1,0:T(8,128)} %bitcast.38, ...), custom_call_target="tpu_custom_call" | custom-call | tf_op jit(solution)/shard_map/pack/pallas_call | solution.py:560
  1.6 0.1 collective-permute-start.2
  1.7 5.6 %collective-permute-start.3 = (f32[7,8,128]{2,1,0:T(8,128)S(1)}, f32[7,8,128]{2,1,0:T(8,128)S(1)}, u32[]{:S(2)}, u32[]{:S(2)}) collective-permute-start(f32[7,8,128]{2,1,0:T(8,128)S(1)} %get-tuple-element.20), channel_id=1, source_target_pairs={{16,32},{48,64},{80,96},{112,128},{144,160},{176,192},{208,224},{2... | collective-permute-start | bytes 86024 | tf_op jit(solution)/shard_map/ppermute | solution.py:635
  7.3 0.5 %border.1 = (f32[72,8,128]{2,1,0:T(8,128)S(1)}, f32[72,8,128]{2,1,0:T(8,128)S(1)}) custom-call(f32[7,8,8,384]{3,2,1,0:T(8,128)S(1)} %get-tuple-element.14.own), custom_call_target="tpu_custom_call" | custom-call | tf_op jit(solution)/shard_map/border/pallas_call | solution.py:582
  7.8 0.7 %collective-permute-start = (f32[72,8,128]{2,1,0:T(8,128)S(1)}, f32[72,8,128]{2,1,0:T(8,128)S(1)}, u32[]{:S(2)}, u32[]{:S(2)}) collective-permute-start(f32[72,8,128]{2,1,0:T(8,128)S(1)} %get-tuple-element.15), channel_id=1, source_target_pairs={{0,1},{2,3},{4,5},{6,7},{8,9},{10,11},{12,13},{14,15},{1,0},{3,2},... | collective-permute-start | bytes 884744 | tf_op jit(solution)/shard_map/ppermute | solution.py:635
  8.5 2.9 %collective-permute-start.1 = (f32[72,8,128]{2,1,0:T(8,128)S(1)}, f32[72,8,128]{2,1,0:T(8,128)S(1)}, u32[]{:S(2)}, u32[]{:S(2)}) collective-permute-start(f32[72,8,128]{2,1,0:T(8,128)S(1)} %get-tuple-element.16), channel_id=1, source_target_pairs={{1,2},{3,4},{5,6},{7,8},{9,10},{11,12},{13,14},{2,1},{4,3},{6,5},{... | collective-permute-start | bytes 884744 | tf_op jit(solution)/shard_map/ppermute | solution.py:635
  11.4 0.0 collective-permute-done.2.zonal_even
  11.4 0.0 collective-permute-done.3.zonal_odd
  11.4 0.1 strips.1
  11.5 1.6 %collective-permute-start.4 = (f32[7,8,128]{2,1,0:T(8,128)S(1)}, f32[7,8,128]{2,1,0:T(8,128)S(1)}, u32[]{:S(2)}, u32[]{:S(2)}) collective-permute-start(f32[7,8,128]{2,1,0:T(8,128)S(1)} %get-tuple-element.21), channel_id=1, source_target_pairs={{0,1},{2,3},{4,5},{6,7},{8,9},{10,11},{12,13},{14,15},{1,0},{3,2},... | collective-permute-start | bytes 86024 | tf_op jit(solution)/shard_map/ppermute | solution.py:635
  13.1 3.6 %collective-permute-start.5 = (f32[7,8,128]{2,1,0:T(8,128)S(1)}, f32[7,8,128]{2,1,0:T(8,128)S(1)}, u32[]{:S(2)}, u32[]{:S(2)}) collective-permute-start(f32[7,8,128]{2,1,0:T(8,128)S(1)} %get-tuple-element.22), channel_id=1, source_target_pairs={{1,2},{3,4},{5,6},{7,8},{9,10},{11,12},{13,14},{2,1},{4,3},{6,5},{... | collective-permute-start | bytes 86024 | tf_op jit(solution)/shard_map/ppermute | solution.py:635
  16.7 5.6 %collective-permute-done.4.strips_even = f32[7,8,128]{2,1,0:T(8,128)S(1)} collective-permute-done((f32[7,8,128]{2,1,0:T(8,128)S(1)}, f32[7,8,128]{2,1,0:T(8,128)S(1)}, u32[]{:S(2)}, u32[]{:S(2)}) %collective-permute-start.4) | collective-permute-done | bytes 28704 | tf_op jit(solution)/shard_map/ppermute | solution.py:635
  22.3 0.0 collective-permute-done.5.strips_odd
  22.3 0.0 collective-permute-done.rows_even
  22.3 0.0 collective-permute-done.1.rows_odd
  22.3 2.5 %solve.1 = f32[2,192,128]{2,1,0:T(8,128)} custom-call(f32[7,8,8,384]{3,2,1,0:T(8,128)S(1)} %get-tuple-element.14.own, f32[72,8,128]{2,1,0:T(8,128)S(1)} %collective-permute-done.rows_even, f32[72,8,128]{2,1,0:T(8,128)S(1)} %collective-permute-done.1.rows_odd, f32[7,8,128]{2,1,0:T(8,128)S(1)} %get-tuple-element.17.firsts, ...), custom_call_target="tpu_custom_call" | custom-call | tf_op jit(solution)/shard_map/solve/pallas_call | solution.py:614
Async XLA Ops:
  1.6 9.7 %collective-permute-start.2 = (f32[7,8,128]{2,1,0:T(8,128)S(1)}, f32[7,8,128]{2,1,0:T(8,128)S(1)}, u32[]{:S(2)}, u32[]{:S(2)}) collective-permute-start(f32[7,8,128]{2,1,0:T(8,128)S(1)} %get-tuple-element.19), channel_id=1, source_target_pairs={{0,16},{32,48},{64,80},{96,112},{128,144},{160,176},{192,208},{224... | collective-permute-start | bytes 86024 | tf_op jit(solution)/shard_map/ppermute | solution.py:635
  1.7 9.7 %collective-permute-start.3 = (f32[7,8,128]{2,1,0:T(8,128)S(1)}, f32[7,8,128]{2,1,0:T(8,128)S(1)}, u32[]{:S(2)}, u32[]{:S(2)}) collective-permute-start(f32[7,8,128]{2,1,0:T(8,128)S(1)} %get-tuple-element.20), channel_id=1, source_target_pairs={{16,32},{48,64},{80,96},{112,128},{144,160},{176,192},{208,224},{2... | collective-permute-start | bytes 86024 | tf_op jit(solution)/shard_map/ppermute | solution.py:635
  7.8 14.5 %collective-permute-start = (f32[72,8,128]{2,1,0:T(8,128)S(1)}, f32[72,8,128]{2,1,0:T(8,128)S(1)}, u32[]{:S(2)}, u32[]{:S(2)}) collective-permute-start(f32[72,8,128]{2,1,0:T(8,128)S(1)} %get-tuple-element.15), channel_id=1, source_target_pairs={{0,1},{2,3},{4,5},{6,7},{8,9},{10,11},{12,13},{14,15},{1,0},{3,2},... | collective-permute-start | bytes 884744 | tf_op jit(solution)/shard_map/ppermute | solution.py:635
  8.5 13.8 %collective-permute-start.1 = (f32[72,8,128]{2,1,0:T(8,128)S(1)}, f32[72,8,128]{2,1,0:T(8,128)S(1)}, u32[]{:S(2)}, u32[]{:S(2)}) collective-permute-start(f32[72,8,128]{2,1,0:T(8,128)S(1)} %get-tuple-element.16), channel_id=1, source_target_pairs={{1,2},{3,4},{5,6},{7,8},{9,10},{11,12},{13,14},{2,1},{4,3},{6,5},{... | collective-permute-start | bytes 884744 | tf_op jit(solution)/shard_map/ppermute | solution.py:635
  11.5 10.8 %collective-permute-start.4 = (f32[7,8,128]{2,1,0:T(8,128)S(1)}, f32[7,8,128]{2,1,0:T(8,128)S(1)}, u32[]{:S(2)}, u32[]{:S(2)}) collective-permute-start(f32[7,8,128]{2,1,0:T(8,128)S(1)} %get-tuple-element.21), channel_id=1, source_target_pairs={{0,1},{2,3},{4,5},{6,7},{8,9},{10,11},{12,13},{14,15},{1,0},{3,2},... | collective-permute-start | bytes 86024 | tf_op jit(solution)/shard_map/ppermute | solution.py:635
  13.1 9.2 %collective-permute-start.5 = (f32[7,8,128]{2,1,0:T(8,128)S(1)}, f32[7,8,128]{2,1,0:T(8,128)S(1)}, u32[]{:S(2)}, u32[]{:S(2)}) collective-permute-start(f32[7,8,128]{2,1,0:T(8,128)S(1)} %get-tuple-element.22), channel_id=1, source_target_pairs={{1,2},{3,4},{5,6},{7,8},{9,10},{11,12},{13,14},{2,1},{4,3},{6,5},{... | collective-permute-start | bytes 86024 | tf_op jit(solution)/shard_map/ppermute | solution.py:635

commit v6 on v5

--- a/solution.py
+++ b/solution.py
@@ -32,7 +32,6 @@
 UNITS = max(len(TO_SOUTH), len(TO_NORTH))
 BORDER = 3
 BORDER_GROUP = 4
-GROUP = 6
 
 COLS = 6
 RIM = 6
@@ -110,6 +109,34 @@
     return [
         face(get(V, r, k), get(K, r, k), get(M, r, k) * get(M, r + 1, k)) for k in range(tiles)
     ]
+
+
+def strip_columns():
+    column = lax.rem(lanes(), COLS)
+    return column == 0, column == COLS - 1
+
+
+def to_first(value):
+    return turn(value, 1 - COLS)
+
+
+def to_last(value):
+    return turn(value, COLS - 1)
+
+
+def left_faces(left, right):
+    _, at_last = strip_columns()
+    both = left[M] * jnp.where(at_last, to_last(right[M]), turn(left[M], -1))
+    return face(left[U], left[K], both)
+
+
+def faces_of_ends(west_face, east_face):
+    _, at_last = strip_columns()
+    return [jnp.where(at_last, w, turn(e, -1)) for w, e in zip(west_face, east_face)]
+
+
+def ends_of(value, r):
+    return turn(value, -(COLS * (r + RIM) + COLS - 1))
 
 
 def weights_of(get, rows, tiles, faces_north, faces_south, interfaces=None):
@@ -167,8 +194,9 @@
     for copy in copies:
         copy.start()
 
+    for copy in copies:
+        copy.wait()
     for f in range(FIELDS):
-        copies[f].wait()
         source = loaded_sea if f == M else loaded.at[f]
         first_cols = jnp.zeros((8, LANES), jnp.float32)
         last_cols = first_cols
@@ -285,8 +313,28 @@
         swap_odd[f] = jnp.where(even, messages[1], messages[0])
 
 
+def inner_kernel(own, firsts, lasts, zonal_even, zonal_odd, inner):
+    tiles = own.shape[-1] // LANES
+    even_zonal = is_even("zonal")
+    from_east = [jnp.where(even_zonal, zonal_even[f], zonal_odd[f]) for f in range(FIELDS)]
+    from_west = [jnp.where(even_zonal, zonal_odd[f], zonal_even[f]) for f in range(FIELDS)]
+    faces_at_ends = faces_of_ends(left_faces(from_west, firsts), left_faces(lasts, from_east))
+
+    def get(f, r, k):
+        return own[f, r, :, pl.ds(k * LANES, LANES)]
+
+    rows = range(1, ROWS - 1)
+    north = [north_faces(get, r, tiles) for r in range(ROWS - 1)]
+    interfaces = [tuple(ends_of(v, r) for v in faces_at_ends) for r in rows]
+    weights = weights_of(get, rows, tiles, north[1:], north[:-1], interfaces)
+    for r, row in zip(rows, weights):
+        for k in range(tiles):
+            for i in range(7):
+                inner[i, r - 1, :, pl.ds(k * LANES, LANES)] = row[k][i]
+
+
 def solve_kernel(
-    own, rows_even, rows_odd, firsts, lasts, zonal_even, zonal_odd, strips_even, strips_odd,
+    own, inner, rows_even, rows_odd, firsts, lasts, zonal_even, zonal_odd, strips_even, strips_odd,
     out, field, coef, state, part,
 ):
     tiles = own.shape[-1] // LANES
@@ -343,28 +391,21 @@
     east_first = assembled(2, lambda f: jnp.where(even_zonal, zonal_even[f], zonal_odd[f]))
     west_last = assembled(3, lambda f: jnp.where(even_zonal, zonal_odd[f], zonal_even[f]))
 
-    def to_first(value):
-        return turn(value, 1 - COLS)
-
-    def to_last(value):
-        return turn(value, COLS - 1)
-
     def strip_weights(left, right):
-        both = left[M] * jnp.where(at_last, to_last(right[M]), turn(left[M], -1))
-        left_faces = face(left[U], left[K], both)
+        faces_left = left_faces(left, right)
         right_faces = face(right[U], right[K], right[M] * turn(right[M], -1))
-        left_west = tuple(turn(v, 1) for v in left_faces)
+        left_west = tuple(turn(v, 1) for v in faces_left)
         right_west = tuple(
-            jnp.where(at_first, to_first(l), turn(v, 1)) for l, v in zip(left_faces, right_faces)
+            jnp.where(at_first, to_first(l), turn(v, 1)) for l, v in zip(faces_left, right_faces)
         )
         weights = []
-        for strip, faces, faces_west in ((left, left_faces, left_west), (right, right_faces, right_west)):
+        for strip, faces, faces_west in ((left, faces_left, left_west), (right, right_faces, right_west)):
             north = face(strip[V], strip[K], strip[M] * turn(strip[M], -COLS))
             south = tuple(turn(v, COLS) for v in north)
             weights.append(
                 collected(strip[M], faces, faces_west, north, south, vertical(strip[KZ], strip[M]))
             )
-        return weights[0], weights[1], left_faces
+        return weights[0], weights[1], faces_left
 
     w_west_last, w_own_first, west_face = strip_weights(west_last, own_first)
     w_own_last, w_east_first, east_face = strip_weights(own_last, east_first)
@@ -433,12 +474,7 @@
                 last_steps[t].append(mine[-1])
             held[t] = tuple(mine) + (mine[0],) * (6 - count) if count else held[t]
 
-    def ends_of(value, r):
-        return turn(value, -(COLS * (r + RIM) + COLS - 1))
-
-    faces_at_ends = [
-        jnp.where(at_last, w, turn(e, -1)) for w, e in zip(west_face, east_face)
-    ]
+    faces_at_ends = faces_of_ends(west_face, east_face)
 
     def fixed(value, n, t, r, k):
         if n and k == 0:
@@ -472,18 +508,24 @@
         faces_south.append((here, there))
         coef[3, 0, :, cols(k)] = -there
     reach = BORDER - 1
-    for begin in range(-reach, ROWS + reach, GROUP):
-        rows = range(begin, begin + GROUP)
-        faces = [faces_south] + [north_faces(get, r, tiles) for r in rows]
-        interfaces = [tuple(ends_of(v, r) for v in faces_at_ends) for r in rows]
-        weights = weights_of(get, rows, tiles, faces[1:], faces[:-1], interfaces)
-        faces_south = faces[-1]
-        for r in rows:
-            for k in range(tiles):
-                for i in range(7):
-                    coef[i, r + BORDER, :, cols(k)] = weights[r - begin][k][i]
+    rows = [*range(-reach, 1), *range(ROWS - 1, ROWS + reach)]
+    north = {r: north_faces(get, r, tiles) for r in rows + [ROWS - 2]}
+    weights = weights_of(
+        get, rows, tiles, [north[r] for r in rows],
+        [north[r - 1] if r > -reach else faces_south for r in rows],
+        [tuple(ends_of(v, r) for v in faces_at_ends) for r in rows],
+    )
+    for r, row in zip(rows, weights):
+        for k in range(tiles):
+            for i in range(7):
+                coef[i, r + BORDER, :, cols(k)] = row[k][i]
     for k in range(tiles):
-        coef[4, ROWS + reach + BORDER, :, cols(k)] = faces_south[k][0]
+        coef[4, ROWS + reach + BORDER, :, cols(k)] = north[rows[-1]][k][0]
+
+    def weight(i, r, k):
+        if 0 < r < ROWS - 1:
+            return inner[i, r - 1, :, cols(k)]
+        return coef[i, r + BORDER, :, cols(k)]
 
     for n in range(STEPS):
         if n < BORDER:
@@ -509,7 +551,7 @@
         for r in range(-more, ROWS + more):
             ends = [ends_of(ghosts[t][n], r) for t in range(2)]
             for k in range(tiles):
-                weights = [coef[i, r + BORDER, :, cols(k)] for i in range(7)]
+                weights = [weight(i, r, k) for i in range(7)]
                 for t in range(2):
                     value = read(n, t, r, k)
                     if k == 0 or k == tiles - 1:
@@ -607,6 +649,18 @@
     )(*strips)
 
 
+def weigh_inner(own, *strips):
+    return pl.pallas_call(
+        inner_kernel,
+        out_shape=jax.ShapeDtypeStruct((7, ROWS - 2, 8, own.shape[-1]), jnp.float32),
+        in_specs=in_vmem(5),
+        out_specs=in_vmem(1)[0],
+        compiler_params=granted(),
+        cost_estimate=work(1_000_000_000),
+        name="inner",
+    )(own, *strips)
+
+
 def solve(own, *others):
     f32 = jnp.float32
     width = own.shape[-1]
@@ -614,7 +668,7 @@
     return pl.pallas_call(
         solve_kernel,
         out_shape=jax.ShapeDtypeStruct((2, width // LANES * 64, LANES), f32),
-        in_specs=in_vmem(9),
+        in_specs=in_vmem(10),
         out_specs=in_vmem(1)[0],
         scratch_shapes=[
             pltpu.VMEM((FIELDS, rows, 8, width), f32),
@@ -644,7 +698,8 @@
     zonal = swapped("zonal", zonal, True)
     rows = swapped("merid", border(own), False)
     strips = swapped("merid", exchange_strips(firsts, lasts, *zonal), False)
-    result = solve(own, *rows, firsts, lasts, *zonal, *strips)
+    inner = weigh_inner(own, firsts, lasts, *zonal)
+    result = solve(own, inner, *rows, firsts, lasts, *zonal, *strips)
     return from_tiles(result, tracers.shape)
 
 

time: 25 us -> 24.7 us (0.988)
  waiting for transfers between devices: 5.62 us -> 5.22 us
    ppermute x6, waiting for transfers between devices: 5.62 us -> 5.22 us  [swapped(): lax.ppermute(array, axis, pairs + [(b, a) for a, b in pairs])]
    pallas_call x0 -> x1, Pallas kernels: none -> 0.39 us  [weigh_inner(): pl.pallas_call(inner_kernel, out_shape=jax.ShapeDtypeStruct((7, ROWS - 2,...]
  transfers between devices with their start and end apart: 6 -> 6, of which waited for: 1 -> 1; matrix products, arithmetic and copies ran while one was open for 0% -> 0% of each run, Pallas kernels for 3% -> 4%
where the time goes in v6:
time: 24.7 us; the launch traced here: 24.5 us
  starting transfers between devices  14.4 us (58%)
  waiting for transfers between devices  5.22 us (21%)
  Pallas kernels  4.81 us (19%)
    ppermute x6, starting transfers between devices, swapped(): lax.ppermute(array, axis, pairs + [(b, a) for a, b in pairs])  14.4 us
    ppermute x6, waiting for transfers between devices, swapped(): lax.ppermute(array, axis, pairs + [(b, a) for a, b in pairs])  5.22 us
    pallas_call x1, Pallas kernels, solve(): pl.pallas_call(solve_kernel, out_shape=jax.ShapeDtypeStruct((2, width //...  2.34 us
    pallas_call x1, Pallas kernels, pack(): pl.pallas_call(pack_kernel, out_shape=(jax.ShapeDtypeStruct((FIELDS, ROWS...  1.48 us
  transfers between devices with their start and end apart: 6, of which 1 were waited for; matrix products, arithmetic and copies ran while one was open for 0% of the time, Pallas kernels for 4%

profile of v6, /device:TPU:128, one launch (start us, length us, event | category | flops | bytes accessed | tf_op | source)
XLA Modules:
  0.0 24.5 jit_solution(6420735104757267581)
XLA Ops:
  0.0 1.5 %pack.1 = (f32[7,8,8,384]{3,2,1,0:T(8,128)S(1)}, f32[7,8,128]{2,1,0:T(8,128)S(1)}, f32[7,8,128]{2,1,0:T(8,128)S(1)}, f32[7,8,128]{2,1,0:T(8,128)S(1)}, f32[7,8,128]{2,1,0:T(8,128)S(1)}) custom-call(f32[2,192,128]{2,1,0:T(8,128)} %bitcast.35, f32[192,128]{1,0:T(8,128)} %bitcast.36, f32[192,128]{1,0:T(8,128)} %bitcast.37, f32[192,128]{1,0:T(8,128)} %bitcast.38, ...), custom_call_target="tpu_custom_call" | custom-call | tf_op jit(solution)/shard_map/pack/pallas_call | solution.py:602
  1.5 0.1 collective-permute-start
  1.6 5.6 %collective-permute-start.1 = (f32[7,8,128]{2,1,0:T(8,128)S(1)}, f32[7,8,128]{2,1,0:T(8,128)S(1)}, u32[]{:S(2)}, u32[]{:S(2)}) collective-permute-start(f32[7,8,128]{2,1,0:T(8,128)S(1)} %get-tuple-element.18), channel_id=1, source_target_pairs={{16,32},{48,64},{80,96},{112,128},{144,160},{176,192},{208,224},{2... | collective-permute-start | bytes 86024 | tf_op jit(solution)/shard_map/ppermute | solution.py:689
  7.2 0.5 %border.1 = (f32[72,8,128]{2,1,0:T(8,128)S(1)}, f32[72,8,128]{2,1,0:T(8,128)S(1)}) custom-call(f32[7,8,8,384]{3,2,1,0:T(8,128)S(1)} %get-tuple-element.14.own), custom_call_target="tpu_custom_call" | custom-call | tf_op jit(solution)/shard_map/border/pallas_call | solution.py:624
  7.6 0.7 %collective-permute-start.2 = (f32[72,8,128]{2,1,0:T(8,128)S(1)}, f32[72,8,128]{2,1,0:T(8,128)S(1)}, u32[]{:S(2)}, u32[]{:S(2)}) collective-permute-start(f32[72,8,128]{2,1,0:T(8,128)S(1)} %get-tuple-element.19), channel_id=1, source_target_pairs={{0,1},{2,3},{4,5},{6,7},{8,9},{10,11},{12,13},{14,15},{1,0},{3,2},... | collective-permute-start | bytes 884744 | tf_op jit(solution)/shard_map/ppermute | solution.py:689
  8.3 2.9 %collective-permute-start.3 = (f32[72,8,128]{2,1,0:T(8,128)S(1)}, f32[72,8,128]{2,1,0:T(8,128)S(1)}, u32[]{:S(2)}, u32[]{:S(2)}) collective-permute-start(f32[72,8,128]{2,1,0:T(8,128)S(1)} %get-tuple-element.20), channel_id=1, source_target_pairs={{1,2},{3,4},{5,6},{7,8},{9,10},{11,12},{13,14},{2,1},{4,3},{6,5},{... | collective-permute-start | bytes 884744 | tf_op jit(solution)/shard_map/ppermute | solution.py:689
  11.2 0.0 collective-permute-done.zonal_even
  11.2 0.0 collective-permute-done.1.zonal_odd
  11.2 0.1 strips.1
  11.4 1.6 %collective-permute-start.4 = (f32[7,8,128]{2,1,0:T(8,128)S(1)}, f32[7,8,128]{2,1,0:T(8,128)S(1)}, u32[]{:S(2)}, u32[]{:S(2)}) collective-permute-start(f32[7,8,128]{2,1,0:T(8,128)S(1)} %get-tuple-element.21), channel_id=1, source_target_pairs={{0,1},{2,3},{4,5},{6,7},{8,9},{10,11},{12,13},{14,15},{1,0},{3,2},... | collective-permute-start | bytes 86024 | tf_op jit(solution)/shard_map/ppermute | solution.py:689
  13.0 3.6 %collective-permute-start.5 = (f32[7,8,128]{2,1,0:T(8,128)S(1)}, f32[7,8,128]{2,1,0:T(8,128)S(1)}, u32[]{:S(2)}, u32[]{:S(2)}) collective-permute-start(f32[7,8,128]{2,1,0:T(8,128)S(1)} %get-tuple-element.22), channel_id=1, source_target_pairs={{1,2},{3,4},{5,6},{7,8},{9,10},{11,12},{13,14},{2,1},{4,3},{6,5},{... | collective-permute-start | bytes 86024 | tf_op jit(solution)/shard_map/ppermute | solution.py:689
  16.5 0.4 %inner.1 = f32[7,6,8,384]{3,2,1,0:T(8,128)S(1)} custom-call(f32[7,8,8,384]{3,2,1,0:T(8,128)S(1)} %get-tuple-element.14.own, f32[7,8,128]{2,1,0:T(8,128)S(1)} %get-tuple-element.15.firsts, f32[7,8,128]{2,1,0:T(8,128)S(1)} %get-tuple-element.16.lasts, f32[7,8,128]{2,1,0:T(8,128)S(1)} %collective-permute-done.zonal_even, ...), custom_call_target="tpu_custom_call" | custom-call | flops 1000000000 | tf_op jit(solution)/shard_map/inner/pallas_call | solution.py:653
  16.9 5.2 %collective-permute-done.4.strips_even = f32[7,8,128]{2,1,0:T(8,128)S(1)} collective-permute-done((f32[7,8,128]{2,1,0:T(8,128)S(1)}, f32[7,8,128]{2,1,0:T(8,128)S(1)}, u32[]{:S(2)}, u32[]{:S(2)}) %collective-permute-start.4) | collective-permute-done | bytes 28704 | tf_op jit(solution)/shard_map/ppermute | solution.py:689
  22.1 0.0 collective-permute-done.5.strips_odd
  22.1 0.0 collective-permute-done.2.rows_even
  22.2 0.0 collective-permute-done.3.rows_odd
  22.2 2.3 %solve.1 = f32[2,192,128]{2,1,0:T(8,128)} custom-call(f32[7,8,8,384]{3,2,1,0:T(8,128)S(1)} %get-tuple-element.14.own, f32[7,6,8,384]{3,2,1,0:T(8,128)S(1)} %inner.1, f32[72,8,128]{2,1,0:T(8,128)S(1)} %collective-permute-done.2.rows_even, f32[72,8,128]{2,1,0:T(8,128)S(1)} %collective-permute-done.3.rows_odd, f32[7,8,128]{2,1,0:T(8,128)S(1)} %get-tuple-element.15.firsts, ...), custom_call_target="tpu_custom_call" | custom-call | tf_op jit(solution)/shard_map/solve/pallas_call | solution.py:668
Async XLA Ops:
  1.5 9.7 %collective-permute-start = (f32[7,8,128]{2,1,0:T(8,128)S(1)}, f32[7,8,128]{2,1,0:T(8,128)S(1)}, u32[]{:S(2)}, u32[]{:S(2)}) collective-permute-start(f32[7,8,128]{2,1,0:T(8,128)S(1)} %get-tuple-element.17), channel_id=1, source_target_pairs={{0,16},{32,48},{64,80},{96,112},{128,144},{160,176},{192,208},{224... | collective-permute-start | bytes 86024 | tf_op jit(solution)/shard_map/ppermute | solution.py:689
  1.6 9.6 %collective-permute-start.1 = (f32[7,8,128]{2,1,0:T(8,128)S(1)}, f32[7,8,128]{2,1,0:T(8,128)S(1)}, u32[]{:S(2)}, u32[]{:S(2)}) collective-permute-start(f32[7,8,128]{2,1,0:T(8,128)S(1)} %get-tuple-element.18), channel_id=1, source_target_pairs={{16,32},{48,64},{80,96},{112,128},{144,160},{176,192},{208,224},{2... | collective-permute-start | bytes 86024 | tf_op jit(solution)/shard_map/ppermute | solution.py:689
  7.6 14.5 %collective-permute-start.2 = (f32[72,8,128]{2,1,0:T(8,128)S(1)}, f32[72,8,128]{2,1,0:T(8,128)S(1)}, u32[]{:S(2)}, u32[]{:S(2)}) collective-permute-start(f32[72,8,128]{2,1,0:T(8,128)S(1)} %get-tuple-element.19), channel_id=1, source_target_pairs={{0,1},{2,3},{4,5},{6,7},{8,9},{10,11},{12,13},{14,15},{1,0},{3,2},... | collective-permute-start | bytes 884744 | tf_op jit(solution)/shard_map/ppermute | solution.py:689
  8.3 13.8 %collective-permute-start.3 = (f32[72,8,128]{2,1,0:T(8,128)S(1)}, f32[72,8,128]{2,1,0:T(8,128)S(1)}, u32[]{:S(2)}, u32[]{:S(2)}) collective-permute-start(f32[72,8,128]{2,1,0:T(8,128)S(1)} %get-tuple-element.20), channel_id=1, source_target_pairs={{1,2},{3,4},{5,6},{7,8},{9,10},{11,12},{13,14},{2,1},{4,3},{6,5},{... | collective-permute-start | bytes 884744 | tf_op jit(solution)/shard_map/ppermute | solution.py:689
  11.4 10.8 %collective-permute-start.4 = (f32[7,8,128]{2,1,0:T(8,128)S(1)}, f32[7,8,128]{2,1,0:T(8,128)S(1)}, u32[]{:S(2)}, u32[]{:S(2)}) collective-permute-start(f32[7,8,128]{2,1,0:T(8,128)S(1)} %get-tuple-element.21), channel_id=1, source_target_pairs={{0,1},{2,3},{4,5},{6,7},{8,9},{10,11},{12,13},{14,15},{1,0},{3,2},... | collective-permute-start | bytes 86024 | tf_op jit(solution)/shard_map/ppermute | solution.py:689
  13.0 9.2 %collective-permute-start.5 = (f32[7,8,128]{2,1,0:T(8,128)S(1)}, f32[7,8,128]{2,1,0:T(8,128)S(1)}, u32[]{:S(2)}, u32[]{:S(2)}) collective-permute-start(f32[7,8,128]{2,1,0:T(8,128)S(1)} %get-tuple-element.22), channel_id=1, source_target_pairs={{1,2},{3,4},{5,6},{7,8},{9,10},{11,12},{13,14},{2,1},{4,3},{6,5},{... | collective-permute-start | bytes 86024 | tf_op jit(solution)/shard_map/ppermute | solution.py:689

commit v7 on v6

--- a/solution.py
+++ b/solution.py
@@ -335,7 +335,7 @@
 
 def solve_kernel(
     own, inner, rows_even, rows_odd, firsts, lasts, zonal_even, zonal_odd, strips_even, strips_odd,
-    out, field, coef, state, part,
+    out, field, coef, state, part, result, sems,
 ):
     tiles = own.shape[-1] // LANES
     lane = lanes()
@@ -522,6 +522,8 @@
     for k in range(tiles):
         coef[4, ROWS + reach + BORDER, :, cols(k)] = north[rows[-1]][k][0]
 
+    leaving = [pltpu.make_async_copy(result.at[t], out.at[t], sems.at[t]) for t in range(2)]
+
     def weight(i, r, k):
         if 0 < r < ROWS - 1:
             return inner[i, r - 1, :, cols(k)]
@@ -548,11 +550,13 @@
                     )
                     state[(n + 1) % 2, t, e, :, cols(k)] = fixed(stepped, n + 1, t, r, k)
         more = min(n, STEPS - 1 - n)
-        for r in range(-more, ROWS + more):
+        final = n == STEPS - 1
+        turns = [(t,) for t in range(2)] if final else [(0, 1)]
+        for tracers, r in [(ts, r) for ts in turns for r in range(-more, ROWS + more)]:
             ends = [ends_of(ghosts[t][n], r) for t in range(2)]
             for k in range(tiles):
                 weights = [weight(i, r, k) for i in range(7)]
-                for t in range(2):
+                for t in tracers:
                     value = read(n, t, r, k)
                     if k == 0 or k == tiles - 1:
                         ghost = ends[t] + (FACTOR_A / FACTOR_B) * value
@@ -567,10 +571,14 @@
                     stepped = stencil(
                         weights, value, to_east, to_west, read(n, t, r + 1, k), read(n, t, r - 1, k)
                     )
-                    if n == STEPS - 1:
-                        out[t, pl.ds(8 * k + r, 8, stride=8 * tiles), :] = stepped
+                    if final:
+                        result[t, pl.ds(8 * k + r, 8, stride=8 * tiles), :] = stepped
                     else:
                         state[(n + 1) % 2, t, r + BORDER, :, cols(k)] = stepped
+            if final and r == ROWS - 1:
+                leaving[tracers[0]].start()
+    for copy in leaving:
+        copy.wait()
 
 
 def granted(mib=16):
@@ -669,12 +677,14 @@
         solve_kernel,
         out_shape=jax.ShapeDtypeStruct((2, width // LANES * 64, LANES), f32),
         in_specs=in_vmem(10),
-        out_specs=in_vmem(1)[0],
+        out_specs=pl.BlockSpec(memory_space=pltpu.HBM),
         scratch_shapes=[
             pltpu.VMEM((FIELDS, rows, 8, width), f32),
             pltpu.VMEM((7, rows, 8, width), f32),
             pltpu.VMEM((2, 2, rows, 8, width), f32),
             pltpu.VMEM((2, rows, 8, width), f32),
+            pltpu.VMEM((2, width // LANES * 64, LANES), f32),
+            pltpu.SemaphoreType.DMA((2,)),
         ],
         compiler_params=granted(),
         name="solve",

time: 24.7 us -> 24.6 us (level)
  no operation moved by 1% of the time
where the time goes in v7:
time: 24.6 us; the launch traced here: 24.5 us
  starting transfers between devices  14.4 us (59%)
  waiting for transfers between devices  5.22 us (21%)
  Pallas kernels  4.79 us (19%)
    ppermute x6, starting transfers between devices, swapped(): lax.ppermute(array, axis, pairs + [(b, a) for a, b in pairs])  14.4 us
    ppermute x6, waiting for transfers between devices, swapped(): lax.ppermute(array, axis, pairs + [(b, a) for a, b in pairs])  5.22 us
    pallas_call x1, Pallas kernels, solve(): pl.pallas_call(solve_kernel, out_shape=jax.ShapeDtypeStruct((2, width //...  2.32 us
    pallas_call x1, Pallas kernels, pack(): pl.pallas_call(pack_kernel, out_shape=(jax.ShapeDtypeStruct((FIELDS, ROWS...  1.48 us
  transfers between devices with their start and end apart: 6, of which 1 were waited for; matrix products, arithmetic and copies ran while one was open for 0% of the time, Pallas kernels for 4%

profile of v7, /device:TPU:128, one launch (start us, length us, event | category | flops | bytes accessed | tf_op | source)
XLA Modules:
  0.0 24.5 jit_solution(7960377741314959)
XLA Ops:
  0.0 1.5 %pack.1 = (f32[7,8,8,384]{3,2,1,0:T(8,128)S(1)}, f32[7,8,128]{2,1,0:T(8,128)S(1)}, f32[7,8,128]{2,1,0:T(8,128)S(1)}, f32[7,8,128]{2,1,0:T(8,128)S(1)}, f32[7,8,128]{2,1,0:T(8,128)S(1)}) custom-call(f32[2,192,128]{2,1,0:T(8,128)} %bitcast.35, f32[192,128]{1,0:T(8,128)} %bitcast.36, f32[192,128]{1,0:T(8,128)} %bitcast.37, f32[192,128]{1,0:T(8,128)} %bitcast.38, ...), custom_call_target="tpu_custom_call" | custom-call | tf_op jit(solution)/shard_map/pack/pallas_call | solution.py:610
  1.5 0.1 collective-permute-start
  1.6 5.6 %collective-permute-start.1 = (f32[7,8,128]{2,1,0:T(8,128)S(1)}, f32[7,8,128]{2,1,0:T(8,128)S(1)}, u32[]{:S(2)}, u32[]{:S(2)}) collective-permute-start(f32[7,8,128]{2,1,0:T(8,128)S(1)} %get-tuple-element.18), channel_id=1, source_target_pairs={{16,32},{48,64},{80,96},{112,128},{144,160},{176,192},{208,224},{2... | collective-permute-start | bytes 86024 | tf_op jit(solution)/shard_map/ppermute | solution.py:699
  7.2 0.5 %border.1 = (f32[72,8,128]{2,1,0:T(8,128)S(1)}, f32[72,8,128]{2,1,0:T(8,128)S(1)}) custom-call(f32[7,8,8,384]{3,2,1,0:T(8,128)S(1)} %get-tuple-element.14.own), custom_call_target="tpu_custom_call" | custom-call | tf_op jit(solution)/shard_map/border/pallas_call | solution.py:632
  7.6 0.7 %collective-permute-start.2 = (f32[72,8,128]{2,1,0:T(8,128)S(1)}, f32[72,8,128]{2,1,0:T(8,128)S(1)}, u32[]{:S(2)}, u32[]{:S(2)}) collective-permute-start(f32[72,8,128]{2,1,0:T(8,128)S(1)} %get-tuple-element.19), channel_id=1, source_target_pairs={{0,1},{2,3},{4,5},{6,7},{8,9},{10,11},{12,13},{14,15},{1,0},{3,2},... | collective-permute-start | bytes 884744 | tf_op jit(solution)/shard_map/ppermute | solution.py:699
  8.3 2.9 %collective-permute-start.3 = (f32[72,8,128]{2,1,0:T(8,128)S(1)}, f32[72,8,128]{2,1,0:T(8,128)S(1)}, u32[]{:S(2)}, u32[]{:S(2)}) collective-permute-start(f32[72,8,128]{2,1,0:T(8,128)S(1)} %get-tuple-element.20), channel_id=1, source_target_pairs={{1,2},{3,4},{5,6},{7,8},{9,10},{11,12},{13,14},{2,1},{4,3},{6,5},{... | collective-permute-start | bytes 884744 | tf_op jit(solution)/shard_map/ppermute | solution.py:699
  11.2 0.0 collective-permute-done.zonal_even
  11.2 0.0 collective-permute-done.1.zonal_odd
  11.2 0.1 strips.1
  11.4 1.6 %collective-permute-start.4 = (f32[7,8,128]{2,1,0:T(8,128)S(1)}, f32[7,8,128]{2,1,0:T(8,128)S(1)}, u32[]{:S(2)}, u32[]{:S(2)}) collective-permute-start(f32[7,8,128]{2,1,0:T(8,128)S(1)} %get-tuple-element.21), channel_id=1, source_target_pairs={{0,1},{2,3},{4,5},{6,7},{8,9},{10,11},{12,13},{14,15},{1,0},{3,2},... | collective-permute-start | bytes 86024 | tf_op jit(solution)/shard_map/ppermute | solution.py:699
  13.0 3.6 %collective-permute-start.5 = (f32[7,8,128]{2,1,0:T(8,128)S(1)}, f32[7,8,128]{2,1,0:T(8,128)S(1)}, u32[]{:S(2)}, u32[]{:S(2)}) collective-permute-start(f32[7,8,128]{2,1,0:T(8,128)S(1)} %get-tuple-element.22), channel_id=1, source_target_pairs={{1,2},{3,4},{5,6},{7,8},{9,10},{11,12},{13,14},{2,1},{4,3},{6,5},{... | collective-permute-start | bytes 86024 | tf_op jit(solution)/shard_map/ppermute | solution.py:699
  16.5 0.4 %inner.1 = f32[7,6,8,384]{3,2,1,0:T(8,128)S(1)} custom-call(f32[7,8,8,384]{3,2,1,0:T(8,128)S(1)} %get-tuple-element.14.own, f32[7,8,128]{2,1,0:T(8,128)S(1)} %get-tuple-element.15.firsts, f32[7,8,128]{2,1,0:T(8,128)S(1)} %get-tuple-element.16.lasts, f32[7,8,128]{2,1,0:T(8,128)S(1)} %collective-permute-done.zonal_even, ...), custom_call_target="tpu_custom_call" | custom-call | flops 1000000000 | tf_op jit(solution)/shard_map/inner/pallas_call | solution.py:661
  16.9 5.2 %collective-permute-done.4.strips_even = f32[7,8,128]{2,1,0:T(8,128)S(1)} collective-permute-done((f32[7,8,128]{2,1,0:T(8,128)S(1)}, f32[7,8,128]{2,1,0:T(8,128)S(1)}, u32[]{:S(2)}, u32[]{:S(2)}) %collective-permute-start.4) | collective-permute-done | bytes 28704 | tf_op jit(solution)/shard_map/ppermute | solution.py:699
  22.1 0.0 collective-permute-done.5.strips_odd
  22.1 0.0 collective-permute-done.2.rows_even
  22.2 0.0 collective-permute-done.3.rows_odd
  22.2 2.3 %solve.1 = f32[2,192,128]{2,1,0:T(8,128)} custom-call(f32[7,8,8,384]{3,2,1,0:T(8,128)S(1)} %get-tuple-element.14.own, f32[7,6,8,384]{3,2,1,0:T(8,128)S(1)} %inner.1, f32[72,8,128]{2,1,0:T(8,128)S(1)} %collective-permute-done.2.rows_even, f32[72,8,128]{2,1,0:T(8,128)S(1)} %collective-permute-done.3.rows_odd, f32[7,8,128]{2,1,0:T(8,128)S(1)} %get-tuple-element.15.firsts, ...), custom_call_target="tpu_custom_call" | custom-call | tf_op jit(solution)/shard_map/solve/pallas_call | solution.py:676
Async XLA Ops:
  1.5 9.7 %collective-permute-start = (f32[7,8,128]{2,1,0:T(8,128)S(1)}, f32[7,8,128]{2,1,0:T(8,128)S(1)}, u32[]{:S(2)}, u32[]{:S(2)}) collective-permute-start(f32[7,8,128]{2,1,0:T(8,128)S(1)} %get-tuple-element.17), channel_id=1, source_target_pairs={{0,16},{32,48},{64,80},{96,112},{128,144},{160,176},{192,208},{224... | collective-permute-start | bytes 86024 | tf_op jit(solution)/shard_map/ppermute | solution.py:699
  1.6 9.6 %collective-permute-start.1 = (f32[7,8,128]{2,1,0:T(8,128)S(1)}, f32[7,8,128]{2,1,0:T(8,128)S(1)}, u32[]{:S(2)}, u32[]{:S(2)}) collective-permute-start(f32[7,8,128]{2,1,0:T(8,128)S(1)} %get-tuple-element.18), channel_id=1, source_target_pairs={{16,32},{48,64},{80,96},{112,128},{144,160},{176,192},{208,224},{2... | collective-permute-start | bytes 86024 | tf_op jit(solution)/shard_map/ppermute | solution.py:699
  7.6 14.5 %collective-permute-start.2 = (f32[72,8,128]{2,1,0:T(8,128)S(1)}, f32[72,8,128]{2,1,0:T(8,128)S(1)}, u32[]{:S(2)}, u32[]{:S(2)}) collective-permute-start(f32[72,8,128]{2,1,0:T(8,128)S(1)} %get-tuple-element.19), channel_id=1, source_target_pairs={{0,1},{2,3},{4,5},{6,7},{8,9},{10,11},{12,13},{14,15},{1,0},{3,2},... | collective-permute-start | bytes 884744 | tf_op jit(solution)/shard_map/ppermute | solution.py:699
  8.3 13.8 %collective-permute-start.3 = (f32[72,8,128]{2,1,0:T(8,128)S(1)}, f32[72,8,128]{2,1,0:T(8,128)S(1)}, u32[]{:S(2)}, u32[]{:S(2)}) collective-permute-start(f32[72,8,128]{2,1,0:T(8,128)S(1)} %get-tuple-element.20), channel_id=1, source_target_pairs={{1,2},{3,4},{5,6},{7,8},{9,10},{11,12},{13,14},{2,1},{4,3},{6,5},{... | collective-permute-start | bytes 884744 | tf_op jit(solution)/shard_map/ppermute | solution.py:699
  11.4 10.8 %collective-permute-start.4 = (f32[7,8,128]{2,1,0:T(8,128)S(1)}, f32[7,8,128]{2,1,0:T(8,128)S(1)}, u32[]{:S(2)}, u32[]{:S(2)}) collective-permute-start(f32[7,8,128]{2,1,0:T(8,128)S(1)} %get-tuple-element.21), channel_id=1, source_target_pairs={{0,1},{2,3},{4,5},{6,7},{8,9},{10,11},{12,13},{14,15},{1,0},{3,2},... | collective-permute-start | bytes 86024 | tf_op jit(solution)/shard_map/ppermute | solution.py:699
  13.0 9.2 %collective-permute-start.5 = (f32[7,8,128]{2,1,0:T(8,128)S(1)}, f32[7,8,128]{2,1,0:T(8,128)S(1)}, u32[]{:S(2)}, u32[]{:S(2)}) collective-permute-start(f32[7,8,128]{2,1,0:T(8,128)S(1)} %get-tuple-element.22), channel_id=1, source_target_pairs={{1,2},{3,4},{5,6},{7,8},{9,10},{11,12},{13,14},{2,1},{4,3},{6,5},{... | collective-permute-start | bytes 86024 | tf_op jit(solution)/shard_map/ppermute | solution.py:699
